TPU v7x, 512 devices: a whole 4x4x16 slice. The times are simulated.
512 devices in a mesh: grid: 32 (over x, z_hi, core), atom: 16 (over z_lo, y).
Axes of the slice: x: 4, y: 4, z: 16 (z_hi: 4, z_lo: 4; z = z_hi * 4 + z_lo), core: 2. Of those that a mesh axis runs over, the one named last changes fastest.
Arguments:
- basis_values: bfloat16 [1024, 128, 512], P(('grid', 'atom')), may hold values from -8 to 8
- block_lists: int32 [1024, 4], P('grid'), may hold values from 0 to 95, as said below
- orbitals: bfloat16 [12288, 4096], P('grid', 'atom'), may hold values from -0.00390625 to 0.00390625
- point_weights: float32 [131072], P(('grid', 'atom')), may hold values from 0.1 to 1
- point_atoms: int32 [131072], P(('grid', 'atom')), may hold values from 0 to 511, as said below
- embed_scale: float32 [256], replicated, may hold values from -4 to 4
- embed_shift: float32 [256], replicated, may hold values from -3 to 3
- message_weight: bfloat16 [2, 256, 256], replicated, may hold values from -0.375 to 0.375
- atom_weight: bfloat16 [2, 256, 256], replicated, may hold values from -0.375 to 0.375
- head_weight: float32 [256], replicated, may hold values from -0.375 to 0.375
Outputs:
- fock_orbitals: float32 [12288, 4096], P('grid', 'atom')
- potential: float32 [131072], P(('grid', 'atom'))
Inputs may be any that keep to these rules, and one draw needn't show every extreme that they name: `block_lists`: each row names 4 different blocks; a batch b of group g = b // 32 names only blocks (g - 1) * 3 to (g + 2) * 3 - 1. `point_atoms`: the 256 points of one device name atom centres of one run of max(8, 1) consecutive centres, counted round.
All inputs are finite; a program needn't handle non-finite values.
Results may differ from a plain program's by a relative error of at most 0.04.
Values may be sent and summed in bfloat16 or wider, within the bound.
No kernel may reach another device: no remote copies, remote signals or barrier semaphores. Data moves between devices by JAX's collectives and lax.ppermute only.
A program may use at most 128 MiB of HBM per device.

v0:
```python
import jax
import jax.numpy as jnp
from jax import lax
from jax.sharding import Mesh
from jax.sharding import PartitionSpec as P

ATOM_DEV = 32
ATOM = ("atom_0", "atom_1")
GRID_ATOM = ("grid", "atom_0", "atom_1")


def padded(cells, sides, width):
    for axis, dim in sides:
        count = lax.axis_size(axis)
        ends = count - 1
        head = lax.slice_in_dim(cells, 0, width, axis=dim)
        tail = lax.slice_in_dim(cells, cells.shape[dim] - width, cells.shape[dim], axis=dim)
        cells = jnp.concatenate(
            [
                lax.ppermute(tail, axis, [(i, (i + 1) % count) for i in range(ends)]),
                cells,
                lax.ppermute(head, axis, [((i + 1) % count, i) for i in range(ends)]),
            ],
            axis=dim,
        )
    return cells


def laid_out(parts, dim):
    parts = jnp.moveaxis(parts, 0, dim)
    dims = parts.shape
    return parts.reshape(*dims[:dim], dims[dim] * dims[dim + 1], *dims[dim + 2 :])


def stacked_from(x, axes, turns):
    parts = x
    for k in turns:
        parts = lax.all_gather(parts, axes[k])
    done = turns[::-1]
    back = [done.index(k) for k in range(len(axes))]
    parts = parts.transpose(*back, *range(len(axes), parts.ndim))
    return parts.reshape(-1, *x.shape)


def gather_axes(x, axes, turns, dim):
    return laid_out(stacked_from(x, axes, turns), dim)


def in_blocks(x, dim, devices):
    before, after = (x.shape[:dim], x.shape[dim + 1 :])
    return jnp.moveaxis(x.reshape(*before, devices, -1, *after), dim, 0)


def sum_at_owner(x, axis, dim):
    devices = lax.axis_size(axis)
    parts = lax.all_to_all(in_blocks(x, dim, devices), axis, 0, 0, tiled=True)
    return jnp.sum(parts, axis=0)


def sent_and_summed(x, axis, dim):
    parts = in_blocks(x, dim, lax.axis_size(axis))
    arrived = lax.all_to_all(parts, axis, split_axis=0, concat_axis=0, tiled=True)
    return arrived.astype(jnp.float32).sum(axis=0)


def side_by_side(arrays, axis, dim, along):
    columns = [a.reshape(*a.shape[:along], -1) for a in arrays]
    both = jnp.concatenate(columns, axis=along)
    filled, at, outs = (sent_and_summed(both, axis, dim), 0, [])
    for a, column in zip(arrays, columns):
        share = filled[..., at : at + column.shape[along]]
        outs.append(share.reshape(*share.shape[:along], *a.shape[along:]))
        at += column.shape[along]
    return tuple(outs)


def copy_for_each(x, axis):
    copies = jnp.broadcast_to(x, (lax.axis_size(axis), *x.shape))
    return lax.all_to_all(copies, axis, split_axis=0, concat_axis=0, tiled=True)


def taken_together(x, axis):
    return copy_for_each(x, axis).astype(jnp.float32).sum(axis=0)


def collect(x, axis, dim):
    return laid_out(copy_for_each(x, axis), dim)


def passed_along(value, axis, steps):
    count = lax.axis_size(axis)
    leading, last = (max(0, -steps), min(count, count - steps))
    return lax.ppermute(value, axis, [(source, source + steps) for source in range(leading, last)])


def orbital_values(piece, lists, blocks):
    count = piece.shape[0]
    chosen = blocks[lists].reshape(count, -1, blocks.shape[2])
    values = jnp.einsum("bpk,bko->bpo", piece, chosen, preferred_element_type=jnp.float32)
    return values.astype(jnp.bfloat16)


def fock_terms(piece, lists, psi_rows, scale_rows, total):
    weighted_psi = (scale_rows[:, :, None] * psi_rows.astype(jnp.float32)).astype(jnp.bfloat16)
    terms = jnp.einsum("bpk,bpo->bko", piece, weighted_psi, preferred_element_type=jnp.float32)
    terms = terms.reshape(-1, total.shape[1], total.shape[2])
    return total.at[lists.reshape(-1)].add(terms)


def atom_update(rows, mass, weight):
    mean = rows / (1.0 + mass[:, None])
    return jax.nn.silu(
        jnp.dot(mean.astype(jnp.bfloat16), weight, preferred_element_type=jnp.float32)
    ).astype(jnp.bfloat16)


def local(
    basis_values,
    block_lists,
    orbitals,
    point_weights,
    point_atoms,
    embed_scale,
    embed_shift,
    message_weight,
    atom_weight,
    head_weight,
):
    own_rows = orbitals.shape[0]
    gathered = padded(orbitals, (("grid", 0),), own_rows)
    width = basis_values.shape[2] // block_lists.shape[1]
    owned = own_rows // width
    blocks = gathered.reshape(-1, width, gathered.shape[1])
    offset = (lax.axis_index("grid") - 1) * owned
    local_lists = block_lists - offset
    group_values = gather_axes(basis_values, ATOM, (0, 1), 0)
    psi = orbital_values(group_values, local_lists, blocks)
    squares = 2.0 * jnp.sum(jnp.square(psi.astype(jnp.float32)), axis=2).reshape(-1)
    density = sum_at_owner(squares, ATOM, 0)
    radius = jnp.cbrt(density)
    hidden = jax.nn.silu(radius[:, None] * embed_scale[None, :] + embed_shift[None, :])
    atom_total = ATOM_DEV * lax.axis_size(ATOM)
    onehot = point_atoms[:, None] == jnp.arange(atom_total, dtype=jnp.int32)[None, :]
    selector = onehot.astype(jnp.bfloat16)
    counts = jnp.dot(point_weights, onehot.astype(jnp.float32), precision=lax.Precision.HIGHEST)
    for layer in range(message_weight.shape[0]):
        message = jax.nn.silu(
            jnp.dot(
                hidden.astype(jnp.bfloat16),
                message_weight[layer],
                preferred_element_type=jnp.float32,
            )
        )
        weighted = (point_weights[:, None] * message).astype(jnp.bfloat16)
        partial_value = lax.dot_general(
            selector, weighted, (((0,), (0,)), ((), ())), preferred_element_type=jnp.float32
        )
        rows, mass = side_by_side(
            (partial_value.astype(jnp.bfloat16), counts.astype(jnp.bfloat16)), ATOM, 0, 1
        )
        rows, mass = (
            taken_together(rows.astype(jnp.bfloat16), "grid").astype(jnp.float32),
            taken_together(mass.astype(jnp.bfloat16), "grid").astype(jnp.float32),
        )
        update = atom_update(rows, mass, atom_weight[layer])
        features = collect(update, ATOM, 0)
        picked = jnp.dot(selector, features, preferred_element_type=jnp.float32)
        hidden = hidden + message * picked
    score = jnp.dot(hidden, head_weight, precision=lax.Precision.HIGHEST)
    potential = radius * (1.0 + jnp.tanh(score))
    scaled = collect(point_weights * potential, ATOM, 0)
    scaled = scaled.reshape(psi.shape[0], psi.shape[1])
    empty = jnp.zeros((blocks.shape[0], width, psi.shape[2]), jnp.float32)
    total = fock_terms(group_values, local_lists, psi, scaled, empty)
    rounded = lax.optimization_barrier(
        total.reshape(3, own_rows, total.shape[2]).astype(jnp.bfloat16)
    )
    from_below = passed_along(rounded[2], "grid", 1)
    from_above = passed_along(rounded[0], "grid", -1)
    fock_orbitals = (
        rounded[1].astype(jnp.float32)
        + from_below.astype(jnp.float32)
        + from_above.astype(jnp.float32)
    )
    return (fock_orbitals, potential)


def solution(mesh):
    finer = Mesh(mesh.devices.reshape(mesh.shape["grid"], 4, 4), ("grid", "atom_0", "atom_1"))
    placed = (
        P(GRID_ATOM, None, None),
        P("grid", None),
        P("grid", ATOM),
        P(GRID_ATOM),
        P(GRID_ATOM),
        P(),
        P(),
        P(),
        P(),
        P(),
    )
    return jax.shard_map(
        local,
        mesh=finer,
        in_specs=placed,
        out_specs=(P("grid", ATOM), P(GRID_ATOM)),
        check_vma=False,
    )
```

profile of v0, /device:TPU:1, one launch (start us, length us, event | category | flops | bytes accessed | tf_op | source)
XLA Modules:
  0.0 422.5 jit_solution(4834249172101484675)
XLA Ops:
  8.0 45.9 %all-gather.5.cloned.1.call-done = bf16[8,128,512]{2,1,0:T(8,128)(2,1)} async-done(((bf16[2,128,512]{2,1,0:T(8,128)(2,1)}), bf16[8,128,512]{2,1,0:T(8,128)(2,1)}) %all-gather.5.cloned.1.call-update) | async-done | bytes 1048592 | tf_op jit(solution)/shard_map/all_gather | solution.py:38
  53.9 8.1 %collective-permute-start = (bf16[384,256]{1,0:T(8,128)(2,1)}, bf16[384,256]{1,0:T(8,128)(2,1)S(1)}, u32[]{:S(2)}, u32[]{:S(2)}) collective-permute-start(bf16[384,256]{1,0:T(8,128)(2,1)} %param.12), channel_id=1, source_target_pairs={{0,16},{16,32},{32,48},{48,64},{64,80},{80,96},{96,112},{112,128},... | collective-permute-start | bytes 589832 | tf_op jit(solution)/shard_map/ppermute | solution.py:20
  67.7 10.8 %collective-permute-done.1 = bf16[384,256]{1,0:T(8,128)(2,1)S(1)} collective-permute-done((bf16[384,256]{1,0:T(8,128)(2,1)}, bf16[384,256]{1,0:T(8,128)(2,1)S(1)}, u32[]{:S(2)}, u32[]{:S(2)}) %collective-permute-start.1) | collective-permute-done | bytes 196640 | tf_op jit(solution)/shard_map/ppermute | solution.py:22
  79.4 6.6 %gather_fusion = bf16[128,128,256]{2,1,0:T(8,128)(2,1)} fusion(bf16[9,128,256]{2,1,0:T(8,128)(2,1)S(1)} %bitcast.59, s32[1024]{0:T(1024)S(1)} %pad_clamp_fusion), kind=kCustom, calls=%fused_computation | custom fusion | bytes 16777728 | tf_op jit(solution)/shard_map/gather | solution.py:98
  86.0 25.2 %all-gather.7.cloned.1.call-done = bf16[16,2,128,512]{3,2,1,0:T(8,128)(2,1)} async-done(((bf16[4,2,128,512]{3,2,1,0:T(8,128)(2,1)}), bf16[16,2,128,512]{3,2,1,0:T(8,128)(2,1)}) %all-gather.7.cloned.1.call-update) | async-done | bytes 4194320 | tf_op jit(solution)/shard_map/all_gather | solution.py:38
  115.8 7.1 %fusion = (f32[32,128]{1,0:T(8,128)S(1)}, bf16[32,256,128]{2,1,0:T(8,128)(2,1)S(1)}) fusion(bf16[32,512,256]{2,1,0:T(8,128)(2,1)} %bitcast.63, bf16[32,128,512]{2,1,0:T(8,128)(2,1)} %bitcast.61), kind=kOutput, calls=%fused_computation.5 | convolution fusion | flops 1077932032 | bytes 14696448 | tf_op jit(solution)/shard_map/bpk,bko->bpo/dot_general | solution.py:99
  123.6 6.1 %all-to-all-start = ((f32[16,1,256]{2,1,0:T(1,128)}), f32[16,1,256]{2,1,0:T(1,128)S(1)}, u32[]{:S(2)}, u32[]{:S(2)}) async-start(f32[16,1,256]{2,1,0:T(1,128)} %bitcast.7), calls=%async_computation | async-start | bytes 32768 | tf_op jit(solution)/shard_map/all_to_all | solution.py:56
  130.4 6.2 %all-to-all-done = f32[16,1,256]{2,1,0:T(1,128)S(1)} async-done(((f32[16,1,256]{2,1,0:T(1,128)}), f32[16,1,256]{2,1,0:T(1,128)S(1)}, u32[]{:S(2)}, u32[]{:S(2)}) %all-to-all-start) | async-done | bytes 16416 | tf_op jit(solution)/shard_map/all_to_all | solution.py:56
  137.5 13.0 %all_to_all.54 = bf16[16,32,257]{2,1,0:T(8,128)(2,1)S(1)} all-to-all(bf16[16,32,257]{2,1,0:T(8,128)(2,1)S(1)} %pad_maximum_fusion.2), channel_id=1, replica_groups=mesh['grid'=32,'atom_0'=4,'atom_1'=4] {'atom_0','atom_1'}, dimensions={0} | all-to-all | bytes 526336 | tf_op jit(solution)/shard_map/all_to_all | solution.py:62
  151.3 15.8 %all-to-all-start.3 = ((bf16[32,1,32]{2,1,0:T(2,128)(2,1)}), bf16[32,1,32]{2,1,0:T(2,128)(2,1)S(1)}, u32[]{:S(2)}, u32[]{:S(2)}) async-start(bf16[32,1,32]{2,1,0:T(2,128)(2,1)} %broadcast_in_dim.40), calls=%async_computation.3 | async-start | bytes 32768 | tf_op jit(solution)/shard_map/all_to_all | solution.py:79
  167.1 14.1 %all-to-all-done.3 = bf16[32,1,32]{2,1,0:T(2,128)(2,1)S(1)} async-done(((bf16[32,1,32]{2,1,0:T(2,128)(2,1)}), bf16[32,1,32]{2,1,0:T(2,128)(2,1)S(1)}, u32[]{:S(2)}, u32[]{:S(2)}) %all-to-all-start.3) | async-done | bytes 2080 | tf_op jit(solution)/shard_map/all_to_all | solution.py:79
  186.2 28.9 %all-to-all-done.2 = bf16[32,32,256]{2,1,0:T(8,128)(2,1)S(1)} async-done(((bf16[32,32,256]{2,1,0:T(8,128)(2,1)}), bf16[32,32,256]{2,1,0:T(8,128)(2,1)S(1)}, u32[]{:S(2)}, u32[]{:S(2)}) %all-to-all-start.2) | async-done | bytes 524320 | tf_op jit(solution)/shard_map/all_to_all | solution.py:79
  216.4 17.7 %all_to_all.55 = bf16[16,32,256]{2,1,0:T(8,128)(2,1)S(1)} all-to-all(bf16[16,32,256]{2,1,0:T(8,128)(2,1)S(1)} %broadcast_in_dim.41), channel_id=1, replica_groups=mesh['grid'=32,'atom_0'=4,'atom_1'=4] {'atom_0','atom_1'}, dimensions={0} | all-to-all | bytes 524288 | tf_op jit(solution)/shard_map/all_to_all | solution.py:79
  236.0 14.6 %all_to_all.56 = bf16[16,32,257]{2,1,0:T(8,128)(2,1)S(1)} all-to-all(bf16[16,32,257]{2,1,0:T(8,128)(2,1)S(1)} %pad_maximum_fusion.1), channel_id=1, replica_groups=mesh['grid'=32,'atom_0'=4,'atom_1'=4] {'atom_0','atom_1'}, dimensions={0} | all-to-all | bytes 526336 | tf_op jit(solution)/shard_map/all_to_all | solution.py:62
  251.4 8.0 %all-to-all-start.7 = ((bf16[32,1,32]{2,1,0:T(2,128)(2,1)}), bf16[32,1,32]{2,1,0:T(2,128)(2,1)S(1)}, u32[]{:S(2)}, u32[]{:S(2)}) async-start(bf16[32,1,32]{2,1,0:T(2,128)(2,1)} %broadcast_in_dim.43), calls=%async_computation.7 | async-start | bytes 32768 | tf_op jit(solution)/shard_map/all_to_all | solution.py:79
  259.5 14.1 %all-to-all-done.7 = bf16[32,1,32]{2,1,0:T(2,128)(2,1)S(1)} async-done(((bf16[32,1,32]{2,1,0:T(2,128)(2,1)}), bf16[32,1,32]{2,1,0:T(2,128)(2,1)S(1)}, u32[]{:S(2)}, u32[]{:S(2)}) %all-to-all-start.7) | async-done | bytes 2080 | tf_op jit(solution)/shard_map/all_to_all | solution.py:79
  278.6 28.9 %all-to-all-done.6 = bf16[32,32,256]{2,1,0:T(8,128)(2,1)S(1)} async-done(((bf16[32,32,256]{2,1,0:T(8,128)(2,1)}), bf16[32,32,256]{2,1,0:T(8,128)(2,1)S(1)}, u32[]{:S(2)}, u32[]{:S(2)}) %all-to-all-start.6) | async-done | bytes 524320 | tf_op jit(solution)/shard_map/all_to_all | solution.py:79
  309.4 8.2 %all-to-all-start.8 = ((bf16[16,32,256]{2,1,0:T(8,128)(2,1)}), bf16[16,32,256]{2,1,0:T(8,128)(2,1)S(1)}, u32[]{:S(2)}, u32[]{:S(2)}) async-start(bf16[16,32,256]{2,1,0:T(8,128)(2,1)} %broadcast_in_dim.44), calls=%async_computation.8 | async-start | bytes 524288 | tf_op jit(solution)/shard_map/all_to_all | solution.py:79
  317.8 9.4 %all-to-all-done.8 = bf16[16,32,256]{2,1,0:T(8,128)(2,1)S(1)} async-done(((bf16[16,32,256]{2,1,0:T(8,128)(2,1)}), bf16[16,32,256]{2,1,0:T(8,128)(2,1)S(1)}, u32[]{:S(2)}, u32[]{:S(2)}) %all-to-all-start.8) | async-done | bytes 262176 | tf_op jit(solution)/shard_map/all_to_all | solution.py:79
  333.2 6.8 %all-to-all-done.9 = f32[16,1,256]{2,1,0:T(1,128)S(1)} async-done(((f32[16,1,256]{2,1,0:T(1,128)}), f32[16,1,256]{2,1,0:T(1,128)S(1)}, u32[]{:S(2)}, u32[]{:S(2)}) %all-to-all-start.9) | async-done | bytes 16416 | tf_op jit(solution)/shard_map/all_to_all | solution.py:79
  340.0 10.2 %convolution_bitcast_fusion = f32[32,512,256]{1,2,0:T(8,128)} fusion(bf16[32,128,512]{2,1,0:T(8,128)(2,1)} %bitcast.62, bf16[32,256,128]{2,1,0:T(8,128)(2,1)S(1)} %get-tuple-element.9, f32[32,128]{1,0:T(8,128)S(1)} %bitcast.72), kind=kOutput, calls=%fused_computation.2 | convolution fusion | flops 1076887552 | bytes 23085056 | tf_op jit(solution)/shard_map/bpk,bpo->bko/dot_general | solution.py:105
  350.2 17.5 %copy.63 = f32[32,512,256]{2,1,0:T(8,128)} copy(f32[32,512,256]{1,2,0:T(8,128)} %convolution_bitcast_fusion) | data formatting | bytes 33554432 | tf_op jit(solution)/shard_map/bpk,bpo->bko/dot_general | solution.py:105
  367.8 24.2 %scatter_fusion = f32[9,128,256]{2,1,0:T(8,128)S(1)} fusion(f32[9,128,256]{2,1,0:T(8,128)S(1)} %broadcast_in_dim.18, s32[128]{0:T(128)S(1)} %fusion.44, f32[128,128,256]{2,1,0:T(8,128)} %bitcast.60), kind=kCustom, calls=%fused_computation.1 | custom fusion | flops 4194304 | bytes 50332160 | tf_op jit(solution)/shard_map/scatter-add | solution.py:107
  400.4 14.4 %collective-permute-done.3 = bf16[384,256]{1,0:T(8,128)(2,1)S(1)} collective-permute-done((bf16[384,256]{1,0:T(8,128)(2,1)S(1)}, bf16[384,256]{1,0:T(8,128)(2,1)S(1)}, u32[]{:S(2)}, u32[]{:S(2)}) %collective-permute-start.3) | collective-permute-done | bytes 196640 | tf_op jit(solution)/shard_map/ppermute | solution.py:93
  (74 shorter events, 46.0 us)
Async XLA Ops:
  7.2 320.3 %copy-start = (f32[256]{0:T(256)S(1)}, f32[256]{0:T(256)}, u32[]{:S(2)}) copy-start(f32[256]{0:T(256)} %param.19) | copy-start | bytes 3076
  7.2 46.7 %all-gather.5.cloned.1.call-start = ((), (), s32[]{:S(2)}) async-start(), calls=%async_computation.10 | async-start | bytes 1310720 | tf_op jit(solution)/shard_map/all_gather | solution.py:38
  7.9 103.3 %all-gather.7.cloned.1.call-start = ((), (), s32[]{:S(2)}) async-start(), calls=%async_computation.11 | async-start | bytes 5242880 | tf_op jit(solution)/shard_map/all_gather | solution.py:38
  53.9 13.8 %collective-permute-start = (bf16[384,256]{1,0:T(8,128)(2,1)}, bf16[384,256]{1,0:T(8,128)(2,1)S(1)}, u32[]{:S(2)}, u32[]{:S(2)}) collective-permute-start(bf16[384,256]{1,0:T(8,128)(2,1)} %param.12), channel_id=1, source_target_pairs={{0,16},{16,32},{32,48},{48,64},{64,80},{80,96},{96,112},{112,128},... | collective-permute-start | bytes 589832 | tf_op jit(solution)/shard_map/ppermute | solution.py:20
  62.1 16.4 %collective-permute-start.1 = (bf16[384,256]{1,0:T(8,128)(2,1)}, bf16[384,256]{1,0:T(8,128)(2,1)S(1)}, u32[]{:S(2)}, u32[]{:S(2)}) collective-permute-start(bf16[384,256]{1,0:T(8,128)(2,1)} %param.12), channel_id=1, source_target_pairs={{16,0},{32,16},{48,32},{64,48},{80,64},{96,80},{112,96},{128,112},... | collective-permute-start | bytes 589832 | tf_op jit(solution)/shard_map/ppermute | solution.py:22
  115.8 13.9 %copy-start.1 = (s32[256]{0:T(256)S(1)}, s32[256]{0:T(256)}, u32[]{:S(2)}) copy-start(s32[256]{0:T(256)} %param.14) | copy-start | bytes 3076
  115.8 13.9 %copy-start.2 = (f32[256]{0:T(256)S(1)}, f32[256]{0:T(256)}, u32[]{:S(2)}) copy-start(f32[256]{0:T(256)} %param.13) | copy-start | bytes 3076
  115.8 20.8 %copy-start.3 = (bf16[2,256,256]{2,1,0:T(8,128)(2,1)S(1)}, bf16[2,256,256]{2,1,0:T(8,128)(2,1)}, u32[]{:S(2)}) copy-start(bf16[2,256,256]{2,1,0:T(8,128)(2,1)} %param.17) | copy-start | bytes 786436
  115.8 20.8 %copy-start.4 = (f32[256]{0:T(256)S(1)}, f32[256]{0:T(256)}, u32[]{:S(2)}) copy-start(f32[256]{0:T(256)} %param.16) | copy-start | bytes 3076
  115.8 20.8 %copy-start.5 = (f32[256]{0:T(256)S(1)}, f32[256]{0:T(256)}, u32[]{:S(2)}) copy-start(f32[256]{0:T(256)} %param.15) | copy-start | bytes 3076
  123.6 13.0 %all-to-all-start = ((f32[16,1,256]{2,1,0:T(1,128)}), f32[16,1,256]{2,1,0:T(1,128)S(1)}, u32[]{:S(2)}, u32[]{:S(2)}) async-start(f32[16,1,256]{2,1,0:T(1,128)} %bitcast.7), calls=%async_computation | async-start | bytes 32768 | tf_op jit(solution)/shard_map/all_to_all | solution.py:56
  151.3 29.9 %all-to-all-start.3 = ((bf16[32,1,32]{2,1,0:T(2,128)(2,1)}), bf16[32,1,32]{2,1,0:T(2,128)(2,1)S(1)}, u32[]{:S(2)}, u32[]{:S(2)}) async-start(bf16[32,1,32]{2,1,0:T(2,128)(2,1)} %broadcast_in_dim.40), calls=%async_computation.3 | async-start | bytes 32768 | tf_op jit(solution)/shard_map/all_to_all | solution.py:79
  182.0 33.2 %all-to-all-start.2 = ((bf16[32,32,256]{2,1,0:T(8,128)(2,1)}), bf16[32,32,256]{2,1,0:T(8,128)(2,1)S(1)}, u32[]{:S(2)}, u32[]{:S(2)}) async-start(bf16[32,32,256]{2,1,0:T(8,128)(2,1)} %broadcast_in_dim.39), calls=%async_computation.2 | async-start | bytes 1048576 | tf_op jit(solution)/shard_map/all_to_all | solution.py:79
  251.4 22.1 %all-to-all-start.7 = ((bf16[32,1,32]{2,1,0:T(2,128)(2,1)}), bf16[32,1,32]{2,1,0:T(2,128)(2,1)S(1)}, u32[]{:S(2)}, u32[]{:S(2)}) async-start(bf16[32,1,32]{2,1,0:T(2,128)(2,1)} %broadcast_in_dim.43), calls=%async_computation.7 | async-start | bytes 32768 | tf_op jit(solution)/shard_map/all_to_all | solution.py:79
  274.4 33.1 %all-to-all-start.6 = ((bf16[32,32,256]{2,1,0:T(8,128)(2,1)}), bf16[32,32,256]{2,1,0:T(8,128)(2,1)S(1)}, u32[]{:S(2)}, u32[]{:S(2)}) async-start(bf16[32,32,256]{2,1,0:T(8,128)(2,1)} %broadcast_in_dim.42), calls=%async_computation.6 | async-start | bytes 1048576 | tf_op jit(solution)/shard_map/all_to_all | solution.py:79
  309.4 17.8 %all-to-all-start.8 = ((bf16[16,32,256]{2,1,0:T(8,128)(2,1)}), bf16[16,32,256]{2,1,0:T(8,128)(2,1)S(1)}, u32[]{:S(2)}, u32[]{:S(2)}) async-start(bf16[16,32,256]{2,1,0:T(8,128)(2,1)} %broadcast_in_dim.44), calls=%async_computation.8 | async-start | bytes 524288 | tf_op jit(solution)/shard_map/all_to_all | solution.py:79
  329.1 11.0 %all-to-all-start.9 = ((f32[16,1,256]{2,1,0:T(1,128)}), f32[16,1,256]{2,1,0:T(1,128)S(1)}, u32[]{:S(2)}, u32[]{:S(2)}) async-start(f32[16,1,256]{2,1,0:T(1,128)} %broadcast_in_dim.45), calls=%async_computation.9 | async-start | bytes 32768 | tf_op jit(solution)/shard_map/all_to_all | solution.py:79
  392.2 8.2 %collective-permute-start.2 = (bf16[384,256]{1,0:T(8,128)(2,1)S(1)}, bf16[384,256]{1,0:T(8,128)(2,1)S(1)}, u32[]{:S(2)}, u32[]{:S(2)}) collective-permute-start(bf16[384,256]{1,0:T(8,128)(2,1)S(1)} %get-tuple-element.6), channel_id=1, source_target_pairs={{0,16},{16,32},{32,48},{48,64},{64,80},{80,96},{96,112},{112,128},... | collective-permute-start | bytes 589832 | tf_op jit(solution)/shard_map/ppermute | solution.py:93
  397.7 17.1 %collective-permute-start.3 = (bf16[384,256]{1,0:T(8,128)(2,1)S(1)}, bf16[384,256]{1,0:T(8,128)(2,1)S(1)}, u32[]{:S(2)}, u32[]{:S(2)}) collective-permute-start(bf16[384,256]{1,0:T(8,128)(2,1)S(1)} %get-tuple-element.7), channel_id=1, source_target_pairs={{16,0},{32,16},{48,32},{64,48},{80,64},{96,80},{112,96},{128,112},... | collective-permute-start | bytes 589832 | tf_op jit(solution)/shard_map/ppermute | solution.py:93
Sparse Core Ops, SparseCore 0:
  10.1 43.7 all-gather.4
  56.0 55.2 all-gather.6
where the time goes:
time: 424 us; the launch traced here: 422 us
  waiting for transfers between devices  209 us (49%)
  starting transfers between devices  68.1 us (16%)
  blocking collectives  45.3 us (11%)
  local copies, waits for them, and re-layouts  34 us (8%)
  other arithmetic  28.5 us (7%)
  matrix products  23.1 us (5%)
  between operations  14.4 us (3%)
    all_to_all x6, waiting for transfers between devices, copy_for_each(): return lax.all_to_all(copies, axis, split_axis=0, concat_axis=0, tiled=True)  102 us
    all_gather x2, waiting for transfers between devices, stacked_from(): parts = lax.all_gather(parts, axes[k])  71.1 us
    all_to_all x6, starting transfers between devices, copy_for_each(): return lax.all_to_all(copies, axis, split_axis=0, concat_axis=0, tiled=True)  44.4 us
    all_to_all x2, blocking collectives, sent_and_summed(): lax.all_to_all(parts, axis, split_axis=0, concat_axis=0, tiled=True)  27.6 us
    scatter-add x1, other arithmetic, fock_terms(): return total.at[lists.reshape(-1)].add(terms)  24.2 us
    all_to_all x1, blocking collectives, copy_for_each(): return lax.all_to_all(copies, axis, split_axis=0, concat_axis=0, tiled=True)  17.7 us
    dot_general x1, local copies, waits for them, and re-layouts, fock_terms(): jnp.einsum('bpk,bpo->bko', piece, weighted_psi, preferred_element_type=jn...  17.5 us
    ppermute x2, waiting for transfers between devices, passed_along(): lax.ppermute(value, axis, [(source, source + steps) for source in range(l...  15.2 us
  transfers between devices with their start and end apart: 13, of which 13 were waited for; matrix products, arithmetic and copies ran while one was open for 2% of the time, Pallas kernels for 0%

commit v1 on v0

v1 whole, which is shorter than its diff:
```python
import jax
import jax.numpy as jnp
from jax import lax
from jax.experimental import pallas as pl
from jax.experimental.pallas import tpu as pltpu
from jax.sharding import Mesh
from jax.sharding import PartitionSpec as P

AXES = ("x", "zh", "c", "zl", "y")
GRID = ("x", "zh", "c")
PLANE = ("x", "c", "y")
COLUMN = ("zh", "zl")
SIDE = 4
BLK = 128
WINDOW = 8
NATOM = 512
ROWS = 16
F32 = jnp.float32
BF16 = jnp.bfloat16

VMEM = 48 * 1024 * 1024


def call(kernel, out_shape, n_in, smem=(), scratch=(), **kw):
    specs = [
        pl.BlockSpec(memory_space=pltpu.SMEM if i in smem else pltpu.VMEM) for i in range(n_in)
    ]
    outs = jax.tree.map(lambda _: pl.BlockSpec(memory_space=pltpu.VMEM), out_shape)
    return pl.pallas_call(
        kernel,
        out_shape=out_shape,
        in_specs=specs,
        out_specs=outs,
        scratch_shapes=list(scratch),
        compiler_params=pltpu.CompilerParams(vmem_limit_bytes=VMEM),
        **kw,
    )


def shape(dims, dtype):
    return jax.ShapeDtypeStruct(dims, dtype)


def spread_kernel(place_ref, row_ref, *refs):
    parts, (dense_ref, flipped_ref) = refs[:SIDE], refs[SIDE:]
    dense_ref[...] = jnp.zeros_like(dense_ref)
    flipped_ref[...] = jnp.zeros_like(flipped_ref)
    for k, part in enumerate(parts):
        for r in range(part.shape[0]):
            n = k * part.shape[0] + r
            row = pl.multiple_of(row_ref[n] * BLK, BLK)
            for j in range(part.shape[2] // BLK):
                col = pl.multiple_of(place_ref[n, j] * BLK, BLK)
                tile = part[r, :, j * BLK : (j + 1) * BLK]
                dense_ref[pl.ds(row, BLK), pl.ds(col, BLK)] = tile
                flipped_ref[pl.ds(col, BLK), pl.ds(row, BLK)] = tile.T


def psi_kernel(dense_ref, *refs):
    own, outer = refs[:SIDE], refs[SIDE : 2 * SIDE]
    partner, psi_ref, dens_ref, acc_ref = refs[2 * SIDE :]
    width = own[0].shape[1]
    for k in range(SIDE):
        chosen = jnp.concatenate([own[k][...], outer[k][...], partner[k]], axis=0)
        psi = jnp.dot(dense_ref[...], chosen, preferred_element_type=F32).astype(BF16)
        psi_ref[:, k * width : (k + 1) * width] = psi
        wide = psi.astype(F32)
        square = wide * wide
        part = square[:, :BLK] + square[:, BLK:]
        if k == 0:
            acc_ref[...] = part
        else:
            acc_ref[...] += part
    for n in range(acc_ref.shape[0] // BLK):
        tile = acc_ref[n * BLK : (n + 1) * BLK, :].T
        dens_ref[n // 2, n % 2 : n % 2 + 1, :] = 2.0 * jnp.sum(tile, axis=0, keepdims=True)


def silu(x):
    return x * jax.nn.sigmoid(x)


def column(tall, n):
    return jnp.concatenate([tall[:, n : n + 1], tall[:, n + 1 : n + 2]], axis=0)


def message_of(hidden, weight, weights_col, selector, meta):
    message = silu(jnp.dot(hidden.astype(BF16), weight, preferred_element_type=F32))
    weighted = (weights_col * message).astype(BF16)
    rows = jnp.dot(selector, weighted, preferred_element_type=F32)
    return message, (rows + meta).astype(BF16)


def first_kernel(
    radius_ref, pw_ref, scale_ref, shift_ref, weight_ref, sel_ref, meta_ref,
    hidden_ref, message_ref, cols_ref, out_ref, scratch,
):
    scratch[...] = jnp.zeros_like(scratch)
    scratch[0:2, :] = radius_ref[...]
    scratch[2:4, :] = pw_ref[...]
    tall = scratch[...].T
    cols_ref[...] = tall
    radius, weights = column(tall, 0), column(tall, 2)
    hidden = silu(radius * scale_ref[...] + shift_ref[...])
    hidden_ref[...] = hidden
    message, payload = message_of(hidden, weight_ref[0], weights, sel_ref[...], meta_ref[...])
    message_ref[...] = message
    out_ref[...] = jnp.broadcast_to(payload[None], out_ref.shape)


def route_first_kernel(x_ref, target_ref, out_ref, match_ref):
    n = x_ref.shape[0] * ROWS
    x = x_ref[...].reshape(n, x_ref.shape[2])
    meta = x[:, :BLK].astype(F32)
    meta = jnp.concatenate([meta[WINDOW:], meta[:WINDOW]], axis=0)
    atom = meta[:, 1:2] * 16.0 + meta[:, 2:3]
    row = lax.broadcasted_iota(jnp.int32, (n, BLK), 0)
    valid = lax.rem(row, ROWS) < WINDOW
    match = jnp.where(jnp.logical_and(atom == target_ref[...], valid), 1.0, 0.0).astype(BF16)
    match_ref[...] = match
    down = (((0,), (0,)), ((), ()))
    sums = lax.dot_general(match, x, down, preferred_element_type=F32)
    mass = lax.dot_general(match, meta.astype(BF16), down, preferred_element_type=F32)
    count = out_ref.shape[0]
    mass = jnp.concatenate([mass, jnp.zeros_like(mass)], axis=1)
    both = jnp.concatenate(
        [sums.reshape(count, WINDOW, -1), mass.reshape(count, WINDOW, -1)], axis=1
    )
    out_ref[...] = both.astype(BF16)


def route_kernel(x_ref, match_ref, out_ref):
    x = x_ref[...].reshape(x_ref.shape[0] * ROWS, x_ref.shape[2])
    down = (((0,), (0,)), ((), ()))
    sums = lax.dot_general(match_ref[...], x, down, preferred_element_type=F32)
    sums = sums.reshape(out_ref.shape[0], WINDOW, -1)
    out_ref[...] = jnp.concatenate([sums, jnp.zeros_like(sums)], axis=1).astype(BF16)


def updated(rows, mass, weight, hidden, message, spread):
    mean = rows / (1.0 + mass)
    mean = jnp.concatenate([mean, jnp.zeros_like(mean)], axis=0).astype(BF16)
    update = silu(jnp.dot(mean, weight, preferred_element_type=F32)).astype(BF16)
    filler = jnp.zeros((BLK - ROWS, update.shape[1]), BF16)
    update = jnp.concatenate([update, filler], axis=0)
    picked = jnp.dot(spread, update, preferred_element_type=F32)
    return hidden + message * picked


def second_kernel(
    z_ref, atom_weight_ref, weight_ref, hidden_ref, message_ref, cols_ref, spread_ref, sel_ref,
    hidden_out, message_out, mass_ref, out_ref,
):
    total = jnp.sum(z_ref[...].astype(F32), axis=0)
    mass = jnp.broadcast_to(total[WINDOW:, 0:1], mass_ref.shape)
    mass_ref[...] = mass
    hidden = updated(
        total[:WINDOW], mass[:, 0:1], atom_weight_ref[0], hidden_ref[...], message_ref[...],
        spread_ref[...],
    )
    hidden_out[...] = hidden
    weights = column(cols_ref[...], 2)
    message, payload = message_of(hidden, weight_ref[1], weights, sel_ref[...], 0.0)
    message_out[...] = message
    out_ref[...] = jnp.broadcast_to(payload[None], out_ref.shape)


def last_kernel(
    z_ref, mass_ref, atom_weight_ref, hidden_ref, message_ref, cols_ref, spread_ref, head_ref,
    potential_ref, scaled_ref,
):
    total = jnp.sum(z_ref[...].astype(F32), axis=0)
    hidden = updated(
        total[:WINDOW], mass_ref[:, 0:1], atom_weight_ref[1], hidden_ref[...], message_ref[...],
        spread_ref[...],
    )
    score = jnp.sum(hidden * head_ref[...], axis=1, keepdims=True)
    radius, weights = column(cols_ref[...], 0), column(cols_ref[...], 2)
    potential = radius * (1.0 + jnp.tanh(score))
    scaled = weights * potential
    lane = lax.broadcasted_iota(jnp.int32, (BLK, BLK), 1)
    flat = jnp.where(lane == 0, potential[:BLK], 0.0)
    flat = jnp.where(lane == 1, potential[BLK:], flat)
    flat = jnp.where(lane == 2, scaled[:BLK], flat)
    flat = jnp.where(lane == 3, scaled[BLK:], flat)
    flat = flat.T
    potential_ref[...] = flat[0:2]
    for k in range(scaled_ref.shape[0]):
        scaled_ref[k] = flat[2:4]


def fock_kernel(flipped_ref, psi_ref, scaled_ref, *refs):
    own, outer = refs[:SIDE], refs[SIDE : 2 * SIDE]
    partner, weighted, scratch = refs[2 * SIDE :]
    for k in range(SIDE):
        scratch[2 * k : 2 * k + 2, :] = scaled_ref[k]
    tall = scratch[...].T
    for n in range(2 * SIDE):
        rows = slice(n * BLK, (n + 1) * BLK)
        weighted[rows, :] = (tall[:, n : n + 1] * psi_ref[rows, :].astype(F32)).astype(BF16)
    deep, width = own[0].shape
    for k in range(SIDE):
        terms = jnp.dot(
            flipped_ref[...], weighted[:, k * width : (k + 1) * width], preferred_element_type=F32
        ).astype(BF16)
        own[k][...] = terms[:deep]
        outer[k][...] = terms[deep : 2 * deep]
        partner[k] = terms[2 * deep :]


def turn(axis, step):
    return [(i, (i + step) % SIDE) for i in range(SIDE)]


def across(value):
    groups = lax.axis_size(GRID)
    pairs = [(g, g + 1 if g % 2 else g - 1) for g in range(1, groups - 1)]
    return lax.ppermute(value, GRID, pairs)


def swap(value):
    return lax.ppermute(value, "c", [(0, 1), (1, 0)])


def exchange(parts, axes):
    return lax.all_to_all(parts, axes, split_axis=0, concat_axis=0, tiled=True)


def local(
    basis_values,
    block_lists,
    orbitals,
    point_weights,
    point_atoms,
    embed_scale,
    embed_shift,
    message_weight,
    atom_weight,
    head_weight,
):
    feat = embed_scale.shape[0]
    points = point_weights.shape[0]
    batches, batch_points, _ = basis_values.shape
    deep, width = orbitals.shape
    owned = deep // BLK
    core, zl, y = lax.axis_index("c"), lax.axis_index("zl"), lax.axis_index("y")
    group = lax.axis_index(GRID)
    plane, column_size = lax.axis_size(PLANE), lax.axis_size(COLUMN)

    across_rows = across(orbitals)
    own = [orbitals] + [lax.ppermute(orbitals, "y", turn("y", k)) for k in range(1, SIDE)]
    parts = [basis_values] + [
        lax.ppermute(basis_values, "zl", turn("zl", k)) for k in range(1, SIDE)
    ]
    outer = [across_rows] + [lax.ppermute(across_rows, "y", turn("y", k)) for k in range(1, SIDE)]
    partner = swap(jnp.stack(own))

    first = point_atoms[0]
    half = NATOM // 2
    lowest = jnp.min((point_atoms - first + half + NATOM) % NATOM - half)
    start = (first + lowest + NATOM) % NATOM
    slot = (point_atoms - start + NATOM) % NATOM
    selector = (jnp.arange(ROWS, dtype=jnp.int32)[:, None] == slot[None, :]).astype(BF16)
    spread = (slot[:, None] == jnp.arange(BLK, dtype=jnp.int32)[None, :]).astype(BF16)
    window = (start + jnp.arange(WINDOW, dtype=jnp.int32)) % NATOM
    mass = jnp.sum(
        jnp.where(jnp.arange(WINDOW)[:, None] == slot[None, :], point_weights[None, :], 0.0), axis=1
    )
    facts = jnp.stack([mass, (window // 16).astype(F32), (window % 16).astype(F32)], axis=1)
    meta = jnp.zeros((ROWS, feat), F32).at[WINDOW:, :3].set(facts)
    targets = exchange(jnp.broadcast_to(window.astype(F32), (column_size, WINDOW)), COLUMN)
    targets = targets.reshape(1, column_size * WINDOW)

    shift_k = jnp.arange(SIDE, dtype=jnp.int32)
    from_zl = (zl - shift_k + SIDE) % SIDE
    batch = (from_zl * SIDE + y)[:, None] * batches + jnp.arange(batches, dtype=jnp.int32)[None, :]
    batch = batch.reshape(-1)
    lists = block_lists[batch] - (group - 1) * owned
    third = lists // owned
    low = jnp.where(core == 0, 1, 2)
    place = jnp.where(third == 1, 0, jnp.where(third == 0, low, 3 - low)) * owned + lists % owned
    row = (from_zl[:, None] * batches + jnp.arange(batches, dtype=jnp.int32)[None, :]).reshape(-1)

    total_points = SIDE * points
    dense, flipped = call(
        spread_kernel,
        (shape((total_points, 3 * deep), BF16), shape((3 * deep, total_points), BF16)),
        2 + SIDE,
        smem=(0, 1),
    )(place.astype(jnp.int32), row, *parts)

    psi, squares = call(
        psi_kernel,
        (
            shape((total_points, SIDE * width), BF16),
            shape((SIDE, batches, batch_points), F32),
        ),
        2 + 2 * SIDE,
        scratch=[pltpu.VMEM((total_points, BLK), F32)],
    )(dense, *own, *outer, partner)
    density = jnp.sum(exchange(squares, ("zl",)), axis=0)
    radius = jnp.cbrt(density)

    weights = point_weights.reshape(batches, batch_points)
    square_f32 = shape((points, feat), F32)
    to_plane = shape((plane, ROWS, feat), BF16)
    to_column = shape((column_size, ROWS, feat), BF16)
    tall = shape((batch_points, 8), F32)
    hidden, message, cols, sent = call(
        first_kernel,
        (square_f32, square_f32, tall, to_plane),
        7,
        scratch=[pltpu.VMEM((8, batch_points), F32)],
    )(radius, weights, embed_scale[None], embed_shift[None], message_weight, selector, meta)
    sums, match = call(
        route_first_kernel, (to_column, shape((plane * ROWS, BLK), BF16)), 2
    )(exchange(sent, PLANE), targets)
    hidden, message, mass_rows, sent = call(
        second_kernel, (square_f32, square_f32, shape((WINDOW, BLK), F32), to_plane), 8
    )(
        exchange(sums, COLUMN), atom_weight, message_weight, hidden, message, cols, spread, selector
    )
    sums = call(route_kernel, to_column, 2)(exchange(sent, PLANE), match)
    potential, scaled = call(
        last_kernel,
        (shape((batches, batch_points), F32), shape((SIDE, batches, batch_points), F32)),
        8,
    )(
        exchange(sums, COLUMN), mass_rows, atom_weight, hidden, message, cols, spread,
        head_weight[None],
    )
    scaled = exchange(scaled, ("zl",))

    piece = shape((deep, width), BF16)
    *terms, for_partner = call(
        fock_kernel,
        tuple([piece] * (2 * SIDE) + [shape((SIDE, deep, width), BF16)]),
        3,
        scratch=[
            pltpu.VMEM((total_points, SIDE * width), BF16),
            pltpu.VMEM((8, batch_points), F32),
        ],
    )(flipped, psi, scaled)
    own_terms, outer_terms = terms[:SIDE], terms[SIDE:]

    outer_back = [outer_terms[0]] + [
        lax.ppermute(outer_terms[k], "y", turn("y", -k)) for k in range(1, SIDE)
    ]
    swapped = swap(for_partner)
    outer_sum = sum(t.astype(F32) for t in outer_back).astype(BF16)
    arrived = across(outer_sum)
    both = [own_terms[k].astype(F32) + swapped[k].astype(F32) for k in range(SIDE)]
    back = [
        lax.ppermute(both[k].astype(BF16), "y", turn("y", -k)).astype(F32) for k in range(1, SIDE)
    ]
    fock = both[0] + back[0] + back[1] + back[2] + arrived.astype(F32)
    return fock, potential.reshape(-1)


def solution(mesh):
    finer = Mesh(mesh.devices.reshape(4, 4, 2, 4, 4), AXES)
    atom = ("zl", "y")
    placed = (
        P(AXES, None, None),
        P(GRID, None),
        P(GRID, atom),
        P(AXES),
        P(AXES),
        P(),
        P(),
        P(),
        P(),
        P(),
    )
    return jax.shard_map(
        local,
        mesh=finer,
        in_specs=placed,
        out_specs=(P(GRID, atom), P(AXES)),
        check_vma=False,
    )
```

time: 424 us -> 230 us (0.54)
  waiting for transfers between devices: 209 us -> 50.6 us
  starting transfers between devices: 68.1 us -> 101 us
  matrix products: 23.1 us -> 0 us
  other arithmetic: 28.5 us -> 6.85 us
  local copies, waits for them, and re-layouts: 34 us -> 13.7 us
  Pallas kernels: 0 us -> 14.2 us
  between operations: 14.4 us -> 2.39 us
  blocking collectives: 45.3 us -> 39.1 us
    all_to_all x7 -> x4, waiting for transfers between devices: 108 us -> 33.9 us  [exchange(): return lax.all_to_all(parts, axes, split_axis=0, concat_axis=0, tiled=True)]
    all_gather x2 -> x0, waiting for transfers between devices: 71.1 us -> none  [stacked_from(): parts = lax.all_gather(parts, axes[k])]
    ppermute x4 -> x19, starting transfers between devices: 17.5 us -> 72.1 us  [the longest x2 15.2 us: across(): return lax.ppermute(value, GRID, pairs)]
    scatter-add x1 -> x0, other arithmetic: 24.2 us -> none  [fock_terms(): return total.at[lists.reshape(-1)].add(terms)]
    dot_general x12 -> x0, matrix products: 23.1 us -> none  [the longest x1 10.2 us: fock_terms(): jnp.einsum('bpk,bpo->bko', piece, weighted_psi, preferred_element_type=jn...]
    all_to_all x7 -> x4, starting transfers between devices: 50.5 us -> 28.9 us  [exchange(): return lax.all_to_all(parts, axes, split_axis=0, concat_axis=0, tiled=True)]
    dot_general x1 -> x0, local copies, waits for them, and re-layouts: 17.5 us -> none  [fock_terms(): jnp.einsum('bpk,bpo->bko', piece, weighted_psi, preferred_element_type=jn...]
    pallas_call x0 -> x8, Pallas kernels: none -> 14.2 us  [the longest x1 5.29 us: local(): call(psi_kernel, (shape((total_points, SIDE * width), BF16), shape((SIDE,...]
  transfers between devices with their start and end apart: 13 -> 23, of which waited for: 13 -> 10; matrix products, arithmetic and copies ran while one was open for 2% -> 4% of each run, Pallas kernels for 0% -> 1%
where the time goes in v1:
time: 230 us; the launch traced here: 228 us
  starting transfers between devices  101 us (44%)
  waiting for transfers between devices  50.6 us (22%)
  blocking collectives  39.1 us (17%)
  Pallas kernels  14.2 us (6%)
  local copies, waits for them, and re-layouts  13.7 us (6%)
  other arithmetic  6.85 us (3%)
  between operations  2.39 us (1%)
    all_to_all x3, blocking collectives, exchange(): return lax.all_to_all(parts, axes, split_axis=0, concat_axis=0, tiled=True)  39.1 us
    all_to_all x4, waiting for transfers between devices, exchange(): return lax.all_to_all(parts, axes, split_axis=0, concat_axis=0, tiled=True)  33.9 us
    all_to_all x4, starting transfers between devices, exchange(): return lax.all_to_all(parts, axes, split_axis=0, concat_axis=0, tiled=True)  28.9 us
    ppermute x2, starting transfers between devices, across(): return lax.ppermute(value, GRID, pairs)  15.2 us
    ppermute x3, starting transfers between devices, local(): lax.ppermute(basis_values, 'zl', turn('zl', k))  12 us
    ppermute x3, starting transfers between devices, local(): lax.ppermute(orbitals, 'y', turn('y', k))  10.7 us
    unnamed x37, local copies, waits for them, and re-layouts  10.5 us
    ppermute x3, starting transfers between devices, local(): lax.ppermute(both[k].astype(BF16), 'y', turn('y', -k)).astype(F32)  9.29 us
  transfers between devices with their start and end apart: 23, of which 10 were waited for; matrix products, arithmetic and copies ran while one was open for 4% of the time, Pallas kernels for 1%

profile of v1, /device:TPU:1, one launch (start us, length us, event | category | flops | bytes accessed | tf_op | source)
XLA Modules:
  0.0 227.8 jit_solution(518711921080551483)
XLA Ops:
  0.6 4.5 %collective-permute-start = (bf16[2,128,512]{2,1,0:T(8,128)(2,1)}, bf16[2,128,512]{2,1,0:T(8,128)(2,1)S(1)}, u32[]{:S(2)}, u32[]{:S(2)}) collective-permute-start(bf16[2,128,512]{2,1,0:T(8,128)(2,1)} %refs_0_.2), channel_id=1, source_target_pairs={{0,4},{4,8},{8,12},{12,0},{1,5},{5,9},{9,13},{13,1},{2,6},{6,10},{... | collective-permute-start | bytes 786440 | tf_op jit(solution)/shard_map/ppermute | solution.py:253
  5.2 4.9 %collective-permute-start.1 = (bf16[2,128,512]{2,1,0:T(8,128)(2,1)}, bf16[2,128,512]{2,1,0:T(8,128)(2,1)S(1)}, u32[]{:S(2)}, u32[]{:S(2)}) collective-permute-start(bf16[2,128,512]{2,1,0:T(8,128)(2,1)} %refs_0_.2), channel_id=1, source_target_pairs={{0,8},{4,12},{8,0},{12,4},{1,9},{5,13},{9,1},{13,5},{2,10},{6,14},... | collective-permute-start | bytes 786440 | tf_op jit(solution)/shard_map/ppermute | solution.py:253
  13.3 4.5 %collective-permute-start.4 = (bf16[384,256]{1,0:T(8,128)(2,1)}, bf16[384,256]{1,0:T(8,128)(2,1)S(1)}, u32[]{:S(2)}, u32[]{:S(2)}) collective-permute-start(bf16[384,256]{1,0:T(8,128)(2,1)} %refs_0_.3), channel_id=1, source_target_pairs={{0,2},{1,3},{2,0},{3,1},{4,6},{5,7},{6,4},{7,5},{8,10},{9,11},{10,... | collective-permute-start | bytes 589832 | tf_op jit(solution)/shard_map/ppermute | solution.py:251
  29.6 11.1 %collective-permute-start.6 = (bf16[384,256]{1,0:T(8,128)(2,1)}, bf16[384,256]{1,0:T(8,128)(2,1)S(1)}, u32[]{:S(2)}, u32[]{:S(2)}) collective-permute-start(bf16[384,256]{1,0:T(8,128)(2,1)} %refs_0_.3), channel_id=1, source_target_pairs={{16,32},{32,16},{48,64},{64,48},{80,96},{96,80},{112,128},{128,112... | collective-permute-start | bytes 589832 | tf_op jit(solution)/shard_map/ppermute | solution.py:218
  52.3 4.1 %collective-permute-start.9 = (bf16[384,256]{1,0:T(8,128)(2,1)S(1)}, bf16[384,256]{1,0:T(8,128)(2,1)S(1)}, u32[]{:S(2)}, u32[]{:S(2)}) collective-permute-start(bf16[384,256]{1,0:T(8,128)(2,1)S(1)} %collective-permute-done.6.refs_4_), channel_id=1, source_target_pairs={{0,3},{1,0},{2,1},{3,2},{4,7},{5,4},{6,5},{7,6},{8,11},{9,8},{10,9... | collective-permute-start | bytes 589832 | tf_op jit(solution)/shard_map/ppermute | solution.py:255
  66.0 5.3 %shard_map.114 = (bf16[1024,1024]{1,0:T(8,128)(2,1)S(1)}, f32[4,2,128]{2,1,0:T(2,128)}) custom-call(bf16[1024,1152]{1,0:T(8,128)(2,1)} %copy-done.1, bf16[384,256]{1,0:T(8,128)(2,1)S(1)} %copy-done.4, bf16[384,256]{1,0:T(8,128)(2,1)S(1)} %collective-permute-done.3.refs_1_, bf16[384,256]{1,0:T(8,128)(2,1)S(1)} %collective-permute-done.4.refs_2_, ...), custom_call_target="tpu_custom_call" | custom-call | tf_op jit(solution)/shard_map/pallas_call | solution.py:292
  71.3 3.5 %all-to-all-start = ((f32[4,2,128]{2,1,0:T(2,128)}), f32[4,2,128]{2,1,0:T(2,128)S(1)}, u32[]{:S(2)}, u32[]{:S(2)}) async-start(f32[4,2,128]{2,1,0:T(2,128)} %get-tuple-element.42), calls=%async_computation | async-start | bytes 8192 | tf_op jit(solution)/shard_map/all_to_all | solution.py:226
  74.9 4.5 %all-to-all-done = f32[4,2,128]{2,1,0:T(2,128)S(1)} async-done(((f32[4,2,128]{2,1,0:T(2,128)}), f32[4,2,128]{2,1,0:T(2,128)S(1)}, u32[]{:S(2)}, u32[]{:S(2)}) %all-to-all-start) | async-done | bytes 4128 | tf_op jit(solution)/shard_map/all_to_all | solution.py:226
  80.0 10.7 %all-to-all-start.2 = ((f32[16,1,8]{2,1,0:T(1,128)}), f32[16,1,8]{2,1,0:T(1,128)S(1)}, u32[]{:S(2)}, u32[]{:S(2)}) async-start(f32[16,1,8]{2,1,0:T(1,128)} %broadcast_in_dim.53), calls=%async_computation.2 | async-start | bytes 16384 | tf_op jit(solution)/shard_map/all_to_all | solution.py:226
  92.1 9.8 %all-to-all-done.2 = f32[16,1,8]{2,1,0:T(1,128)S(1)} async-done(((f32[16,1,8]{2,1,0:T(1,128)}), f32[16,1,8]{2,1,0:T(1,128)S(1)}, u32[]{:S(2)}, u32[]{:S(2)}) %all-to-all-start.2) | async-done | bytes 544 | tf_op jit(solution)/shard_map/all_to_all | solution.py:226
  102.0 11.2 %all-to-all-start.1 = ((bf16[32,16,256]{2,1,0:T(8,128)(2,1)}), bf16[32,16,256]{2,1,0:T(8,128)(2,1)S(1)}, u32[]{:S(2)}, u32[]{:S(2)}) async-start(bf16[32,16,256]{2,1,0:T(8,128)(2,1)} %copy-done.7), calls=%async_computation.1 | async-start | bytes 524288 | tf_op jit(solution)/shard_map/all_to_all | solution.py:226
  114.5 7.5 %all-to-all-done.1.x_ref = bf16[32,16,256]{2,1,0:T(8,128)(2,1)S(1)} async-done(((bf16[32,16,256]{2,1,0:T(8,128)(2,1)}), bf16[32,16,256]{2,1,0:T(8,128)(2,1)S(1)}, u32[]{:S(2)}, u32[]{:S(2)}) %all-to-all-start.1) | async-done | bytes 262176 | tf_op jit(solution)/shard_map/all_to_all | solution.py:226
  123.7 3.5 %all-to-all-start.3 = ((bf16[16,16,256]{2,1,0:T(8,128)(2,1)}), bf16[16,16,256]{2,1,0:T(8,128)(2,1)S(1)}, u32[]{:S(2)}, u32[]{:S(2)}) async-start(bf16[16,16,256]{2,1,0:T(8,128)(2,1)} %copy-done.11), calls=%async_computation.3 | async-start | bytes 262144 | tf_op jit(solution)/shard_map/all_to_all | solution.py:226
  127.4 12.0 %all-to-all-done.3.z_ref = bf16[16,16,256]{2,1,0:T(8,128)(2,1)S(1)} async-done(((bf16[16,16,256]{2,1,0:T(8,128)(2,1)}), bf16[16,16,256]{2,1,0:T(8,128)(2,1)S(1)}, u32[]{:S(2)}, u32[]{:S(2)}) %all-to-all-start.3) | async-done | bytes 131104 | tf_op jit(solution)/shard_map/all_to_all | solution.py:226
  140.0 15.1 %all_to_all.36.x_ref = bf16[32,16,256]{2,1,0:T(8,128)(2,1)S(1)} all-to-all(bf16[32,16,256]{2,1,0:T(8,128)(2,1)S(1)} %get-tuple-element.48), channel_id=1, replica_groups=mesh['x'=4,'zh'=4,'c'=2,'zl'=4,'y'=4] {'x','c','y'}, dimensions={0} | all-to-all | bytes 524288 | tf_op jit(solution)/shard_map/all_to_all | solution.py:226
  156.2 15.5 %all_to_all.37.z_ref = bf16[16,16,256]{2,1,0:T(8,128)(2,1)S(1)} all-to-all(bf16[16,16,256]{2,1,0:T(8,128)(2,1)S(1)} %shard_map.118), channel_id=1, replica_groups=mesh['x'=4,'zh'=4,'c'=2,'zl'=4,'y'=4] {'zh','zl'}, dimensions={0} | all-to-all | bytes 262144 | tf_op jit(solution)/shard_map/all_to_all | solution.py:226
  173.0 8.5 %all_to_all.38.scaled_ref = f32[4,2,128]{2,1,0:T(2,128)S(1)} all-to-all(f32[4,2,128]{2,1,0:T(2,128)S(1)} %get-tuple-element.53), channel_id=1, replica_groups=mesh['x'=4,'zh'=4,'c'=2,'zl'=4,'y'=4] {'zl'}, dimensions={0} | all-to-all | bytes 8192 | tf_op jit(solution)/shard_map/all_to_all | solution.py:226
  181.5 4.5 %shard_map.120 = (bf16[384,256]{1,0:T(8,128)(2,1)S(1)}, bf16[384,256]{1,0:T(8,128)(2,1)S(1)}, bf16[384,256]{1,0:T(8,128)(2,1)S(1)}, bf16[384,256]{1,0:T(8,128)(2...) custom-call(bf16[1152,1024]{1,0:T(8,128)(2,1)} %copy-done, ...), custom_call_target="tpu_custom_call" | custom-call | tf_op jit(solution)/shard_map/pallas_call | solution.py:335
  185.9 5.7 %collective-permute-start.11 = (bf16[4,384,256]{2,1,0:T(8,128)(2,1)S(1)}, bf16[4,384,256]{2,1,0:T(8,128)(2,1)S(1)}, u32[]{:S(2)}, u32[]{:S(2)}) collective-permute-start(bf16[4,384,256]{2,1,0:T(8,128)(2,1)S(1)} %get-tuple-element.55), channel_id=1, source_target_pairs={{0,16},{16,0},{1,17},{17,1},{2,18},{18,2},{3,19},{19,3},{4,20},{20... | collective-permute-start | bytes 2359304 | tf_op jit(solution)/shard_map/ppermute | solution.py:222
  193.9 3.7 %collective-permute-start.16 = (bf16[384,256]{1,0:T(8,128)(2,1)S(1)}, bf16[384,256]{1,0:T(8,128)(2,1)S(1)}, u32[]{:S(2)}, u32[]{:S(2)}) collective-permute-start(bf16[384,256]{1,0:T(8,128)(2,1)S(1)} %get-tuple-element.61), channel_id=1, source_target_pairs={{0,2},{1,3},{2,0},{3,1},{4,6},{5,7},{6,4},{7,5},{8,10},{9,11},{10,... | collective-permute-start | bytes 589832 | tf_op jit(solution)/shard_map/ppermute | solution.py:347
  200.4 5.1 %collective-permute-done.17 = bf16[384,256]{1,0:T(8,128)(2,1)S(1)} collective-permute-done((bf16[384,256]{1,0:T(8,128)(2,1)S(1)}, bf16[384,256]{1,0:T(8,128)(2,1)S(1)}, u32[]{:S(2)}, u32[]{:S(2)}) %collective-permute-start.17) | collective-permute-done | bytes 196640 | tf_op jit(solution)/shard_map/ppermute | solution.py:347
  207.8 4.1 %collective-permute-start.18 = (bf16[384,256]{1,0:T(8,128)(2,1)S(1)}, bf16[384,256]{1,0:T(8,128)(2,1)S(1)}, u32[]{:S(2)}, u32[]{:S(2)}) collective-permute-start(bf16[384,256]{1,0:T(8,128)(2,1)S(1)} %add_convert_fusion), channel_id=1, source_target_pairs={{16,32},{32,16},{48,64},{64,48},{80,96},{96,80},{112,128},{128,112... | collective-permute-start | bytes 589832 | tf_op jit(solution)/shard_map/ppermute | solution.py:218
  214.2 5.3 %collective-permute-start.13 = (bf16[384,256]{1,0:T(8,128)(2,1)S(1)}, bf16[384,256]{1,0:T(8,128)(2,1)S(1)}, u32[]{:S(2)}, u32[]{:S(2)}) collective-permute-start(bf16[384,256]{1,0:T(8,128)(2,1)S(1)} %get-tuple-element.66), channel_id=1, source_target_pairs={{0,2},{1,3},{2,0},{3,1},{4,6},{5,7},{6,4},{7,5},{8,10},{9,11},{10,... | collective-permute-start | bytes 589832 | tf_op jit(solution)/shard_map/ppermute | solution.py:354
  221.4 3.6 %collective-permute-done.18 = bf16[384,256]{1,0:T(8,128)(2,1)S(1)} collective-permute-done((bf16[384,256]{1,0:T(8,128)(2,1)S(1)}, bf16[384,256]{1,0:T(8,128)(2,1)S(1)}, u32[]{:S(2)}, u32[]{:S(2)}) %collective-permute-start.18) | collective-permute-done | bytes 196640 | tf_op jit(solution)/shard_map/ppermute | solution.py:218
  (99 shorter events, 57.2 us)
Async XLA Ops:
  0.6 49.5 %collective-permute-start = (bf16[2,128,512]{2,1,0:T(8,128)(2,1)}, bf16[2,128,512]{2,1,0:T(8,128)(2,1)S(1)}, u32[]{:S(2)}, u32[]{:S(2)}) collective-permute-start(bf16[2,128,512]{2,1,0:T(8,128)(2,1)} %refs_0_.2), channel_id=1, source_target_pairs={{0,4},{4,8},{8,12},{12,0},{1,5},{5,9},{9,13},{13,1},{2,6},{6,10},{... | collective-permute-start | bytes 786440 | tf_op jit(solution)/shard_map/ppermute | solution.py:253
  5.2 47.1 %collective-permute-start.1 = (bf16[2,128,512]{2,1,0:T(8,128)(2,1)}, bf16[2,128,512]{2,1,0:T(8,128)(2,1)S(1)}, u32[]{:S(2)}, u32[]{:S(2)}) collective-permute-start(bf16[2,128,512]{2,1,0:T(8,128)(2,1)} %refs_0_.2), channel_id=1, source_target_pairs={{0,8},{4,12},{8,0},{12,4},{1,9},{5,13},{9,1},{13,5},{2,10},{6,14},... | collective-permute-start | bytes 786440 | tf_op jit(solution)/shard_map/ppermute | solution.py:253
  10.1 16.9 %collective-permute-start.3 = (bf16[384,256]{1,0:T(8,128)(2,1)}, bf16[384,256]{1,0:T(8,128)(2,1)S(1)}, u32[]{:S(2)}, u32[]{:S(2)}) collective-permute-start(bf16[384,256]{1,0:T(8,128)(2,1)} %refs_0_.3), channel_id=1, source_target_pairs={{0,1},{1,2},{2,3},{3,0},{4,5},{5,6},{6,7},{7,4},{8,9},{9,10},{10,1... | collective-permute-start | bytes 589832 | tf_op jit(solution)/shard_map/ppermute | solution.py:251
  13.3 16.3 %collective-permute-start.4 = (bf16[384,256]{1,0:T(8,128)(2,1)}, bf16[384,256]{1,0:T(8,128)(2,1)S(1)}, u32[]{:S(2)}, u32[]{:S(2)}) collective-permute-start(bf16[384,256]{1,0:T(8,128)(2,1)} %refs_0_.3), channel_id=1, source_target_pairs={{0,2},{1,3},{2,0},{3,1},{4,6},{5,7},{6,4},{7,5},{8,10},{9,11},{10,... | collective-permute-start | bytes 589832 | tf_op jit(solution)/shard_map/ppermute | solution.py:251
  17.8 22.9 %collective-permute-start.5 = (bf16[384,256]{1,0:T(8,128)(2,1)}, bf16[384,256]{1,0:T(8,128)(2,1)S(1)}, u32[]{:S(2)}, u32[]{:S(2)}) collective-permute-start(bf16[384,256]{1,0:T(8,128)(2,1)} %refs_0_.3), channel_id=1, source_target_pairs={{0,3},{1,0},{2,1},{3,2},{4,7},{5,4},{6,5},{7,6},{8,11},{9,8},{10,9... | collective-permute-start | bytes 589832 | tf_op jit(solution)/shard_map/ppermute | solution.py:251
  27.0 29.4 %collective-permute-start.2 = (bf16[2,128,512]{2,1,0:T(8,128)(2,1)}, bf16[2,128,512]{2,1,0:T(8,128)(2,1)S(1)}, u32[]{:S(2)}, u32[]{:S(2)}) collective-permute-start(bf16[2,128,512]{2,1,0:T(8,128)(2,1)} %refs_0_.2), channel_id=1, source_target_pairs={{0,12},{4,0},{8,4},{12,8},{1,13},{5,1},{9,5},{13,9},{2,14},{6,2},{... | collective-permute-start | bytes 786440 | tf_op jit(solution)/shard_map/ppermute | solution.py:253
  29.6 18.2 %collective-permute-start.6 = (bf16[384,256]{1,0:T(8,128)(2,1)}, bf16[384,256]{1,0:T(8,128)(2,1)S(1)}, u32[]{:S(2)}, u32[]{:S(2)}) collective-permute-start(bf16[384,256]{1,0:T(8,128)(2,1)} %refs_0_.3), channel_id=1, source_target_pairs={{16,32},{32,16},{48,64},{64,48},{80,96},{96,80},{112,128},{128,112... | collective-permute-start | bytes 589832 | tf_op jit(solution)/shard_map/ppermute | solution.py:218
  41.8 21.3 %collective-permute-start.10 = (bf16[4,384,256]{2,1,0:T(8,128)(2,1)S(1)}, bf16[4,384,256]{2,1,0:T(8,128)(2,1)S(1)}, u32[]{:S(2)}, u32[]{:S(2)}) collective-permute-start(bf16[4,384,256]{2,1,0:T(8,128)(2,1)S(1)} %pad_maximum_fusion), channel_id=1, source_target_pairs={{0,16},{16,0},{1,17},{17,1},{2,18},{18,2},{3,19},{19,3},{4,20},{20... | collective-permute-start | bytes 2359304 | tf_op jit(solution)/shard_map/ppermute | solution.py:222
  47.8 13.8 %collective-permute-start.7 = (bf16[384,256]{1,0:T(8,128)(2,1)S(1)}, bf16[384,256]{1,0:T(8,128)(2,1)S(1)}, u32[]{:S(2)}, u32[]{:S(2)}) collective-permute-start(bf16[384,256]{1,0:T(8,128)(2,1)S(1)} %collective-permute-done.6.refs_4_), channel_id=1, source_target_pairs={{0,1},{1,2},{2,3},{3,0},{4,5},{5,6},{6,7},{7,4},{8,9},{9,10},{10,1... | collective-permute-start | bytes 589832 | tf_op jit(solution)/shard_map/ppermute | solution.py:255
  50.1 11.5 %collective-permute-start.8 = (bf16[384,256]{1,0:T(8,128)(2,1)S(1)}, bf16[384,256]{1,0:T(8,128)(2,1)S(1)}, u32[]{:S(2)}, u32[]{:S(2)}) collective-permute-start(bf16[384,256]{1,0:T(8,128)(2,1)S(1)} %collective-permute-done.6.refs_4_), channel_id=1, source_target_pairs={{0,2},{1,3},{2,0},{3,1},{4,6},{5,7},{6,4},{7,5},{8,10},{9,11},{10,... | collective-permute-start | bytes 589832 | tf_op jit(solution)/shard_map/ppermute | solution.py:255
  52.3 10.8 %collective-permute-start.9 = (bf16[384,256]{1,0:T(8,128)(2,1)S(1)}, bf16[384,256]{1,0:T(8,128)(2,1)S(1)}, u32[]{:S(2)}, u32[]{:S(2)}) collective-permute-start(bf16[384,256]{1,0:T(8,128)(2,1)S(1)} %collective-permute-done.6.refs_4_), channel_id=1, source_target_pairs={{0,3},{1,0},{2,1},{3,2},{4,7},{5,4},{6,5},{7,6},{8,11},{9,8},{10,9... | collective-permute-start | bytes 589832 | tf_op jit(solution)/shard_map/ppermute | solution.py:255
  71.3 100.4 %copy-start.17 = (f32[256]{0:T(256)S(1)}, f32[256]{0:T(256)}, u32[]{:S(2)}) copy-start(f32[256]{0:T(256)} %param.21) | copy-start | bytes 3076
  71.3 8.1 %all-to-all-start = ((f32[4,2,128]{2,1,0:T(2,128)}), f32[4,2,128]{2,1,0:T(2,128)S(1)}, u32[]{:S(2)}, u32[]{:S(2)}) async-start(f32[4,2,128]{2,1,0:T(2,128)} %get-tuple-element.42), calls=%async_computation | async-start | bytes 8192 | tf_op jit(solution)/shard_map/all_to_all | solution.py:226
  80.0 21.9 %all-to-all-start.2 = ((f32[16,1,8]{2,1,0:T(1,128)}), f32[16,1,8]{2,1,0:T(1,128)S(1)}, u32[]{:S(2)}, u32[]{:S(2)}) async-start(f32[16,1,8]{2,1,0:T(1,128)} %broadcast_in_dim.53), calls=%async_computation.2 | async-start | bytes 16384 | tf_op jit(solution)/shard_map/all_to_all | solution.py:226
  102.0 20.0 %all-to-all-start.1 = ((bf16[32,16,256]{2,1,0:T(8,128)(2,1)}), bf16[32,16,256]{2,1,0:T(8,128)(2,1)S(1)}, u32[]{:S(2)}, u32[]{:S(2)}) async-start(bf16[32,16,256]{2,1,0:T(8,128)(2,1)} %copy-done.7), calls=%async_computation.1 | async-start | bytes 524288 | tf_op jit(solution)/shard_map/all_to_all | solution.py:226
  123.7 15.6 %all-to-all-start.3 = ((bf16[16,16,256]{2,1,0:T(8,128)(2,1)}), bf16[16,16,256]{2,1,0:T(8,128)(2,1)S(1)}, u32[]{:S(2)}, u32[]{:S(2)}) async-start(bf16[16,16,256]{2,1,0:T(8,128)(2,1)} %copy-done.11), calls=%async_computation.3 | async-start | bytes 262144 | tf_op jit(solution)/shard_map/all_to_all | solution.py:226
  185.9 26.0 %collective-permute-start.11 = (bf16[4,384,256]{2,1,0:T(8,128)(2,1)S(1)}, bf16[4,384,256]{2,1,0:T(8,128)(2,1)S(1)}, u32[]{:S(2)}, u32[]{:S(2)}) collective-permute-start(bf16[4,384,256]{2,1,0:T(8,128)(2,1)S(1)} %get-tuple-element.55), channel_id=1, source_target_pairs={{0,16},{16,0},{1,17},{17,1},{2,18},{18,2},{3,19},{19,3},{4,20},{20... | collective-permute-start | bytes 2359304 | tf_op jit(solution)/shard_map/ppermute | solution.py:222
  191.6 13.8 %collective-permute-start.17 = (bf16[384,256]{1,0:T(8,128)(2,1)S(1)}, bf16[384,256]{1,0:T(8,128)(2,1)S(1)}, u32[]{:S(2)}, u32[]{:S(2)}) collective-permute-start(bf16[384,256]{1,0:T(8,128)(2,1)S(1)} %get-tuple-element.62), channel_id=1, source_target_pairs={{0,1},{1,2},{2,3},{3,0},{4,5},{5,6},{6,7},{7,4},{8,9},{9,10},{10,1... | collective-permute-start | bytes 589832 | tf_op jit(solution)/shard_map/ppermute | solution.py:347
  193.9 11.6 %collective-permute-start.16 = (bf16[384,256]{1,0:T(8,128)(2,1)S(1)}, bf16[384,256]{1,0:T(8,128)(2,1)S(1)}, u32[]{:S(2)}, u32[]{:S(2)}) collective-permute-start(bf16[384,256]{1,0:T(8,128)(2,1)S(1)} %get-tuple-element.61), channel_id=1, source_target_pairs={{0,2},{1,3},{2,0},{3,1},{4,6},{5,7},{6,4},{7,5},{8,10},{9,11},{10,... | collective-permute-start | bytes 589832 | tf_op jit(solution)/shard_map/ppermute | solution.py:347
  197.5 10.1 %collective-permute-start.15 = (bf16[384,256]{1,0:T(8,128)(2,1)S(1)}, bf16[384,256]{1,0:T(8,128)(2,1)S(1)}, u32[]{:S(2)}, u32[]{:S(2)}) collective-permute-start(bf16[384,256]{1,0:T(8,128)(2,1)S(1)} %get-tuple-element.60), channel_id=1, source_target_pairs={{0,3},{1,0},{2,1},{3,2},{4,7},{5,4},{6,5},{7,6},{8,11},{9,8},{10,9... | collective-permute-start | bytes 589832 | tf_op jit(solution)/shard_map/ppermute | solution.py:347
  207.8 17.2 %collective-permute-start.18 = (bf16[384,256]{1,0:T(8,128)(2,1)S(1)}, bf16[384,256]{1,0:T(8,128)(2,1)S(1)}, u32[]{:S(2)}, u32[]{:S(2)}) collective-permute-start(bf16[384,256]{1,0:T(8,128)(2,1)S(1)} %add_convert_fusion), channel_id=1, source_target_pairs={{16,32},{32,16},{48,64},{64,48},{80,96},{96,80},{112,128},{128,112... | collective-permute-start | bytes 589832 | tf_op jit(solution)/shard_map/ppermute | solution.py:218
  212.1 12.9 %collective-permute-start.14 = (bf16[384,256]{1,0:T(8,128)(2,1)S(1)}, bf16[384,256]{1,0:T(8,128)(2,1)S(1)}, u32[]{:S(2)}, u32[]{:S(2)}) collective-permute-start(bf16[384,256]{1,0:T(8,128)(2,1)S(1)} %get-tuple-element.65), channel_id=1, source_target_pairs={{0,1},{1,2},{2,3},{3,0},{4,5},{5,6},{6,7},{7,4},{8,9},{9,10},{10,1... | collective-permute-start | bytes 589832 | tf_op jit(solution)/shard_map/ppermute | solution.py:354
  214.2 10.8 %collective-permute-start.13 = (bf16[384,256]{1,0:T(8,128)(2,1)S(1)}, bf16[384,256]{1,0:T(8,128)(2,1)S(1)}, u32[]{:S(2)}, u32[]{:S(2)}) collective-permute-start(bf16[384,256]{1,0:T(8,128)(2,1)S(1)} %get-tuple-element.66), channel_id=1, source_target_pairs={{0,2},{1,3},{2,0},{3,1},{4,6},{5,7},{6,4},{7,5},{8,10},{9,11},{10,... | collective-permute-start | bytes 589832 | tf_op jit(solution)/shard_map/ppermute | solution.py:354
  219.5 7.5 %collective-permute-start.12 = (bf16[384,256]{1,0:T(8,128)(2,1)S(1)}, bf16[384,256]{1,0:T(8,128)(2,1)S(1)}, u32[]{:S(2)}, u32[]{:S(2)}) collective-permute-start(bf16[384,256]{1,0:T(8,128)(2,1)S(1)} %get-tuple-element.64), channel_id=1, source_target_pairs={{0,3},{1,0},{2,1},{3,2},{4,7},{5,4},{6,5},{7,6},{8,11},{9,8},{10,9... | collective-permute-start | bytes 589832 | tf_op jit(solution)/shard_map/ppermute | solution.py:354
  (17 other events, 261.0 us)

commit v2 on v1

--- a/solution.py
+++ b/solution.py
@@ -18,7 +18,7 @@
 F32 = jnp.float32
 BF16 = jnp.bfloat16
 
-VMEM = 48 * 1024 * 1024
+VMEM = 16 * 1024 * 1024
 
 
 def call(kernel, out_shape, n_in, smem=(), scratch=(), **kw):
@@ -41,27 +41,77 @@
     return jax.ShapeDtypeStruct(dims, dtype)
 
 
-def spread_kernel(place_ref, row_ref, *refs):
+def prepare_kernel(atoms_ref, weights_ref, sel_ref, spread_ref, meta_ref, window_ref, scratch):
+    atoms = atoms_ref[...].astype(F32)
+    half = NATOM // 2
+    first = atoms[0:1, 0:1]
+    apart = atoms - first
+    apart = jnp.where(apart < -half, apart + NATOM, jnp.where(apart >= half, apart - NATOM, apart))
+    start = first + jnp.min(jnp.min(apart, axis=1, keepdims=True), axis=0, keepdims=True)
+    start = jnp.where(start < 0, start + NATOM, jnp.where(start >= NATOM, start - NATOM, start))
+    slot = atoms - start
+    slot = jnp.where(slot < 0, slot + NATOM, slot)
+    points = 2 * BLK
+    wide = jnp.concatenate([slot[0:1], slot[1:2]], axis=1)
+    weights = jnp.concatenate([weights_ref[0:1], weights_ref[1:2]], axis=1)
+    rows = lax.broadcasted_iota(jnp.int32, (ROWS, points), 0).astype(F32)
+    chosen = rows == wide
+    sel_ref[...] = jnp.where(chosen, 1.0, 0.0).astype(BF16)
+    scratch[...] = jnp.zeros_like(scratch)
+    scratch[0:2, :] = slot
+    tall = scratch[...].T
+    lanes = lax.broadcasted_iota(jnp.int32, (points, BLK), 1).astype(F32)
+    spread_ref[...] = jnp.where(lanes == column(tall, 0), 1.0, 0.0).astype(BF16)
+    mass = jnp.sum(jnp.where(chosen, weights, 0.0), axis=1, keepdims=True)[:WINDOW]
+    atom = start + lax.broadcasted_iota(jnp.int32, (WINDOW, 1), 0).astype(F32)
+    atom = jnp.where(atom >= NATOM, atom - NATOM, atom)
+    high = jnp.floor(atom * (1.0 / 16.0))
+    low = atom - 16.0 * high
+    lane = lax.broadcasted_iota(jnp.int32, (WINDOW, points), 1)
+    facts = jnp.where(lane == 0, mass, jnp.where(lane == 1, high, jnp.where(lane == 2, low, 0.0)))
+    meta_ref[...] = jnp.concatenate([jnp.zeros_like(facts), facts], axis=0)
+    row = lax.broadcasted_iota(jnp.int32, window_ref.shape, 0)
+    window_ref[...] = jnp.where(
+        row == 0, high[0:1], jnp.where(row == 1, low[0:1], 0.0)
+    ).astype(BF16)
+
+
+def spread_kernel(place_ref, list_ref, *refs):
     parts, (dense_ref, flipped_ref) = refs[:SIDE], refs[SIDE:]
+    zl, y, group, core = (place_ref[i] for i in range(4))
     dense_ref[...] = jnp.zeros_like(dense_ref)
     flipped_ref[...] = jnp.zeros_like(flipped_ref)
+    per, _, wide = parts[0].shape
+    owned = dense_ref.shape[1] // BLK // 3
     for k, part in enumerate(parts):
-        for r in range(part.shape[0]):
-            n = k * part.shape[0] + r
-            row = pl.multiple_of(row_ref[n] * BLK, BLK)
-            for j in range(part.shape[2] // BLK):
-                col = pl.multiple_of(place_ref[n, j] * BLK, BLK)
+        origin = lax.rem(zl - k + SIDE, SIDE)
+        for r in range(per):
+            batch = (origin * SIDE + y) * per + r
+            row = pl.multiple_of((origin * per + r) * BLK, BLK)
+            for j in range(wide // BLK):
+                block = list_ref[batch, j] - (group - 1) * owned
+                below, above = block < owned, block >= 2 * owned
+                outside = jnp.logical_or(below, above)
+                outer = below == (core == 0)
+                within = jnp.where(below, block, jnp.where(above, block - 2 * owned, block - owned))
+                third = jnp.where(outside, jnp.where(outer, 1, 2), 0)
+                col = pl.multiple_of((third * owned + within) * BLK, BLK)
                 tile = part[r, :, j * BLK : (j + 1) * BLK]
                 dense_ref[pl.ds(row, BLK), pl.ds(col, BLK)] = tile
                 flipped_ref[pl.ds(col, BLK), pl.ds(row, BLK)] = tile.T
 
 
-def psi_kernel(dense_ref, *refs):
-    own, outer = refs[:SIDE], refs[SIDE : 2 * SIDE]
-    partner, psi_ref, dens_ref, acc_ref = refs[2 * SIDE :]
-    width = own[0].shape[1]
-    for k in range(SIDE):
-        chosen = jnp.concatenate([own[k][...], outer[k][...], partner[k]], axis=0)
+def psi_kernel(place_ref, dense_ref, rows_ref, psi_ref, dens_ref, acc_ref):
+    _, _, _, core, x = (place_ref[i] for i in range(5))
+    side, tall, width = rows_ref.shape
+    deep = dense_ref.shape[1] // 3
+    lane = lax.broadcasted_iota(jnp.int32, (1, BLK), 1)
+    device = lane // WINDOW
+    atoms = (lane % WINDOW).astype(F32)
+    for k in range(side):
+        chosen = jnp.concatenate(
+            [rows_ref[k, :deep], rows_ref[k, deep + ROWS : tall - ROWS]], axis=0
+        )
         psi = jnp.dot(dense_ref[...], chosen, preferred_element_type=F32).astype(BF16)
         psi_ref[:, k * width : (k + 1) * width] = psi
         wide = psi.astype(F32)
@@ -71,9 +121,19 @@
             acc_ref[...] = part
         else:
             acc_ref[...] += part
+        for at, owner in ((deep, core), (tall - ROWS, 1 - core)):
+            window = rows_ref[k, at : at + ROWS, :BLK].astype(F32)
+            window = window[0:1] * 16.0 + window[1:2]
+            atoms += jnp.where(device == owner * side + k, window, 0.0)
+    atoms = jnp.where(atoms >= NATOM, atoms - NATOM, atoms)
+    atoms = jnp.where(device < 2 * side, atoms, 0.0)
+    dens_ref[...] = jnp.zeros_like(dens_ref)
+    for n in range(dens_ref.shape[0]):
+        dens_ref[n, 2:3, :] = atoms
     for n in range(acc_ref.shape[0] // BLK):
         tile = acc_ref[n * BLK : (n + 1) * BLK, :].T
-        dens_ref[n // 2, n % 2 : n % 2 + 1, :] = 2.0 * jnp.sum(tile, axis=0, keepdims=True)
+        row = 2.0 * jnp.sum(tile, axis=0, keepdims=True)
+        dens_ref[x * side + n // 2, n % 2 : n % 2 + 1, :] = row
 
 
 def silu(x):
@@ -108,15 +168,21 @@
     out_ref[...] = jnp.broadcast_to(payload[None], out_ref.shape)
 
 
-def route_first_kernel(x_ref, target_ref, out_ref, match_ref):
+def route_first_kernel(place_ref, x_ref, target_ref, out_ref, match_ref):
     n = x_ref.shape[0] * ROWS
+    zl = place_ref[0]
+    half = [target_ref[k * SIDE + zl, 2:3, :] for k in range(SIDE)]
+    targets = jnp.concatenate(
+        [half[0] + pltpu.roll(half[1], BLK // 2, 1), half[2] + pltpu.roll(half[3], BLK // 2, 1)],
+        axis=1,
+    )
     x = x_ref[...].reshape(n, x_ref.shape[2])
     meta = x[:, :BLK].astype(F32)
     meta = jnp.concatenate([meta[WINDOW:], meta[:WINDOW]], axis=0)
     atom = meta[:, 1:2] * 16.0 + meta[:, 2:3]
-    row = lax.broadcasted_iota(jnp.int32, (n, BLK), 0)
+    row = lax.broadcasted_iota(jnp.int32, (n, targets.shape[1]), 0)
     valid = lax.rem(row, ROWS) < WINDOW
-    match = jnp.where(jnp.logical_and(atom == target_ref[...], valid), 1.0, 0.0).astype(BF16)
+    match = jnp.where(jnp.logical_and(atom == targets, valid), 1.0, 0.0).astype(BF16)
     match_ref[...] = match
     down = (((0,), (0,)), ((), ()))
     sums = lax.dot_general(match, x, down, preferred_element_type=F32)
@@ -189,27 +255,25 @@
         scaled_ref[k] = flat[2:4]
 
 
-def fock_kernel(flipped_ref, psi_ref, scaled_ref, *refs):
-    own, outer = refs[:SIDE], refs[SIDE : 2 * SIDE]
-    partner, weighted, scratch = refs[2 * SIDE :]
-    for k in range(SIDE):
+def fock_kernel(flipped_ref, psi_ref, scaled_ref, out_ref, weighted, scratch):
+    side, _, width = out_ref.shape
+    for k in range(side):
         scratch[2 * k : 2 * k + 2, :] = scaled_ref[k]
     tall = scratch[...].T
-    for n in range(2 * SIDE):
+    for n in range(2 * side):
         rows = slice(n * BLK, (n + 1) * BLK)
         weighted[rows, :] = (tall[:, n : n + 1] * psi_ref[rows, :].astype(F32)).astype(BF16)
-    deep, width = own[0].shape
-    for k in range(SIDE):
-        terms = jnp.dot(
+    for k in range(side):
+        out_ref[k] = jnp.dot(
             flipped_ref[...], weighted[:, k * width : (k + 1) * width], preferred_element_type=F32
         ).astype(BF16)
-        own[k][...] = terms[:deep]
-        outer[k][...] = terms[deep : 2 * deep]
-        partner[k] = terms[2 * deep :]
-
-
-def turn(axis, step):
-    return [(i, (i + step) % SIDE) for i in range(SIDE)]
+
+
+def from_behind(value, axis):
+    return [value] + [
+        lax.ppermute(value, axis, [(i, (i + k) % SIDE) for i in range(SIDE)])
+        for k in range(1, SIDE)
+    ]
 
 
 def across(value):
@@ -242,44 +306,26 @@
     points = point_weights.shape[0]
     batches, batch_points, _ = basis_values.shape
     deep, width = orbitals.shape
-    owned = deep // BLK
-    core, zl, y = lax.axis_index("c"), lax.axis_index("zl"), lax.axis_index("y")
-    group = lax.axis_index(GRID)
+    place = jnp.stack([lax.axis_index(a) for a in ("zl", "y", GRID, "c", "x")]).astype(jnp.int32)
     plane, column_size = lax.axis_size(PLANE), lax.axis_size(COLUMN)
-
-    across_rows = across(orbitals)
-    own = [orbitals] + [lax.ppermute(orbitals, "y", turn("y", k)) for k in range(1, SIDE)]
-    parts = [basis_values] + [
-        lax.ppermute(basis_values, "zl", turn("zl", k)) for k in range(1, SIDE)
-    ]
-    outer = [across_rows] + [lax.ppermute(across_rows, "y", turn("y", k)) for k in range(1, SIDE)]
-    partner = swap(jnp.stack(own))
-
-    first = point_atoms[0]
-    half = NATOM // 2
-    lowest = jnp.min((point_atoms - first + half + NATOM) % NATOM - half)
-    start = (first + lowest + NATOM) % NATOM
-    slot = (point_atoms - start + NATOM) % NATOM
-    selector = (jnp.arange(ROWS, dtype=jnp.int32)[:, None] == slot[None, :]).astype(BF16)
-    spread = (slot[:, None] == jnp.arange(BLK, dtype=jnp.int32)[None, :]).astype(BF16)
-    window = (start + jnp.arange(WINDOW, dtype=jnp.int32)) % NATOM
-    mass = jnp.sum(
-        jnp.where(jnp.arange(WINDOW)[:, None] == slot[None, :], point_weights[None, :], 0.0), axis=1
-    )
-    facts = jnp.stack([mass, (window // 16).astype(F32), (window % 16).astype(F32)], axis=1)
-    meta = jnp.zeros((ROWS, feat), F32).at[WINDOW:, :3].set(facts)
-    targets = exchange(jnp.broadcast_to(window.astype(F32), (column_size, WINDOW)), COLUMN)
-    targets = targets.reshape(1, column_size * WINDOW)
-
-    shift_k = jnp.arange(SIDE, dtype=jnp.int32)
-    from_zl = (zl - shift_k + SIDE) % SIDE
-    batch = (from_zl * SIDE + y)[:, None] * batches + jnp.arange(batches, dtype=jnp.int32)[None, :]
-    batch = batch.reshape(-1)
-    lists = block_lists[batch] - (group - 1) * owned
-    third = lists // owned
-    low = jnp.where(core == 0, 1, 2)
-    place = jnp.where(third == 1, 0, jnp.where(third == 0, low, 3 - low)) * owned + lists % owned
-    row = (from_zl[:, None] * batches + jnp.arange(batches, dtype=jnp.int32)[None, :]).reshape(-1)
+    square_f32 = shape((points, feat), F32)
+
+    outer = across(orbitals)
+    parts = from_behind(basis_values, "zl")
+    selector, spread, meta, window = call(
+        prepare_kernel,
+        (
+            shape((ROWS, points), BF16),
+            shape((points, BLK), BF16),
+            shape((ROWS, feat), F32),
+            shape((ROWS, width), BF16),
+        ),
+        2,
+        scratch=[pltpu.VMEM((8, batch_points), F32)],
+    )(point_atoms.reshape(batches, batch_points), point_weights.reshape(batches, batch_points))
+    own = jnp.concatenate([orbitals, window], axis=0)
+    rows = jnp.concatenate([own, outer, swap(own)], axis=0)
+    gathered = exchange(jnp.broadcast_to(rows, (SIDE, *rows.shape)), ("y",))
 
     total_points = SIDE * points
     dense, flipped = call(
@@ -287,73 +333,65 @@
         (shape((total_points, 3 * deep), BF16), shape((3 * deep, total_points), BF16)),
         2 + SIDE,
         smem=(0, 1),
-    )(place.astype(jnp.int32), row, *parts)
-
+    )(place, block_lists, *parts)
     psi, squares = call(
         psi_kernel,
         (
             shape((total_points, SIDE * width), BF16),
-            shape((SIDE, batches, batch_points), F32),
+            shape((SIDE * SIDE, 4, batch_points), F32),
         ),
-        2 + 2 * SIDE,
+        3,
+        smem=(0,),
         scratch=[pltpu.VMEM((total_points, BLK), F32)],
-    )(dense, *own, *outer, partner)
-    density = jnp.sum(exchange(squares, ("zl",)), axis=0)
-    radius = jnp.cbrt(density)
+    )(place, dense, gathered)
+    squares = exchange(squares, ("x", "zl"))
+    radius = jnp.cbrt(jnp.sum(squares[:, :2], axis=0))
 
     weights = point_weights.reshape(batches, batch_points)
-    square_f32 = shape((points, feat), F32)
     to_plane = shape((plane, ROWS, feat), BF16)
     to_column = shape((column_size, ROWS, feat), BF16)
     tall = shape((batch_points, 8), F32)
     hidden, message, cols, sent = call(
         first_kernel,
-        (square_f32, square_f32, tall, to_plane),
+        (square_f32, square_f32, tall, to_column),
         7,
         scratch=[pltpu.VMEM((8, batch_points), F32)],
     )(radius, weights, embed_scale[None], embed_shift[None], message_weight, selector, meta)
     sums, match = call(
-        route_first_kernel, (to_column, shape((plane * ROWS, BLK), BF16)), 2
-    )(exchange(sent, PLANE), targets)
+        route_first_kernel,
+        (to_plane, shape((column_size * ROWS, plane * WINDOW), BF16)),
+        3,
+        smem=(0,),
+    )(place, exchange(sent, COLUMN), squares)
     hidden, message, mass_rows, sent = call(
-        second_kernel, (square_f32, square_f32, shape((WINDOW, BLK), F32), to_plane), 8
+        second_kernel, (square_f32, square_f32, shape((WINDOW, BLK), F32), to_column), 8
     )(
-        exchange(sums, COLUMN), atom_weight, message_weight, hidden, message, cols, spread, selector
-    )
-    sums = call(route_kernel, to_column, 2)(exchange(sent, PLANE), match)
+        exchange(sums, PLANE), atom_weight, message_weight, hidden, message, cols, spread, selector
+    )
+    sums = call(route_kernel, to_plane, 2)(exchange(sent, COLUMN), match)
     potential, scaled = call(
         last_kernel,
         (shape((batches, batch_points), F32), shape((SIDE, batches, batch_points), F32)),
         8,
     )(
-        exchange(sums, COLUMN), mass_rows, atom_weight, hidden, message, cols, spread,
+        exchange(sums, PLANE), mass_rows, atom_weight, hidden, message, cols, spread,
         head_weight[None],
     )
     scaled = exchange(scaled, ("zl",))
 
-    piece = shape((deep, width), BF16)
-    *terms, for_partner = call(
+    terms = call(
         fock_kernel,
-        tuple([piece] * (2 * SIDE) + [shape((SIDE, deep, width), BF16)]),
+        shape((SIDE, 3 * deep, width), BF16),
         3,
         scratch=[
             pltpu.VMEM((total_points, SIDE * width), BF16),
             pltpu.VMEM((8, batch_points), F32),
         ],
     )(flipped, psi, scaled)
-    own_terms, outer_terms = terms[:SIDE], terms[SIDE:]
-
-    outer_back = [outer_terms[0]] + [
-        lax.ppermute(outer_terms[k], "y", turn("y", -k)) for k in range(1, SIDE)
-    ]
-    swapped = swap(for_partner)
-    outer_sum = sum(t.astype(F32) for t in outer_back).astype(BF16)
-    arrived = across(outer_sum)
-    both = [own_terms[k].astype(F32) + swapped[k].astype(F32) for k in range(SIDE)]
-    back = [
-        lax.ppermute(both[k].astype(BF16), "y", turn("y", -k)).astype(F32) for k in range(1, SIDE)
-    ]
-    fock = both[0] + back[0] + back[1] + back[2] + arrived.astype(F32)
+    total = jnp.sum(exchange(terms, ("y",)).astype(F32), axis=0)
+    own, outer, partner = total[:deep], total[deep : 2 * deep], total[2 * deep :]
+    arrived = across(outer.astype(BF16))
+    fock = own + arrived.astype(F32) + swap(partner.astype(BF16)).astype(F32)
     return fock, potential.reshape(-1)
 
 

time: 230 us -> 219 us (0.952)
  blocking collectives: 39.1 us -> 132 us
  starting transfers between devices: 101 us -> 34.7 us
  waiting for transfers between devices: 50.6 us -> 23.6 us
  other arithmetic: 6.85 us -> 3.16 us
    all_to_all x3 -> x7, blocking collectives: 39.1 us -> 132 us  [exchange(): return lax.all_to_all(parts, axes, split_axis=0, concat_axis=0, tiled=True)]
    ppermute x15 -> x3, starting transfers between devices: 49.3 us -> 10.3 us  [from_behind(): lax.ppermute(value, axis, [(i, (i + k) % SIDE) for i in range(SIDE)])]
    all_to_all x4 -> x1, waiting for transfers between devices: 33.9 us -> 0.01 us  [exchange(): return lax.all_to_all(parts, axes, split_axis=0, concat_axis=0, tiled=True)]
    all_to_all x4 -> x1, starting transfers between devices: 28.9 us -> 3.77 us  [exchange(): return lax.all_to_all(parts, axes, split_axis=0, concat_axis=0, tiled=True)]
    ppermute x2, waiting for transfers between devices: 6.08 us -> 20.2 us  [across(): return lax.ppermute(value, GRID, pairs)]
    ppermute x15 -> x3, waiting for transfers between devices: 10.6 us -> 3.46 us  [from_behind(): lax.ppermute(value, axis, [(i, (i + k) % SIDE) for i in range(SIDE)])]
    ppermute x2, starting transfers between devices: 15.2 us -> 9.89 us  [across(): return lax.ppermute(value, GRID, pairs)]
    ppermute x2, starting transfers between devices: 7.61 us -> 10.7 us  [swap(): return lax.ppermute(value, 'c', [(0, 1), (1, 0)])]
  transfers between devices with their start and end apart: 23 -> 8, of which waited for: 10 -> 4; matrix products, arithmetic and copies ran while one was open for 4% -> 1% of each run, Pallas kernels for 1% -> 1%
where the time goes in v2:
time: 219 us; the launch traced here: 217 us
  blocking collectives  132 us (60%)
  starting transfers between devices  34.7 us (16%)
  waiting for transfers between devices  23.6 us (11%)
  Pallas kernels  11.9 us (5%)
  local copies, waits for them, and re-layouts  11.4 us (5%)
  other arithmetic  3.16 us (1%)
    all_to_all x7, blocking collectives, exchange(): return lax.all_to_all(parts, axes, split_axis=0, concat_axis=0, tiled=True)  132 us
    ppermute x2, waiting for transfers between devices, across(): return lax.ppermute(value, GRID, pairs)  20.2 us
    ppermute x2, starting transfers between devices, swap(): return lax.ppermute(value, 'c', [(0, 1), (1, 0)])  10.7 us
    ppermute x3, starting transfers between devices, from_behind(): lax.ppermute(value, axis, [(i, (i + k) % SIDE) for i in range(SIDE)])  10.3 us
    ppermute x2, starting transfers between devices, across(): return lax.ppermute(value, GRID, pairs)  9.89 us
    unnamed x41, local copies, waits for them, and re-layouts  9.17 us
  transfers between devices with their start and end apart: 8, of which 4 were waited for; matrix products, arithmetic and copies ran while one was open for 1% of the time, Pallas kernels for 1%

profile of v2, /device:TPU:1, one launch (start us, length us, event | category | flops | bytes accessed | tf_op | source)
XLA Modules:
  0.0 217.4 jit_solution(12807453900573889420)
XLA Ops:
  4.6 8.8 %collective-permute-start.4 = (bf16[400,256]{1,0:T(8,128)(2,1)S(1)}, bf16[400,256]{1,0:T(8,128)(2,1)S(1)}, u32[]{:S(2)}, u32[]{:S(2)}) collective-permute-start(bf16[400,256]{1,0:T(8,128)(2,1)S(1)} %pad_maximum_fusion.1), channel_id=1, source_target_pairs={{0,16},{16,0},{1,17},{17,1},{2,18},{18,2},{3,19},{19,3},{4,20},{20... | collective-permute-start | bytes 614408 | tf_op jit(solution)/shard_map/ppermute | solution.py:286
  13.4 3.3 %collective-permute-start.3 = (bf16[384,256]{1,0:T(8,128)(2,1)}, bf16[384,256]{1,0:T(8,128)(2,1)S(1)}, u32[]{:S(2)}, u32[]{:S(2)}) collective-permute-start(bf16[384,256]{1,0:T(8,128)(2,1)} %param.12), channel_id=1, source_target_pairs={{16,32},{32,16},{48,64},{64,48},{80,96},{96,80},{112,128},{128,112... | collective-permute-start | bytes 589832 | tf_op jit(solution)/shard_map/ppermute | solution.py:282
  16.7 11.4 %collective-permute-done.3 = bf16[384,256]{1,0:T(8,128)(2,1)S(1)} collective-permute-done((bf16[384,256]{1,0:T(8,128)(2,1)}, bf16[384,256]{1,0:T(8,128)(2,1)S(1)}, u32[]{:S(2)}, u32[]{:S(2)}) %collective-permute-start.3) | collective-permute-done | bytes 196640 | tf_op jit(solution)/shard_map/ppermute | solution.py:282
  29.1 1.6 broadcast_in_dim.12
  30.7 3.8 %all-to-all-start = ((bf16[4,1184,256]{2,1,0:T(8,128)(2,1)}), bf16[4,1184,256]{2,1,0:T(8,128)(2,1)S(1)}, u32[]{:S(2)}, u32[]{:S(2)}) async-start(bf16[4,1184,256]{2,1,0:T(8,128)(2,1)} %broadcast_in_dim.12), calls=%async_computation | async-start | bytes 4849664 | tf_op jit(solution)/shard_map/all_to_all | solution.py:290
  34.5 3.2 %collective-permute-start.1 = (bf16[2,128,512]{2,1,0:T(8,128)(2,1)S(1)}, bf16[2,128,512]{2,1,0:T(8,128)(2,1)S(1)}, u32[]{:S(2)}, u32[]{:S(2)}) collective-permute-start(bf16[2,128,512]{2,1,0:T(8,128)(2,1)S(1)} %copy-done.6), channel_id=1, source_target_pairs={{0,8},{4,12},{8,0},{12,4},{1,9},{5,13},{9,1},{13,5},{2,10},{6,14},... | collective-permute-start | bytes 786440 | tf_op jit(solution)/shard_map/ppermute | solution.py:274
  37.7 1.9 collective-permute-start
  39.6 5.2 %collective-permute-start.2 = (bf16[2,128,512]{2,1,0:T(8,128)(2,1)S(1)}, bf16[2,128,512]{2,1,0:T(8,128)(2,1)S(1)}, u32[]{:S(2)}, u32[]{:S(2)}) collective-permute-start(bf16[2,128,512]{2,1,0:T(8,128)(2,1)S(1)} %copy-done.6), channel_id=1, source_target_pairs={{0,12},{4,0},{8,4},{12,8},{1,13},{5,1},{9,5},{13,9},{2,14},{6,2},{... | collective-permute-start | bytes 786440 | tf_op jit(solution)/shard_map/ppermute | solution.py:274
  47.0 2.7 %collective-permute-done.2.refs_3_ = bf16[2,128,512]{2,1,0:T(8,128)(2,1)S(1)} collective-permute-done((bf16[2,128,512]{2,1,0:T(8,128)(2,1)S(1)}, bf16[2,128,512]{2,1,0:T(8,128)(2,1)S(1)}, u32[]{:S(2)}, u32[]{:S(2)}) %collective-permute-start.2) | collective-permute-done | bytes 262176 | tf_op jit(solution)/shard_map/ppermute | solution.py:274
  50.3 1.6 shard_map.113
  51.9 1.4 copy-done
  54.7 1.7 copy-done.1
  57.1 3.5 %shard_map.115 = (bf16[1024,1024]{1,0:T(8,128)(2,1)S(1)}, f32[16,4,128]{2,1,0:T(4,128)S(1)}) custom-call(s32[5]{0:T(128)S(1)} %copy-done.12, bf16[1024,1152]{1,0:T(8,128)(2,1)S(1)} %copy-done.1, bf16[4,1184,256]{2,1,0:T(8,128)(2,1)S(1)} %all-to-all-done.rows_ref), custom_call_target="tpu_custom_call" | custom-call | tf_op jit(solution)/shard_map/pallas_call | solution.py:337
  60.6 21.7 %all_to_all.40.target_ref = f32[16,4,128]{2,1,0:T(4,128)S(1)} all-to-all(f32[16,4,128]{2,1,0:T(4,128)S(1)} %get-tuple-element.26), channel_id=1, replica_groups=mesh['x'=4,'zh'=4,'c'=2,'zl'=4,'y'=4] {'x','zl'}, dimensions={0} | all-to-all | bytes 65536 | tf_op jit(solution)/shard_map/all_to_all | solution.py:290
  83.0 24.8 %all_to_all.41.x_ref = bf16[16,16,256]{2,1,0:T(8,128)(2,1)S(1)} all-to-all(bf16[16,16,256]{2,1,0:T(8,128)(2,1)S(1)} %get-tuple-element.29), channel_id=1, replica_groups=mesh['x'=4,'zh'=4,'c'=2,'zl'=4,'y'=4] {'zh','zl'}, dimensions={0} | all-to-all | bytes 262144 | tf_op jit(solution)/shard_map/all_to_all | solution.py:290
  108.7 18.3 %all_to_all.42.z_ref = bf16[32,16,256]{2,1,0:T(8,128)(2,1)S(1)} all-to-all(bf16[32,16,256]{2,1,0:T(8,128)(2,1)S(1)} %get-tuple-element.30), channel_id=1, replica_groups=mesh['x'=4,'zh'=4,'c'=2,'zl'=4,'y'=4] {'x','c','y'}, dimensions={0} | all-to-all | bytes 524288 | tf_op jit(solution)/shard_map/all_to_all | solution.py:290
  127.7 15.0 %all_to_all.43.x_ref = bf16[16,16,256]{2,1,0:T(8,128)(2,1)S(1)} all-to-all(bf16[16,16,256]{2,1,0:T(8,128)(2,1)S(1)} %get-tuple-element.35), channel_id=1, replica_groups=mesh['x'=4,'zh'=4,'c'=2,'zl'=4,'y'=4] {'zh','zl'}, dimensions={0} | all-to-all | bytes 262144 | tf_op jit(solution)/shard_map/all_to_all | solution.py:290
  143.0 15.4 %all_to_all.44.z_ref = bf16[32,16,256]{2,1,0:T(8,128)(2,1)S(1)} all-to-all(bf16[32,16,256]{2,1,0:T(8,128)(2,1)S(1)} %shard_map.119), channel_id=1, replica_groups=mesh['x'=4,'zh'=4,'c'=2,'zl'=4,'y'=4] {'x','c','y'}, dimensions={0} | all-to-all | bytes 524288 | tf_op jit(solution)/shard_map/all_to_all | solution.py:290
  159.6 7.2 %all_to_all.45.scaled_ref = f32[4,2,128]{2,1,0:T(2,128)S(1)} all-to-all(f32[4,2,128]{2,1,0:T(2,128)S(1)} %get-tuple-element.40), channel_id=1, replica_groups=mesh['x'=4,'zh'=4,'c'=2,'zl'=4,'y'=4] {'zl'}, dimensions={0} | all-to-all | bytes 8192 | tf_op jit(solution)/shard_map/all_to_all | solution.py:290
  166.7 2.8 %shard_map.121 = bf16[4,1152,256]{2,1,0:T(8,128)(2,1)S(1)} custom-call(bf16[1152,1024]{1,0:T(8,128)(2,1)S(1)} %copy-done.3, bf16[1024,1024]{1,0:T(8,128)(2,1)S(1)} %get-tuple-element.25.psi_ref, f32[4,2,128]{2,1,0:T(2,128)S(1)} %all_to_all.45.scaled_ref), custom_call_target="tpu_custom_call" | custom-call | tf_op jit(solution)/shard_map/pallas_call | solution.py:382
  169.6 29.3 %all_to_all.46 = bf16[4,1152,256]{2,1,0:T(8,128)(2,1)S(1)} all-to-all(bf16[4,1152,256]{2,1,0:T(8,128)(2,1)S(1)} %shard_map.121), channel_id=1, replica_groups=mesh['x'=4,'zh'=4,'c'=2,'zl'=4,'y'=4] {'y'}, dimensions={0} | all-to-all | bytes 4718592 | tf_op jit(solution)/shard_map/all_to_all | solution.py:290
  199.4 6.6 %collective-permute-start.5 = (bf16[384,256]{1,0:T(8,128)(2,1)S(1)}, bf16[384,256]{1,0:T(8,128)(2,1)S(1)}, u32[]{:S(2)}, u32[]{:S(2)}) collective-permute-start(bf16[384,256]{1,0:T(8,128)(2,1)S(1)} %get-tuple-element.42), channel_id=1, source_target_pairs={{16,32},{32,16},{48,64},{64,48},{80,96},{96,80},{112,128},{128,112... | collective-permute-start | bytes 589832 | tf_op jit(solution)/shard_map/ppermute | solution.py:282
  205.9 1.9 collective-permute-start.6
  207.9 8.7 %collective-permute-done.5 = bf16[384,256]{1,0:T(8,128)(2,1)S(1)} collective-permute-done((bf16[384,256]{1,0:T(8,128)(2,1)S(1)}, bf16[384,256]{1,0:T(8,128)(2,1)S(1)}, u32[]{:S(2)}, u32[]{:S(2)}) %collective-permute-start.5) | collective-permute-done | bytes 196640 | tf_op jit(solution)/shard_map/ppermute | solution.py:282
  (59 shorter events, 14.6 us)
Async XLA Ops:
  0.6 0.7 copy-start.14
  1.3 0.7 copy-start.18
  4.6 23.6 %collective-permute-start.4 = (bf16[400,256]{1,0:T(8,128)(2,1)S(1)}, bf16[400,256]{1,0:T(8,128)(2,1)S(1)}, u32[]{:S(2)}, u32[]{:S(2)}) collective-permute-start(bf16[400,256]{1,0:T(8,128)(2,1)S(1)} %pad_maximum_fusion.1), channel_id=1, source_target_pairs={{0,16},{16,0},{1,17},{17,1},{2,18},{18,2},{3,19},{19,3},{4,20},{20... | collective-permute-start | bytes 614408 | tf_op jit(solution)/shard_map/ppermute | solution.py:286
  13.4 14.8 %collective-permute-start.3 = (bf16[384,256]{1,0:T(8,128)(2,1)}, bf16[384,256]{1,0:T(8,128)(2,1)S(1)}, u32[]{:S(2)}, u32[]{:S(2)}) collective-permute-start(bf16[384,256]{1,0:T(8,128)(2,1)} %param.12), channel_id=1, source_target_pairs={{16,32},{32,16},{48,64},{64,48},{80,96},{96,80},{112,128},{128,112... | collective-permute-start | bytes 589832 | tf_op jit(solution)/shard_map/ppermute | solution.py:282
  30.7 3.8 %copy-start.6 = (bf16[2,128,512]{2,1,0:T(8,128)(2,1)S(1)}, bf16[2,128,512]{2,1,0:T(8,128)(2,1)}, u32[]{:S(2)}) copy-start(bf16[2,128,512]{2,1,0:T(8,128)(2,1)} %refs_0_.1) | copy-start | bytes 786436
  30.7 24.0 %all-to-all-start = ((bf16[4,1184,256]{2,1,0:T(8,128)(2,1)}), bf16[4,1184,256]{2,1,0:T(8,128)(2,1)S(1)}, u32[]{:S(2)}, u32[]{:S(2)}) async-start(bf16[4,1184,256]{2,1,0:T(8,128)(2,1)} %broadcast_in_dim.12), calls=%async_computation | async-start | bytes 4849664 | tf_op jit(solution)/shard_map/all_to_all | solution.py:290
  34.5 12.5 %collective-permute-start.1 = (bf16[2,128,512]{2,1,0:T(8,128)(2,1)S(1)}, bf16[2,128,512]{2,1,0:T(8,128)(2,1)S(1)}, u32[]{:S(2)}, u32[]{:S(2)}) collective-permute-start(bf16[2,128,512]{2,1,0:T(8,128)(2,1)S(1)} %copy-done.6), channel_id=1, source_target_pairs={{0,8},{4,12},{8,0},{12,4},{1,9},{5,13},{9,1},{13,5},{2,10},{6,14},... | collective-permute-start | bytes 786440 | tf_op jit(solution)/shard_map/ppermute | solution.py:274
  37.7 9.3 %collective-permute-start = (bf16[2,128,512]{2,1,0:T(8,128)(2,1)S(1)}, bf16[2,128,512]{2,1,0:T(8,128)(2,1)S(1)}, u32[]{:S(2)}, u32[]{:S(2)}) collective-permute-start(bf16[2,128,512]{2,1,0:T(8,128)(2,1)S(1)} %copy-done.6), channel_id=1, source_target_pairs={{0,4},{4,8},{8,12},{12,0},{1,5},{5,9},{9,13},{13,1},{2,6},{6,10},{... | collective-permute-start | bytes 786440 | tf_op jit(solution)/shard_map/ppermute | solution.py:274
  39.6 10.0 %collective-permute-start.2 = (bf16[2,128,512]{2,1,0:T(8,128)(2,1)S(1)}, bf16[2,128,512]{2,1,0:T(8,128)(2,1)S(1)}, u32[]{:S(2)}, u32[]{:S(2)}) collective-permute-start(bf16[2,128,512]{2,1,0:T(8,128)(2,1)S(1)} %copy-done.6), channel_id=1, source_target_pairs={{0,12},{4,0},{8,4},{12,8},{1,13},{5,1},{9,5},{13,9},{2,14},{6,2},{... | collective-permute-start | bytes 786440 | tf_op jit(solution)/shard_map/ppermute | solution.py:274
  51.9 1.5 copy-start
  53.3 1.4 copy-start.2
  54.7 1.7 copy-start.1
  57.0 25.4 %copy-start.4 = (bf16[2,256,256]{2,1,0:T(8,128)(2,1)S(1)}, bf16[2,256,256]{2,1,0:T(8,128)(2,1)}, u32[]{:S(2)}) copy-start(bf16[2,256,256]{2,1,0:T(8,128)(2,1)} %weight_ref.3) | copy-start | bytes 786436
  57.0 25.4 %copy-start.8 = (bf16[16,256]{1,0:T(8,128)(2,1)S(1)}, bf16[16,256]{1,0:T(8,128)(2,1)}, u32[]{:S(2)}) copy-start(bf16[16,256]{1,0:T(8,128)(2,1)} %copy-done.7) | copy-start | bytes 24580
  57.0 25.4 %copy-start.10 = (f32[16,256]{1,0:T(8,128)S(1)}, f32[16,256]{1,0:T(8,128)}, u32[]{:S(2)}) copy-start(f32[16,256]{1,0:T(8,128)} %copy-done.9) | copy-start | bytes 49156
  57.0 25.4 %copy-start.15 = (f32[256]{0:T(256)S(1)}, f32[256]{0:T(256)}, u32[]{:S(2)}) copy-start(f32[256]{0:T(256)} %param.13) | copy-start | bytes 3076
  57.0 25.4 %copy-start.16 = (f32[256]{0:T(256)S(1)}, f32[256]{0:T(256)}, u32[]{:S(2)}) copy-start(f32[256]{0:T(256)} %param.15) | copy-start | bytes 3076
  57.1 25.4 %copy-start.17 = (f32[256]{0:T(256)S(1)}, f32[256]{0:T(256)}, u32[]{:S(2)}) copy-start(f32[256]{0:T(256)} %param.16) | copy-start | bytes 3076
  57.1 50.7 %copy-start.13 = (s32[5]{0:T(128)S(1)}, s32[5]{0:T(128)}, u32[]{:S(2)}) copy-start(s32[5]{0:T(128)} %stack.23.place_ref) | copy-start | bytes 64
  60.6 66.4 %copy-start.5 = (bf16[2,256,256]{2,1,0:T(8,128)(2,1)S(1)}, bf16[2,256,256]{2,1,0:T(8,128)(2,1)}, u32[]{:S(2)}) copy-start(bf16[2,256,256]{2,1,0:T(8,128)(2,1)} %atom_weight_ref.3) | copy-start | bytes 786436
  127.0 31.3 %copy-start.19 = (f32[256]{0:T(256)S(1)}, f32[256]{0:T(256)}, u32[]{:S(2)}) copy-start(f32[256]{0:T(256)} %param.19) | copy-start | bytes 3076
  127.7 39.0 %copy-start.3 = (bf16[1152,1024]{1,0:T(8,128)(2,1)S(1)}, bf16[1152,1024]{1,0:T(8,128)(2,1)}, u32[]{:S(2)}) copy-start(bf16[1152,1024]{1,0:T(8,128)(2,1)} %copy-done.2) | copy-start | bytes 7077892
  199.4 17.2 %collective-permute-start.5 = (bf16[384,256]{1,0:T(8,128)(2,1)S(1)}, bf16[384,256]{1,0:T(8,128)(2,1)S(1)}, u32[]{:S(2)}, u32[]{:S(2)}) collective-permute-start(bf16[384,256]{1,0:T(8,128)(2,1)S(1)} %get-tuple-element.42), channel_id=1, source_target_pairs={{16,32},{32,16},{48,64},{64,48},{80,96},{96,80},{112,128},{128,112... | collective-permute-start | bytes 589832 | tf_op jit(solution)/shard_map/ppermute | solution.py:282
  205.9 10.7 %collective-permute-start.6 = (bf16[384,256]{1,0:T(8,128)(2,1)S(1)}, bf16[384,256]{1,0:T(8,128)(2,1)S(1)}, u32[]{:S(2)}, u32[]{:S(2)}) collective-permute-start(bf16[384,256]{1,0:T(8,128)(2,1)S(1)} %get-tuple-element.43), channel_id=1, source_target_pairs={{0,16},{16,0},{1,17},{17,1},{2,18},{18,2},{3,19},{19,3},{4,20},{20... | collective-permute-start | bytes 589832 | tf_op jit(solution)/shard_map/ppermute | solution.py:286
  (4 other events, 2.5 us)

commit v3 on v2

--- a/solution.py
+++ b/solution.py
@@ -76,41 +76,50 @@
     ).astype(BF16)
 
 
-def spread_kernel(place_ref, list_ref, *refs):
-    parts, (dense_ref, flipped_ref) = refs[:SIDE], refs[SIDE:]
-    zl, y, group, core = (place_ref[i] for i in range(4))
+def psi_kernel(place_ref, list_ref, parts_hbm, near_hbm, *refs):
+    outer = refs[:SIDE]
+    psi_ref, dens_ref, flipped_out, dense_ref, flipped_ref, acc_ref, *refs = refs[SIDE:]
+    parts_ref, near_ref, sems = refs
+    side = parts_ref.shape[0]
+    part_copies = [
+        pltpu.make_async_copy(parts_hbm.at[k], parts_ref.at[k], sems.at[k]) for k in range(side)
+    ]
+    near_copy = pltpu.make_async_copy(near_hbm, near_ref, sems.at[side])
+    for copy in part_copies:
+        copy.start()
+    near_copy.start()
+    _, y, group, core, x = (place_ref[i] for i in range(5))
     dense_ref[...] = jnp.zeros_like(dense_ref)
     flipped_ref[...] = jnp.zeros_like(flipped_ref)
-    per, _, wide = parts[0].shape
-    owned = dense_ref.shape[1] // BLK // 3
-    for k, part in enumerate(parts):
-        origin = lax.rem(zl - k + SIDE, SIDE)
+    _, per, _, wide = parts_ref.shape
+    deep, width = outer[0].shape
+    owned = deep // BLK
+    for k in range(side):
+        part_copies[k].wait()
         for r in range(per):
-            batch = (origin * SIDE + y) * per + r
-            row = pl.multiple_of((origin * per + r) * BLK, BLK)
+            batch = (k * side + y) * per + r
+            row = (k * per + r) * BLK
             for j in range(wide // BLK):
                 block = list_ref[batch, j] - (group - 1) * owned
                 below, above = block < owned, block >= 2 * owned
-                outside = jnp.logical_or(below, above)
-                outer = below == (core == 0)
                 within = jnp.where(below, block, jnp.where(above, block - 2 * owned, block - owned))
-                third = jnp.where(outside, jnp.where(outer, 1, 2), 0)
+                far = jnp.where(below == (core == 0), 2, 1)
+                third = jnp.where(jnp.logical_or(below, above), far, 0)
                 col = pl.multiple_of((third * owned + within) * BLK, BLK)
-                tile = part[r, :, j * BLK : (j + 1) * BLK]
-                dense_ref[pl.ds(row, BLK), pl.ds(col, BLK)] = tile
-                flipped_ref[pl.ds(col, BLK), pl.ds(row, BLK)] = tile.T
-
-
-def psi_kernel(place_ref, dense_ref, rows_ref, psi_ref, dens_ref, acc_ref):
-    _, _, _, core, x = (place_ref[i] for i in range(5))
-    side, tall, width = rows_ref.shape
-    deep = dense_ref.shape[1] // 3
+                tile = parts_ref[k, r, :, j * BLK : (j + 1) * BLK]
+                dense_ref[row : row + BLK, pl.ds(col, BLK)] = tile
+                flipped_ref[pl.ds(col, BLK), row : row + BLK] = tile.T
+    copy = pltpu.make_async_copy(flipped_ref, flipped_out, sems.at[side + 1])
+    copy.start()
+    near_copy.wait()
     lane = lax.broadcasted_iota(jnp.int32, (1, BLK), 1)
     device = lane // WINDOW
     atoms = (lane % WINDOW).astype(F32)
     for k in range(side):
+        at = lax.rem(y - k + side, side)
+        own, partner = core * side + at, (1 - core) * side + at
         chosen = jnp.concatenate(
-            [rows_ref[k, :deep], rows_ref[k, deep + ROWS : tall - ROWS]], axis=0
+            [near_ref[own, :deep], near_ref[partner, :deep], outer[k][...]], axis=0
         )
         psi = jnp.dot(dense_ref[...], chosen, preferred_element_type=F32).astype(BF16)
         psi_ref[:, k * width : (k + 1) * width] = psi
@@ -121,10 +130,10 @@
             acc_ref[...] = part
         else:
             acc_ref[...] += part
-        for at, owner in ((deep, core), (tall - ROWS, 1 - core)):
-            window = rows_ref[k, at : at + ROWS, :BLK].astype(F32)
-            window = window[0:1] * 16.0 + window[1:2]
-            atoms += jnp.where(device == owner * side + k, window, 0.0)
+    for n in range(2 * side):
+        window = near_ref[n, deep:, :BLK].astype(F32)
+        window = window[0:1] * 16.0 + window[1:2]
+        atoms += jnp.where(device == n, window, 0.0)
     atoms = jnp.where(atoms >= NATOM, atoms - NATOM, atoms)
     atoms = jnp.where(device < 2 * side, atoms, 0.0)
     dens_ref[...] = jnp.zeros_like(dens_ref)
@@ -134,6 +143,7 @@
         tile = acc_ref[n * BLK : (n + 1) * BLK, :].T
         row = 2.0 * jnp.sum(tile, axis=0, keepdims=True)
         dens_ref[x * side + n // 2, n % 2 : n % 2 + 1, :] = row
+    copy.wait()
 
 
 def silu(x):
@@ -148,7 +158,7 @@
     message = silu(jnp.dot(hidden.astype(BF16), weight, preferred_element_type=F32))
     weighted = (weights_col * message).astype(BF16)
     rows = jnp.dot(selector, weighted, preferred_element_type=F32)
-    return message, (rows + meta).astype(BF16)
+    return message, rows + meta
 
 
 def first_kernel(
@@ -165,7 +175,15 @@
     hidden_ref[...] = hidden
     message, payload = message_of(hidden, weight_ref[0], weights, sel_ref[...], meta_ref[...])
     message_ref[...] = message
-    out_ref[...] = jnp.broadcast_to(payload[None], out_ref.shape)
+    out_ref[...] = jnp.broadcast_to(payload.astype(BF16)[None], out_ref.shape)
+
+
+def folded(rows):
+    return jnp.concatenate([rows[..., :BLK], rows[..., BLK:]], axis=-2)
+
+
+def unfolded(rows):
+    return jnp.concatenate([rows[:WINDOW], rows[WINDOW:]], axis=1)
 
 
 def route_first_kernel(place_ref, x_ref, target_ref, out_ref, match_ref):
@@ -197,10 +215,16 @@
 
 def route_kernel(x_ref, match_ref, out_ref):
     x = x_ref[...].reshape(x_ref.shape[0] * ROWS, x_ref.shape[2])
+    wide = x.astype(F32)
+    rest = jnp.concatenate([wide[WINDOW:], wide[:WINDOW]], axis=0).astype(BF16)
     down = (((0,), (0,)), ((), ()))
-    sums = lax.dot_general(match_ref[...], x, down, preferred_element_type=F32)
-    sums = sums.reshape(out_ref.shape[0], WINDOW, -1)
-    out_ref[...] = jnp.concatenate([sums, jnp.zeros_like(sums)], axis=1).astype(BF16)
+    halves = [
+        lax.dot_general(match_ref[...], half, down, preferred_element_type=F32).reshape(
+            out_ref.shape[0], WINDOW, -1
+        )
+        for half in (x, rest)
+    ]
+    out_ref[...] = jnp.concatenate(halves, axis=1).astype(BF16)
 
 
 def updated(rows, mass, weight, hidden, message, spread):
@@ -228,6 +252,7 @@
     weights = column(cols_ref[...], 2)
     message, payload = message_of(hidden, weight_ref[1], weights, sel_ref[...], 0.0)
     message_out[...] = message
+    payload = folded(payload[:WINDOW]).astype(BF16)
     out_ref[...] = jnp.broadcast_to(payload[None], out_ref.shape)
 
 
@@ -237,7 +262,7 @@
 ):
     total = jnp.sum(z_ref[...].astype(F32), axis=0)
     hidden = updated(
-        total[:WINDOW], mass_ref[:, 0:1], atom_weight_ref[1], hidden_ref[...], message_ref[...],
+        unfolded(total), mass_ref[:, 0:1], atom_weight_ref[1], hidden_ref[...], message_ref[...],
         spread_ref[...],
     )
     score = jnp.sum(hidden * head_ref[...], axis=1, keepdims=True)
@@ -255,18 +280,53 @@
         scaled_ref[k] = flat[2:4]
 
 
-def fock_kernel(flipped_ref, psi_ref, scaled_ref, out_ref, weighted, scratch):
-    side, _, width = out_ref.shape
+def scaled_psi(psi_ref, scaled_ref, weighted, scratch):
+    side = scaled_ref.shape[0]
     for k in range(side):
         scratch[2 * k : 2 * k + 2, :] = scaled_ref[k]
     tall = scratch[...].T
     for n in range(2 * side):
         rows = slice(n * BLK, (n + 1) * BLK)
         weighted[rows, :] = (tall[:, n : n + 1] * psi_ref[rows, :].astype(F32)).astype(BF16)
+
+
+def outer_kernel(
+    place_ref, flipped_hbm, psi_ref, scaled_ref, out_ref, weighted, flipped_ref, scratch, sem
+):
+    side, deep, width = out_ref.shape
+    copy = pltpu.make_async_copy(flipped_hbm.at[2 * deep :], flipped_ref, sem)
+    copy.start()
+    y = place_ref[1]
+    scaled_psi(psi_ref, scaled_ref, weighted, scratch)
+    copy.wait()
     for k in range(side):
-        out_ref[k] = jnp.dot(
-            flipped_ref[...], weighted[:, k * width : (k + 1) * width], preferred_element_type=F32
+        terms = jnp.dot(
+            flipped_ref[...],
+            weighted[:, k * width : (k + 1) * width],
+            preferred_element_type=F32,
+        )
+        out_ref[lax.rem(y - k + side, side)] = terms.astype(BF16)
+
+
+def near_kernel(
+    place_ref, flipped_hbm, psi_ref, scaled_ref, out_ref, weighted, flipped_ref, scratch, sem
+):
+    count, deep, width = out_ref.shape
+    side = count // 2
+    copy = pltpu.make_async_copy(flipped_hbm.at[: 2 * deep], flipped_ref, sem)
+    copy.start()
+    y, core = place_ref[1], place_ref[3]
+    scaled_psi(psi_ref, scaled_ref, weighted, scratch)
+    copy.wait()
+    for k in range(side):
+        terms = jnp.dot(
+            flipped_ref[...],
+            weighted[:, k * width : (k + 1) * width],
+            preferred_element_type=F32,
         ).astype(BF16)
+        at = lax.rem(y - k + side, side)
+        out_ref[core * side + at] = terms[:deep]
+        out_ref[(1 - core) * side + at] = terms[deep:]
 
 
 def from_behind(value, axis):
@@ -280,10 +340,6 @@
     groups = lax.axis_size(GRID)
     pairs = [(g, g + 1 if g % 2 else g - 1) for g in range(1, groups - 1)]
     return lax.ppermute(value, GRID, pairs)
-
-
-def swap(value):
-    return lax.ppermute(value, "c", [(0, 1), (1, 0)])
 
 
 def exchange(parts, axes):
@@ -310,8 +366,8 @@
     plane, column_size = lax.axis_size(PLANE), lax.axis_size(COLUMN)
     square_f32 = shape((points, feat), F32)
 
+    parts = lax.all_gather(basis_values, "zl")
     outer = across(orbitals)
-    parts = from_behind(basis_values, "zl")
     selector, spread, meta, window = call(
         prepare_kernel,
         (
@@ -324,26 +380,33 @@
         scratch=[pltpu.VMEM((8, batch_points), F32)],
     )(point_atoms.reshape(batches, batch_points), point_weights.reshape(batches, batch_points))
     own = jnp.concatenate([orbitals, window], axis=0)
-    rows = jnp.concatenate([own, outer, swap(own)], axis=0)
-    gathered = exchange(jnp.broadcast_to(rows, (SIDE, *rows.shape)), ("y",))
+    chip = ("c", "y")
+    near = exchange(jnp.broadcast_to(own, (2 * SIDE, *own.shape)), chip)
+    outer = from_behind(outer, "y")
 
     total_points = SIDE * points
-    dense, flipped = call(
-        spread_kernel,
-        (shape((total_points, 3 * deep), BF16), shape((3 * deep, total_points), BF16)),
-        2 + SIDE,
-        smem=(0, 1),
-    )(place, block_lists, *parts)
-    psi, squares = call(
+    everywhere = pl.BlockSpec(memory_space=pltpu.VMEM)
+    scalars = pl.BlockSpec(memory_space=pltpu.SMEM)
+    anywhere = pl.BlockSpec(memory_space=pl.ANY)
+    psi, squares, flipped = pl.pallas_call(
         psi_kernel,
-        (
+        out_shape=(
             shape((total_points, SIDE * width), BF16),
             shape((SIDE * SIDE, 4, batch_points), F32),
+            shape((3 * deep, total_points), BF16),
         ),
-        3,
-        smem=(0,),
-        scratch=[pltpu.VMEM((total_points, BLK), F32)],
-    )(place, dense, gathered)
+        in_specs=[scalars] * 2 + [anywhere] * 2 + [everywhere] * SIDE,
+        out_specs=(everywhere, everywhere, anywhere),
+        scratch_shapes=[
+            pltpu.VMEM((total_points, 3 * deep), BF16),
+            pltpu.VMEM((3 * deep, total_points), BF16),
+            pltpu.VMEM((total_points, BLK), F32),
+            pltpu.VMEM(parts.shape, BF16),
+            pltpu.VMEM(near.shape, BF16),
+            pltpu.SemaphoreType.DMA((SIDE + 2,)),
+        ],
+        compiler_params=pltpu.CompilerParams(vmem_limit_bytes=VMEM),
+    )(place, block_lists, parts, near, *outer)
     squares = exchange(squares, ("x", "zl"))
     radius = jnp.cbrt(jnp.sum(squares[:, :2], axis=0))
 
@@ -364,11 +427,18 @@
         smem=(0,),
     )(place, exchange(sent, COLUMN), squares)
     hidden, message, mass_rows, sent = call(
-        second_kernel, (square_f32, square_f32, shape((WINDOW, BLK), F32), to_column), 8
+        second_kernel,
+        (
+            square_f32,
+            square_f32,
+            shape((WINDOW, BLK), F32),
+            shape((column_size, ROWS, BLK), BF16),
+        ),
+        8,
     )(
         exchange(sums, PLANE), atom_weight, message_weight, hidden, message, cols, spread, selector
     )
-    sums = call(route_kernel, to_plane, 2)(exchange(sent, COLUMN), match)
+    sums = call(route_kernel, shape((plane, ROWS, BLK), BF16), 2)(exchange(sent, COLUMN), match)
     potential, scaled = call(
         last_kernel,
         (shape((batches, batch_points), F32), shape((SIDE, batches, batch_points), F32)),
@@ -379,19 +449,25 @@
     )
     scaled = exchange(scaled, ("zl",))
 
-    terms = call(
-        fock_kernel,
-        shape((SIDE, 3 * deep, width), BF16),
-        3,
-        scratch=[
-            pltpu.VMEM((total_points, SIDE * width), BF16),
-            pltpu.VMEM((8, batch_points), F32),
-        ],
-    )(flipped, psi, scaled)
-    total = jnp.sum(exchange(terms, ("y",)).astype(F32), axis=0)
-    own, outer, partner = total[:deep], total[deep : 2 * deep], total[2 * deep :]
-    arrived = across(outer.astype(BF16))
-    fock = own + arrived.astype(F32) + swap(partner.astype(BF16)).astype(F32)
+    def fock_terms(kernel, devices, rows):
+        return pl.pallas_call(
+            kernel,
+            out_shape=shape((devices, deep, width), BF16),
+            in_specs=[scalars, anywhere, everywhere, everywhere],
+            out_specs=everywhere,
+            scratch_shapes=[
+                pltpu.VMEM((total_points, SIDE * width), BF16),
+                pltpu.VMEM((rows, total_points), BF16),
+                pltpu.VMEM((8, batch_points), F32),
+                pltpu.SemaphoreType.DMA,
+            ],
+            compiler_params=pltpu.CompilerParams(vmem_limit_bytes=VMEM),
+        )(place, flipped, psi, scaled)
+
+    outer = fock_terms(outer_kernel, SIDE, deep)
+    near = fock_terms(near_kernel, 2 * SIDE, 2 * deep)
+    arrived = across(jnp.sum(exchange(outer, ("y",)).astype(F32), axis=0).astype(BF16))
+    fock = jnp.sum(exchange(near, chip).astype(F32), axis=0) + arrived.astype(F32)
     return fock, potential.reshape(-1)
 
 

time: 219 us -> 208 us (0.950)
  blocking collectives: 132 us -> 89.4 us
  waiting for transfers between devices: 23.6 us -> 39.5 us
  between operations: 0.92 us -> 14.3 us
  Pallas kernels: 11.9 us -> 15.2 us
  starting transfers between devices: 34.7 us -> 37.3 us
    all_to_all x7 -> x6, blocking collectives: 132 us -> 89.4 us  [exchange(): return lax.all_to_all(parts, axes, split_axis=0, concat_axis=0, tiled=True)]
    all_to_all x1 -> x3, waiting for transfers between devices: 0.01 us -> 22.2 us  [exchange(): return lax.all_to_all(parts, axes, split_axis=0, concat_axis=0, tiled=True)]
    all_to_all x1 -> x3, starting transfers between devices: 3.77 us -> 20.4 us  [exchange(): return lax.all_to_all(parts, axes, split_axis=0, concat_axis=0, tiled=True)]
    ppermute x2 -> x0, starting transfers between devices: 10.7 us -> none  [swap(): return lax.ppermute(value, 'c', [(0, 1), (1, 0)])]
    ppermute x2, waiting for transfers between devices: 20.2 us -> 11.2 us  [across(): return lax.ppermute(value, GRID, pairs)]
    pallas_call x5, Pallas kernels: 8.8 us -> 12.2 us  [the longest x2 5.93 us: fock_terms(): pl.pallas_call(kernel, out_shape=shape((devices, deep, width), BF16), in_...]
    ppermute x2, starting transfers between devices: 9.89 us -> 7.11 us  [across(): return lax.ppermute(value, GRID, pairs)]
    unnamed x41 -> x33, local copies, waits for them, and re-layouts: 9.17 us -> 8.1 us
  transfers between devices with their start and end apart: 8 -> 9, of which waited for: 4 -> 6; matrix products, arithmetic and copies ran while one was open for 1% -> 1% of each run, Pallas kernels for 1% -> 2%
where the time goes in v3:
time: 208 us; the launch traced here: 207 us
  blocking collectives  89.4 us (43%)
  waiting for transfers between devices  39.5 us (19%)
  starting transfers between devices  37.3 us (18%)
  Pallas kernels  15.2 us (7%)
  between operations  14.3 us (7%)
  local copies, waits for them, and re-layouts  9.53 us (5%)
  other arithmetic  2.15 us (1%)
    all_to_all x6, blocking collectives, exchange(): return lax.all_to_all(parts, axes, split_axis=0, concat_axis=0, tiled=True)  89.4 us
    all_to_all x3, waiting for transfers between devices, exchange(): return lax.all_to_all(parts, axes, split_axis=0, concat_axis=0, tiled=True)  22.2 us
    all_to_all x3, starting transfers between devices, exchange(): return lax.all_to_all(parts, axes, split_axis=0, concat_axis=0, tiled=True)  20.4 us
    ppermute x2, waiting for transfers between devices, across(): return lax.ppermute(value, GRID, pairs)  11.2 us
    ppermute x3, starting transfers between devices, from_behind(): lax.ppermute(value, axis, [(i, (i + k) % SIDE) for i in range(SIDE)])  9.81 us
    unnamed x33, local copies, waits for them, and re-layouts  8.1 us
    ppermute x2, starting transfers between devices, across(): return lax.ppermute(value, GRID, pairs)  7.11 us
    pallas_call x2, Pallas kernels, fock_terms(): pl.pallas_call(kernel, out_shape=shape((devices, deep, width), BF16), in_...  5.93 us
  transfers between devices with their start and end apart: 9, of which 6 were waited for; matrix products, arithmetic and copies ran while one was open for 1% of the time, Pallas kernels for 2%

profile of v3, /device:TPU:1, one launch (start us, length us, event | category | flops | bytes accessed | tf_op | source)
XLA Modules:
  0.0 207.5 jit_solution(2902922043772522164)
XLA Ops:
  12.0 10.5 %all-to-all-start = ((bf16[8,400,256]{2,1,0:T(8,128)(2,1)}), bf16[8,400,256]{2,1,0:T(8,128)(2,1)S(1)}, u32[]{:S(2)}, u32[]{:S(2)}) async-start(bf16[8,400,256]{2,1,0:T(8,128)(2,1)} %broadcast_in_dim.12), calls=%async_computation | async-start | bytes 3276800 | tf_op jit(solution)/shard_map/all_to_all | solution.py:346
  22.5 4.3 %collective-permute-start = (bf16[384,256]{1,0:T(8,128)(2,1)S(1)}, bf16[384,256]{1,0:T(8,128)(2,1)S(1)}, u32[]{:S(2)}, u32[]{:S(2)}) collective-permute-start(bf16[384,256]{1,0:T(8,128)(2,1)S(1)} %copy-done.14), channel_id=1, source_target_pairs={{16,32},{32,16},{48,64},{64,48},{80,96},{96,80},{112,128},{128,112... | collective-permute-start | bytes 589832 | tf_op jit(solution)/shard_map/ppermute | solution.py:342
  26.8 11.2 %collective-permute-done.refs_0_ = bf16[384,256]{1,0:T(8,128)(2,1)S(1)} collective-permute-done((bf16[384,256]{1,0:T(8,128)(2,1)S(1)}, bf16[384,256]{1,0:T(8,128)(2,1)S(1)}, u32[]{:S(2)}, u32[]{:S(2)}) %collective-permute-start) | collective-permute-done | bytes 196640 | tf_op jit(solution)/shard_map/ppermute | solution.py:342
  38.0 4.8 %collective-permute-start.3 = (bf16[384,256]{1,0:T(8,128)(2,1)S(1)}, bf16[384,256]{1,0:T(8,128)(2,1)S(1)}, u32[]{:S(2)}, u32[]{:S(2)}) collective-permute-start(bf16[384,256]{1,0:T(8,128)(2,1)S(1)} %collective-permute-done.refs_0_), channel_id=1, source_target_pairs={{0,3},{1,0},{2,1},{3,2},{4,7},{5,4},{6,5},{7,6},{8,11},{9,8},{10,9... | collective-permute-start | bytes 589832 | tf_op jit(solution)/shard_map/ppermute | solution.py:334
  42.8 2.5 %collective-permute-start.2 = (bf16[384,256]{1,0:T(8,128)(2,1)S(1)}, bf16[384,256]{1,0:T(8,128)(2,1)S(1)}, u32[]{:S(2)}, u32[]{:S(2)}) collective-permute-start(bf16[384,256]{1,0:T(8,128)(2,1)S(1)} %collective-permute-done.refs_0_), channel_id=1, source_target_pairs={{0,2},{1,3},{2,0},{3,1},{4,6},{5,7},{6,4},{7,5},{8,10},{9,11},{10,... | collective-permute-start | bytes 589832 | tf_op jit(solution)/shard_map/ppermute | solution.py:334
  45.3 2.5 %collective-permute-start.1 = (bf16[384,256]{1,0:T(8,128)(2,1)S(1)}, bf16[384,256]{1,0:T(8,128)(2,1)S(1)}, u32[]{:S(2)}, u32[]{:S(2)}) collective-permute-start(bf16[384,256]{1,0:T(8,128)(2,1)S(1)} %collective-permute-done.refs_0_), channel_id=1, source_target_pairs={{0,1},{1,2},{2,3},{3,0},{4,5},{5,6},{6,7},{7,4},{8,9},{9,10},{10,1... | collective-permute-start | bytes 589832 | tf_op jit(solution)/shard_map/ppermute | solution.py:334
  48.0 2.9 %collective-permute-done.2.refs_2_ = bf16[384,256]{1,0:T(8,128)(2,1)S(1)} collective-permute-done((bf16[384,256]{1,0:T(8,128)(2,1)S(1)}, bf16[384,256]{1,0:T(8,128)(2,1)S(1)}, u32[]{:S(2)}, u32[]{:S(2)}) %collective-permute-start.2) | collective-permute-done | bytes 196640 | tf_op jit(solution)/shard_map/ppermute | solution.py:334
  50.9 2.5 %collective-permute-done.1.refs_1_ = bf16[384,256]{1,0:T(8,128)(2,1)S(1)} collective-permute-done((bf16[384,256]{1,0:T(8,128)(2,1)S(1)}, bf16[384,256]{1,0:T(8,128)(2,1)S(1)}, u32[]{:S(2)}, u32[]{:S(2)}) %collective-permute-start.1) | collective-permute-done | bytes 196640 | tf_op jit(solution)/shard_map/ppermute | solution.py:334
  54.7 1.4 copy-done.3
  57.4 5.3 %shard_map.114 = (bf16[1024,1024]{1,0:T(8,128)(2,1)S(1)}, f32[16,4,128]{2,1,0:T(4,128)S(1)}, bf16[1152,1024]{1,0:T(8,128)(2,1)S(1)}) custom-call(s32[5]{0:T(128)S(1)} %stack.23.place_ref, s32[32,4]{1,0:T(8,128)S(1)} %copy.13.list_ref, bf16[4,2,128,512]{3,2,1,0:T(8,128)(2,1)S(1)} %bitcast.12, bf16[8,400,256]{2,1,0:T(8,128)(2,1)S(1)} %copy-done.3, ...), custom_call_target="tpu_custom_call" | custom-call | tf_op jit(solution)/shard_map/pallas_call | solution.py:391
  62.7 14.8 %all_to_all.45.target_ref = f32[16,4,128]{2,1,0:T(4,128)S(1)} all-to-all(f32[16,4,128]{2,1,0:T(4,128)S(1)} %get-tuple-element.24), channel_id=1, replica_groups=mesh['x'=4,'zh'=4,'c'=2,'zl'=4,'y'=4] {'x','zl'}, dimensions={0} | all-to-all | bytes 65536 | tf_op jit(solution)/shard_map/all_to_all | solution.py:346
  78.2 24.1 %all_to_all.46.x_ref = bf16[16,16,256]{2,1,0:T(8,128)(2,1)S(1)} all-to-all(bf16[16,16,256]{2,1,0:T(8,128)(2,1)S(1)} %get-tuple-element.27), channel_id=1, replica_groups=mesh['x'=4,'zh'=4,'c'=2,'zl'=4,'y'=4] {'zh','zl'}, dimensions={0} | all-to-all | bytes 262144 | tf_op jit(solution)/shard_map/all_to_all | solution.py:346
  103.2 15.7 %all_to_all.47.z_ref = bf16[32,16,256]{2,1,0:T(8,128)(2,1)S(1)} all-to-all(bf16[32,16,256]{2,1,0:T(8,128)(2,1)S(1)} %get-tuple-element.28), channel_id=1, replica_groups=mesh['x'=4,'zh'=4,'c'=2,'zl'=4,'y'=4] {'x','c','y'}, dimensions={0} | all-to-all | bytes 524288 | tf_op jit(solution)/shard_map/all_to_all | solution.py:346
  119.6 15.0 %all_to_all.48.x_ref = bf16[16,16,128]{2,1,0:T(8,128)(2,1)S(1)} all-to-all(bf16[16,16,128]{2,1,0:T(8,128)(2,1)S(1)} %get-tuple-element.33), channel_id=1, replica_groups=mesh['x'=4,'zh'=4,'c'=2,'zl'=4,'y'=4] {'zh','zl'}, dimensions={0} | all-to-all | bytes 131072 | tf_op jit(solution)/shard_map/all_to_all | solution.py:346
  134.8 13.1 %all_to_all.49.z_ref = bf16[32,16,128]{2,1,0:T(8,128)(2,1)S(1)} all-to-all(bf16[32,16,128]{2,1,0:T(8,128)(2,1)S(1)} %shard_map.118), channel_id=1, replica_groups=mesh['x'=4,'zh'=4,'c'=2,'zl'=4,'y'=4] {'x','c','y'}, dimensions={0} | all-to-all | bytes 262144 | tf_op jit(solution)/shard_map/all_to_all | solution.py:346
  149.1 6.8 %all_to_all.50.scaled_ref = f32[4,2,128]{2,1,0:T(2,128)S(1)} all-to-all(f32[4,2,128]{2,1,0:T(2,128)S(1)} %get-tuple-element.38), channel_id=1, replica_groups=mesh['x'=4,'zh'=4,'c'=2,'zl'=4,'y'=4] {'zl'}, dimensions={0} | all-to-all | bytes 8192 | tf_op jit(solution)/shard_map/all_to_all | solution.py:346
  155.8 2.9 %shard_map.121 = bf16[4,384,256]{2,1,0:T(8,128)(2,1)} custom-call(s32[5]{0:T(128)S(1)} %stack.23.place_ref, bf16[1152,1024]{1,0:T(8,128)(2,1)S(1)} %get-tuple-element.22.flipped_hbm, bf16[1024,1024]{1,0:T(8,128)(2,1)S(1)} %get-tuple-element.23.psi_ref, f32[4,2,128]{2,1,0:T(2,128)S(1)} %all_to_all.50.scaled_ref), custom_call_target="tpu_custom_call" | custom-call | tf_op jit(solution)/shard_map/pallas_call | solution.py:453
  158.8 3.5 %all-to-all-start.8 = ((bf16[4,384,256]{2,1,0:T(8,128)(2,1)}), bf16[4,384,256]{2,1,0:T(8,128)(2,1)S(1)}, u32[]{:S(2)}, u32[]{:S(2)}) async-start(bf16[4,384,256]{2,1,0:T(8,128)(2,1)} %shard_map.121), calls=%async_computation.8 | async-start | bytes 1572864 | tf_op jit(solution)/shard_map/all_to_all | solution.py:346
  162.3 1.6 copy-done.1
  163.9 3.0 %shard_map.120 = bf16[8,384,256]{2,1,0:T(8,128)(2,1)S(1)} custom-call(s32[5]{0:T(128)S(1)} %stack.23.place_ref, bf16[1152,1024]{1,0:T(8,128)(2,1)S(1)} %get-tuple-element.22.flipped_hbm, bf16[1024,1024]{1,0:T(8,128)(2,1)S(1)} %copy-done.1, f32[4,2,128]{2,1,0:T(2,128)S(1)} %all_to_all.50.scaled_ref), custom_call_target="tpu_custom_call" | custom-call | tf_op jit(solution)/shard_map/pallas_call | solution.py:453
  168.1 4.6 %all-to-all-done.8 = bf16[4,384,256]{2,1,0:T(8,128)(2,1)S(1)} async-done(((bf16[4,384,256]{2,1,0:T(8,128)(2,1)}), bf16[4,384,256]{2,1,0:T(8,128)(2,1)S(1)}, u32[]{:S(2)}, u32[]{:S(2)}) %all-to-all-start.8) | async-done | bytes 786464 | tf_op jit(solution)/shard_map/all_to_all | solution.py:346
  172.7 6.4 %all-to-all-start.7 = ((bf16[8,384,256]{2,1,0:T(8,128)(2,1)}), bf16[8,384,256]{2,1,0:T(8,128)(2,1)S(1)}, u32[]{:S(2)}, u32[]{:S(2)}) async-start(bf16[8,384,256]{2,1,0:T(8,128)(2,1)} %copy-done.4), calls=%async_computation.7 | async-start | bytes 3145728 | tf_op jit(solution)/shard_map/all_to_all | solution.py:346
  179.2 2.8 %collective-permute-start.4 = (bf16[384,256]{1,0:T(8,128)(2,1)S(1)}, bf16[384,256]{1,0:T(8,128)(2,1)S(1)}, u32[]{:S(2)}, u32[]{:S(2)}) collective-permute-start(bf16[384,256]{1,0:T(8,128)(2,1)S(1)} %reduce_sum.32), channel_id=1, source_target_pairs={{16,32},{32,16},{48,64},{64,48},{80,96},{96,80},{112,128},{128,112... | collective-permute-start | bytes 589832 | tf_op jit(solution)/shard_map/ppermute | solution.py:342
  182.0 17.6 %all-to-all-done.7 = bf16[8,384,256]{2,1,0:T(8,128)(2,1)S(1)} async-done(((bf16[8,384,256]{2,1,0:T(8,128)(2,1)}), bf16[8,384,256]{2,1,0:T(8,128)(2,1)S(1)}, u32[]{:S(2)}, u32[]{:S(2)}) %all-to-all-start.7) | async-done | bytes 1572896 | tf_op jit(solution)/shard_map/all_to_all | solution.py:346
  (51 shorter events, 13.5 us)
Async XLA Ops:
  7.2 47.5 %all-gather.3.cloned.1.call-start = ((), (), s32[]{:S(2)}) async-start(), calls=%async_computation.9 | async-start | bytes 1310720 | tf_op jit(solution)/shard_map/all_gather | solution.py:369
  7.9 0.7 copy-start.8
  12.0 10.5 %copy-start.14 = (bf16[384,256]{1,0:T(8,128)(2,1)S(1)}, bf16[384,256]{1,0:T(8,128)(2,1)}, u32[]{:S(2)}) copy-start(bf16[384,256]{1,0:T(8,128)(2,1)} %param.12) | copy-start | bytes 589828
  12.0 35.9 %copy-start.15 = (s32[32,4]{0,1:T(4,128)S(1)}, s32[32,4]{0,1:T(4,128)}, u32[]{:S(2)}) copy-start(s32[32,4]{0,1:T(4,128)} %param.11) | copy-start | bytes 1540
  12.0 41.4 %all-to-all-start = ((bf16[8,400,256]{2,1,0:T(8,128)(2,1)}), bf16[8,400,256]{2,1,0:T(8,128)(2,1)S(1)}, u32[]{:S(2)}, u32[]{:S(2)}) async-start(bf16[8,400,256]{2,1,0:T(8,128)(2,1)} %broadcast_in_dim.12), calls=%async_computation | async-start | bytes 3276800 | tf_op jit(solution)/shard_map/all_to_all | solution.py:346
  22.5 15.5 %collective-permute-start = (bf16[384,256]{1,0:T(8,128)(2,1)S(1)}, bf16[384,256]{1,0:T(8,128)(2,1)S(1)}, u32[]{:S(2)}, u32[]{:S(2)}) collective-permute-start(bf16[384,256]{1,0:T(8,128)(2,1)S(1)} %copy-done.14), channel_id=1, source_target_pairs={{16,32},{32,16},{48,64},{64,48},{80,96},{96,80},{112,128},{128,112... | collective-permute-start | bytes 589832 | tf_op jit(solution)/shard_map/ppermute | solution.py:342
  38.0 10.0 %collective-permute-start.3 = (bf16[384,256]{1,0:T(8,128)(2,1)S(1)}, bf16[384,256]{1,0:T(8,128)(2,1)S(1)}, u32[]{:S(2)}, u32[]{:S(2)}) collective-permute-start(bf16[384,256]{1,0:T(8,128)(2,1)S(1)} %collective-permute-done.refs_0_), channel_id=1, source_target_pairs={{0,3},{1,0},{2,1},{3,2},{4,7},{5,4},{6,5},{7,6},{8,11},{9,8},{10,9... | collective-permute-start | bytes 589832 | tf_op jit(solution)/shard_map/ppermute | solution.py:334
  42.8 8.0 %collective-permute-start.2 = (bf16[384,256]{1,0:T(8,128)(2,1)S(1)}, bf16[384,256]{1,0:T(8,128)(2,1)S(1)}, u32[]{:S(2)}, u32[]{:S(2)}) collective-permute-start(bf16[384,256]{1,0:T(8,128)(2,1)S(1)} %collective-permute-done.refs_0_), channel_id=1, source_target_pairs={{0,2},{1,3},{2,0},{3,1},{4,6},{5,7},{6,4},{7,5},{8,10},{9,11},{10,... | collective-permute-start | bytes 589832 | tf_op jit(solution)/shard_map/ppermute | solution.py:334
  45.3 8.0 %collective-permute-start.1 = (bf16[384,256]{1,0:T(8,128)(2,1)S(1)}, bf16[384,256]{1,0:T(8,128)(2,1)S(1)}, u32[]{:S(2)}, u32[]{:S(2)}) collective-permute-start(bf16[384,256]{1,0:T(8,128)(2,1)S(1)} %collective-permute-done.refs_0_), channel_id=1, source_target_pairs={{0,1},{1,2},{2,3},{3,0},{4,5},{5,6},{6,7},{7,4},{8,9},{9,10},{10,1... | collective-permute-start | bytes 589832 | tf_op jit(solution)/shard_map/ppermute | solution.py:334
  53.4 1.2 copy-start.2
  54.7 1.4 copy-start.3
  56.1 1.2 copy-start.5
  57.3 20.2 %copy-start.7 = (bf16[2,256,256]{2,1,0:T(8,128)(2,1)S(1)}, bf16[2,256,256]{2,1,0:T(8,128)(2,1)}, u32[]{:S(2)}) copy-start(bf16[2,256,256]{2,1,0:T(8,128)(2,1)} %weight_ref.3) | copy-start | bytes 786436
  57.3 20.2 %copy-start.9 = (f32[256]{0:T(256)S(1)}, f32[256]{0:T(256)}, u32[]{:S(2)}) copy-start(f32[256]{0:T(256)} %param.13) | copy-start | bytes 3076
  57.3 20.2 %copy-start.10 = (f32[256]{0:T(256)S(1)}, f32[256]{0:T(256)}, u32[]{:S(2)}) copy-start(f32[256]{0:T(256)} %param.15) | copy-start | bytes 3076
  57.3 20.3 %copy-start.11 = (f32[256]{0:T(256)S(1)}, f32[256]{0:T(256)}, u32[]{:S(2)}) copy-start(f32[256]{0:T(256)} %param.16) | copy-start | bytes 3076
  57.3 61.6 %copy-start.6 = (bf16[2,256,256]{2,1,0:T(8,128)(2,1)S(1)}, bf16[2,256,256]{2,1,0:T(8,128)(2,1)}, u32[]{:S(2)}) copy-start(bf16[2,256,256]{2,1,0:T(8,128)(2,1)} %atom_weight_ref.3) | copy-start | bytes 786436
  62.7 93.2 %copy-start = (bf16[1024,1024]{1,0:T(8,128)(2,1)}, bf16[1024,1024]{1,0:T(8,128)(2,1)S(1)}, u32[]{:S(2)}) copy-start(bf16[1024,1024]{1,0:T(8,128)(2,1)S(1)} %get-tuple-element.23.psi_ref) | copy-start | bytes 6291460
  78.1 69.7 %copy-start.12 = (f32[256]{0:T(256)S(1)}, f32[256]{0:T(256)}, u32[]{:S(2)}) copy-start(f32[256]{0:T(256)} %param.19) | copy-start | bytes 3076
  158.8 13.9 %all-to-all-start.8 = ((bf16[4,384,256]{2,1,0:T(8,128)(2,1)}), bf16[4,384,256]{2,1,0:T(8,128)(2,1)S(1)}, u32[]{:S(2)}, u32[]{:S(2)}) async-start(bf16[4,384,256]{2,1,0:T(8,128)(2,1)} %shard_map.121), calls=%async_computation.8 | async-start | bytes 1572864 | tf_op jit(solution)/shard_map/all_to_all | solution.py:346
  162.3 1.6 copy-start.1
  166.9 1.2 copy-start.4
  172.7 27.0 %all-to-all-start.7 = ((bf16[8,384,256]{2,1,0:T(8,128)(2,1)}), bf16[8,384,256]{2,1,0:T(8,128)(2,1)S(1)}, u32[]{:S(2)}, u32[]{:S(2)}) async-start(bf16[8,384,256]{2,1,0:T(8,128)(2,1)} %copy-done.4), calls=%async_computation.7 | async-start | bytes 3145728 | tf_op jit(solution)/shard_map/all_to_all | solution.py:346
  179.2 20.7 %collective-permute-start.4 = (bf16[384,256]{1,0:T(8,128)(2,1)S(1)}, bf16[384,256]{1,0:T(8,128)(2,1)S(1)}, u32[]{:S(2)}, u32[]{:S(2)}) collective-permute-start(bf16[384,256]{1,0:T(8,128)(2,1)S(1)} %reduce_sum.32), channel_id=1, source_target_pairs={{16,32},{32,16},{48,64},{64,48},{80,96},{96,80},{112,128},{128,112... | collective-permute-start | bytes 589832 | tf_op jit(solution)/shard_map/ppermute | solution.py:342
  (1 other events, 0.7 us)
Sparse Core Ops, SparseCore 0:
  10.1 44.5 all-gather.2

commit v4 on v3

--- a/solution.py
+++ b/solution.py
@@ -15,6 +15,7 @@
 WINDOW = 8
 NATOM = 512
 ROWS = 16
+SPARE = 16
 F32 = jnp.float32
 BF16 = jnp.bfloat16
 
@@ -70,35 +71,48 @@
     lane = lax.broadcasted_iota(jnp.int32, (WINDOW, points), 1)
     facts = jnp.where(lane == 0, mass, jnp.where(lane == 1, high, jnp.where(lane == 2, low, 0.0)))
     meta_ref[...] = jnp.concatenate([jnp.zeros_like(facts), facts], axis=0)
-    row = lax.broadcasted_iota(jnp.int32, window_ref.shape, 0)
-    window_ref[...] = jnp.where(
-        row == 0, high[0:1], jnp.where(row == 1, low[0:1], 0.0)
-    ).astype(BF16)
-
-
-def psi_kernel(place_ref, list_ref, parts_hbm, near_hbm, *refs):
-    outer = refs[:SIDE]
-    psi_ref, dens_ref, flipped_out, dense_ref, flipped_ref, acc_ref, *refs = refs[SIDE:]
-    parts_ref, near_ref, sems = refs
-    side = parts_ref.shape[0]
-    part_copies = [
-        pltpu.make_async_copy(parts_hbm.at[k], parts_ref.at[k], sems.at[k]) for k in range(side)
-    ]
-    near_copy = pltpu.make_async_copy(near_hbm, near_ref, sems.at[side])
-    for copy in part_copies:
-        copy.start()
-    near_copy.start()
-    _, y, group, core, x = (place_ref[i] for i in range(5))
+    row = lax.broadcasted_iota(jnp.int32, (ROWS, BLK), 0)
+    window = jnp.where(row == 0, high[0:1], jnp.where(row == 1, low[0:1], 0.0)).astype(BF16)
+    window_ref[...] = jnp.broadcast_to(window[None], window_ref.shape)
+
+
+def rows_kernel(own_ref, outer_ref, windows_ref, out_ref):
+    deep, width = own_ref.shape
+    lane = lax.broadcasted_iota(jnp.int32, (ROWS, width), 1)
+    windows = jnp.zeros((ROWS, width), F32)
+    for n in range(windows_ref.shape[0]):
+        windows = jnp.where(lane == n, windows_ref[n, :, 0:1].astype(F32), windows)
+    windows = windows.astype(BF16)
+    for k in range(out_ref.shape[0]):
+        out_ref[k, :deep] = own_ref[...]
+        out_ref[k, deep : 2 * deep] = outer_ref[...]
+        out_ref[k, 2 * deep :] = windows
+
+
+def psi_kernel(place_ref, list_ref, near_ref, partner_ref, *refs):
+    parts = refs[:SIDE]
+    psi_ref, dens_ref, target_ref, flipped_hbm, dense_ref, flipped_ref, acc_ref, sem = refs[SIDE:]
+    side = len(parts)
+    per, _, wide = parts[0].shape
+    zl, y, group, core = (place_ref[i] for i in range(4))
     dense_ref[...] = jnp.zeros_like(dense_ref)
     flipped_ref[...] = jnp.zeros_like(flipped_ref)
-    _, per, _, wide = parts_ref.shape
-    deep, width = outer[0].shape
+    _, deep, width = partner_ref.shape
     owned = deep // BLK
+    lane = lax.broadcasted_iota(jnp.int32, target_ref.shape, 1)
+    device = lane // WINDOW
+    atoms = (lane % WINDOW).astype(F32)
     for k in range(side):
-        part_copies[k].wait()
+        window = near_ref[k, 2 * deep :, :BLK].astype(F32)
+        window = window[0:1] * 16.0 + window[1:2]
+        for n in range(2 * side):
+            atoms += jnp.where(device == n * side + k, window[:, n : n + 1], 0.0)
+    target_ref[...] = jnp.where(atoms >= NATOM, atoms - NATOM, atoms)
+    for k, part in enumerate(parts):
+        origin = lax.rem(zl - k + side, side)
         for r in range(per):
-            batch = (k * side + y) * per + r
-            row = (k * per + r) * BLK
+            batch = (origin * side + y) * per + r
+            row = pl.multiple_of((origin * per + r) * BLK, BLK)
             for j in range(wide // BLK):
                 block = list_ref[batch, j] - (group - 1) * owned
                 below, above = block < owned, block >= 2 * owned
@@ -106,43 +120,27 @@
                 far = jnp.where(below == (core == 0), 2, 1)
                 third = jnp.where(jnp.logical_or(below, above), far, 0)
                 col = pl.multiple_of((third * owned + within) * BLK, BLK)
-                tile = parts_ref[k, r, :, j * BLK : (j + 1) * BLK]
-                dense_ref[row : row + BLK, pl.ds(col, BLK)] = tile
-                flipped_ref[pl.ds(col, BLK), row : row + BLK] = tile.T
-    copy = pltpu.make_async_copy(flipped_ref, flipped_out, sems.at[side + 1])
+                tile = part[r, :, j * BLK : (j + 1) * BLK]
+                dense_ref[pl.ds(row, BLK), pl.ds(col, BLK)] = tile
+                flipped_ref[pl.ds(col, BLK), pl.ds(row, BLK)] = tile.T
+    copy = pltpu.make_async_copy(flipped_ref, flipped_hbm.at[0], sem)
     copy.start()
-    near_copy.wait()
-    lane = lax.broadcasted_iota(jnp.int32, (1, BLK), 1)
-    device = lane // WINDOW
-    atoms = (lane % WINDOW).astype(F32)
     for k in range(side):
-        at = lax.rem(y - k + side, side)
-        own, partner = core * side + at, (1 - core) * side + at
         chosen = jnp.concatenate(
-            [near_ref[own, :deep], near_ref[partner, :deep], outer[k][...]], axis=0
+            [near_ref[k, :deep], partner_ref[k], near_ref[k, deep : 2 * deep]], axis=0
         )
         psi = jnp.dot(dense_ref[...], chosen, preferred_element_type=F32).astype(BF16)
         psi_ref[:, k * width : (k + 1) * width] = psi
-        wide = psi.astype(F32)
-        square = wide * wide
+        wide_psi = psi.astype(F32)
+        square = wide_psi * wide_psi
         part = square[:, :BLK] + square[:, BLK:]
         if k == 0:
             acc_ref[...] = part
         else:
             acc_ref[...] += part
-    for n in range(2 * side):
-        window = near_ref[n, deep:, :BLK].astype(F32)
-        window = window[0:1] * 16.0 + window[1:2]
-        atoms += jnp.where(device == n, window, 0.0)
-    atoms = jnp.where(atoms >= NATOM, atoms - NATOM, atoms)
-    atoms = jnp.where(device < 2 * side, atoms, 0.0)
-    dens_ref[...] = jnp.zeros_like(dens_ref)
-    for n in range(dens_ref.shape[0]):
-        dens_ref[n, 2:3, :] = atoms
     for n in range(acc_ref.shape[0] // BLK):
         tile = acc_ref[n * BLK : (n + 1) * BLK, :].T
-        row = 2.0 * jnp.sum(tile, axis=0, keepdims=True)
-        dens_ref[x * side + n // 2, n % 2 : n % 2 + 1, :] = row
+        dens_ref[n // 2, n % 2 : n % 2 + 1, :] = 2.0 * jnp.sum(tile, axis=0, keepdims=True)
     copy.wait()
 
 
@@ -186,14 +184,9 @@
     return jnp.concatenate([rows[:WINDOW], rows[WINDOW:]], axis=1)
 
 
-def route_first_kernel(place_ref, x_ref, target_ref, out_ref, match_ref):
+def route_first_kernel(x_ref, target_ref, out_ref, match_ref):
     n = x_ref.shape[0] * ROWS
-    zl = place_ref[0]
-    half = [target_ref[k * SIDE + zl, 2:3, :] for k in range(SIDE)]
-    targets = jnp.concatenate(
-        [half[0] + pltpu.roll(half[1], BLK // 2, 1), half[2] + pltpu.roll(half[3], BLK // 2, 1)],
-        axis=1,
-    )
+    targets = target_ref[...]
     x = x_ref[...].reshape(n, x_ref.shape[2])
     meta = x[:, :BLK].astype(F32)
     meta = jnp.concatenate([meta[WINDOW:], meta[:WINDOW]], axis=0)
@@ -294,9 +287,8 @@
     place_ref, flipped_hbm, psi_ref, scaled_ref, out_ref, weighted, flipped_ref, scratch, sem
 ):
     side, deep, width = out_ref.shape
-    copy = pltpu.make_async_copy(flipped_hbm.at[2 * deep :], flipped_ref, sem)
+    copy = pltpu.make_async_copy(flipped_hbm.at[0, 2 * deep :], flipped_ref, sem)
     copy.start()
-    y = place_ref[1]
     scaled_psi(psi_ref, scaled_ref, weighted, scratch)
     copy.wait()
     for k in range(side):
@@ -305,7 +297,7 @@
             weighted[:, k * width : (k + 1) * width],
             preferred_element_type=F32,
         )
-        out_ref[lax.rem(y - k + side, side)] = terms.astype(BF16)
+        out_ref[k] = terms.astype(BF16)
 
 
 def near_kernel(
@@ -313,9 +305,9 @@
 ):
     count, deep, width = out_ref.shape
     side = count // 2
-    copy = pltpu.make_async_copy(flipped_hbm.at[: 2 * deep], flipped_ref, sem)
+    copy = pltpu.make_async_copy(flipped_hbm.at[0, : 2 * deep], flipped_ref, sem)
     copy.start()
-    y, core = place_ref[1], place_ref[3]
+    core = place_ref[3]
     scaled_psi(psi_ref, scaled_ref, weighted, scratch)
     copy.wait()
     for k in range(side):
@@ -324,9 +316,8 @@
             weighted[:, k * width : (k + 1) * width],
             preferred_element_type=F32,
         ).astype(BF16)
-        at = lax.rem(y - k + side, side)
-        out_ref[core * side + at] = terms[:deep]
-        out_ref[(1 - core) * side + at] = terms[deep:]
+        out_ref[core * side + k] = terms[:deep]
+        out_ref[(1 - core) * side + k] = terms[deep:]
 
 
 def from_behind(value, axis):
@@ -340,6 +331,10 @@
     groups = lax.axis_size(GRID)
     pairs = [(g, g + 1 if g % 2 else g - 1) for g in range(1, groups - 1)]
     return lax.ppermute(value, GRID, pairs)
+
+
+def swap(value):
+    return lax.ppermute(value, "c", [(0, 1), (1, 0)])
 
 
 def exchange(parts, axes):
@@ -362,11 +357,10 @@
     points = point_weights.shape[0]
     batches, batch_points, _ = basis_values.shape
     deep, width = orbitals.shape
-    place = jnp.stack([lax.axis_index(a) for a in ("zl", "y", GRID, "c", "x")]).astype(jnp.int32)
+    place = jnp.stack([lax.axis_index(a) for a in ("zl", "y", GRID, "c")]).astype(jnp.int32)
     plane, column_size = lax.axis_size(PLANE), lax.axis_size(COLUMN)
     square_f32 = shape((points, feat), F32)
 
-    parts = lax.all_gather(basis_values, "zl")
     outer = across(orbitals)
     selector, spread, meta, window = call(
         prepare_kernel,
@@ -374,41 +368,43 @@
             shape((ROWS, points), BF16),
             shape((points, BLK), BF16),
             shape((ROWS, feat), F32),
-            shape((ROWS, width), BF16),
+            shape((2 * SIDE, ROWS, BLK), BF16),
         ),
         2,
         scratch=[pltpu.VMEM((8, batch_points), F32)],
     )(point_atoms.reshape(batches, batch_points), point_weights.reshape(batches, batch_points))
-    own = jnp.concatenate([orbitals, window], axis=0)
-    chip = ("c", "y")
-    near = exchange(jnp.broadcast_to(own, (2 * SIDE, *own.shape)), chip)
-    outer = from_behind(outer, "y")
+    windows = exchange(window, ("x", "c"))
+    rows = call(rows_kernel, shape((SIDE, 2 * deep + ROWS, width), BF16), 3)(
+        orbitals, outer, windows
+    )
+    near = exchange(rows, ("y",))
+    near, *parts = lax.optimization_barrier((near, *from_behind(basis_values, "zl")))
+    partner = swap(near[:, :deep])
 
     total_points = SIDE * points
     everywhere = pl.BlockSpec(memory_space=pltpu.VMEM)
     scalars = pl.BlockSpec(memory_space=pltpu.SMEM)
     anywhere = pl.BlockSpec(memory_space=pl.ANY)
-    psi, squares, flipped = pl.pallas_call(
+    psi, squares, targets, flipped = pl.pallas_call(
         psi_kernel,
         out_shape=(
             shape((total_points, SIDE * width), BF16),
-            shape((SIDE * SIDE, 4, batch_points), F32),
-            shape((3 * deep, total_points), BF16),
+            shape((SIDE, batches, batch_points), F32),
+            shape((1, plane * WINDOW), F32),
+            shape((SPARE, 3 * deep, total_points), BF16),
         ),
-        in_specs=[scalars] * 2 + [anywhere] * 2 + [everywhere] * SIDE,
-        out_specs=(everywhere, everywhere, anywhere),
+        in_specs=[scalars] * 2 + [everywhere] * (2 + SIDE),
+        out_specs=(everywhere, everywhere, everywhere, anywhere),
         scratch_shapes=[
             pltpu.VMEM((total_points, 3 * deep), BF16),
             pltpu.VMEM((3 * deep, total_points), BF16),
             pltpu.VMEM((total_points, BLK), F32),
-            pltpu.VMEM(parts.shape, BF16),
-            pltpu.VMEM(near.shape, BF16),
-            pltpu.SemaphoreType.DMA((SIDE + 2,)),
+            pltpu.SemaphoreType.DMA,
         ],
         compiler_params=pltpu.CompilerParams(vmem_limit_bytes=VMEM),
-    )(place, block_lists, parts, near, *outer)
-    squares = exchange(squares, ("x", "zl"))
-    radius = jnp.cbrt(jnp.sum(squares[:, :2], axis=0))
+    )(place, block_lists, near, partner, *parts)
+    squares = exchange(squares, ("zl",))
+    radius = jnp.cbrt(jnp.sum(squares, axis=0))
 
     weights = point_weights.reshape(batches, batch_points)
     to_plane = shape((plane, ROWS, feat), BF16)
@@ -423,9 +419,8 @@
     sums, match = call(
         route_first_kernel,
         (to_plane, shape((column_size * ROWS, plane * WINDOW), BF16)),
-        3,
-        smem=(0,),
-    )(place, exchange(sent, COLUMN), squares)
+        2,
+    )(exchange(sent, COLUMN), targets)
     hidden, message, mass_rows, sent = call(
         second_kernel,
         (
@@ -467,7 +462,7 @@
     outer = fock_terms(outer_kernel, SIDE, deep)
     near = fock_terms(near_kernel, 2 * SIDE, 2 * deep)
     arrived = across(jnp.sum(exchange(outer, ("y",)).astype(F32), axis=0).astype(BF16))
-    fock = jnp.sum(exchange(near, chip).astype(F32), axis=0) + arrived.astype(F32)
+    fock = jnp.sum(exchange(near, ("c", "y")).astype(F32), axis=0) + arrived.astype(F32)
     return fock, potential.reshape(-1)
 
 

time: 208 us -> 205 us (0.986)
  between operations: 14.3 us -> 0.85 us
  blocking collectives: 89.4 us -> 93.7 us
  starting transfers between devices: 37.3 us -> 40.8 us
  Pallas kernels: 15.2 us -> 17.9 us
    ppermute x2, waiting for transfers between devices: 11.2 us -> 0.01 us  [across(): return lax.ppermute(value, GRID, pairs)]
    ppermute x3, waiting for transfers between devices: 5.34 us -> 13.9 us  [from_behind(): lax.ppermute(value, axis, [(i, (i + k) % SIDE) for i in range(SIDE)])]
    all_to_all x3, starting transfers between devices: 20.4 us -> 14.2 us  [exchange(): return lax.all_to_all(parts, axes, split_axis=0, concat_axis=0, tiled=True)]
    ppermute x2, starting transfers between devices: 7.11 us -> 13 us  [across(): return lax.ppermute(value, GRID, pairs)]
    all_to_all x6 -> x7, blocking collectives: 89.4 us -> 93.7 us  [exchange(): return lax.all_to_all(parts, axes, split_axis=0, concat_axis=0, tiled=True)]
    ppermute x0 -> x1, starting transfers between devices: none -> 3.38 us  [swap(): return lax.ppermute(value, 'c', [(0, 1), (1, 0)])]
    unnamed x33 -> x41, local copies, waits for them, and re-layouts: 8.1 us -> 9.85 us
  transfers between devices with their start and end apart: 9 -> 9, of which waited for: 6 -> 5; matrix products, arithmetic and copies ran while one was open for 1% -> 0% of each run, Pallas kernels for 2% -> 2%
where the time goes in v4:
time: 205 us; the launch traced here: 204 us
  blocking collectives  93.7 us (46%)
  starting transfers between devices  40.8 us (20%)
  waiting for transfers between devices  38.7 us (19%)
  Pallas kernels  17.9 us (9%)
  local copies, waits for them, and re-layouts  10.8 us (5%)
    all_to_all x7, blocking collectives, exchange(): return lax.all_to_all(parts, axes, split_axis=0, concat_axis=0, tiled=True)  93.7 us
    all_to_all x3, waiting for transfers between devices, exchange(): return lax.all_to_all(parts, axes, split_axis=0, concat_axis=0, tiled=True)  22.9 us
    all_to_all x3, starting transfers between devices, exchange(): return lax.all_to_all(parts, axes, split_axis=0, concat_axis=0, tiled=True)  14.2 us
    ppermute x3, waiting for transfers between devices, from_behind(): lax.ppermute(value, axis, [(i, (i + k) % SIDE) for i in range(SIDE)])  13.9 us
    ppermute x2, starting transfers between devices, across(): return lax.ppermute(value, GRID, pairs)  13 us
    ppermute x3, starting transfers between devices, from_behind(): lax.ppermute(value, axis, [(i, (i + k) % SIDE) for i in range(SIDE)])  10.2 us
    unnamed x41, local copies, waits for them, and re-layouts  9.85 us
    pallas_call x2, Pallas kernels, fock_terms(): pl.pallas_call(kernel, out_shape=shape((devices, deep, width), BF16), in_...  7.39 us
  transfers between devices with their start and end apart: 9, of which 5 were waited for; matrix products, arithmetic and copies ran while one was open for 0% of the time, Pallas kernels for 2%

profile of v4, /device:TPU:1, one launch (start us, length us, event | category | flops | bytes accessed | tf_op | source)
XLA Modules:
  0.0 204.0 jit_solution(9769612756116857773)
XLA Ops:
  0.6 10.2 %collective-permute-start = (bf16[384,256]{1,0:T(8,128)(2,1)}, bf16[384,256]{1,0:T(8,128)(2,1)S(1)}, u32[]{:S(2)}, u32[]{:S(2)}) collective-permute-start(bf16[384,256]{1,0:T(8,128)(2,1)} %own_ref.1), channel_id=1, source_target_pairs={{16,32},{32,16},{48,64},{64,48},{80,96},{96,80},{112,128},{128,112... | collective-permute-start | bytes 589832 | tf_op jit(solution)/shard_map/ppermute | solution.py:333
  12.6 12.3 %all_to_all.50.windows_ref = bf16[8,16,128]{2,1,0:T(8,128)(2,1)S(1)} all-to-all(bf16[8,16,128]{2,1,0:T(8,128)(2,1)S(1)} %get-tuple-element.27), channel_id=1, replica_groups=mesh['x'=4,'zh'=4,'c'=2,'zl'=4,'y'=4] {'x','c'}, dimensions={0} | all-to-all | bytes 65536 | tf_op jit(solution)/shard_map/all_to_all | solution.py:341
  27.2 4.3 %all-to-all-start.1 = ((bf16[4,784,256]{2,1,0:T(8,128)(2,1)}), bf16[4,784,256]{2,1,0:T(8,128)(2,1)S(1)}, u32[]{:S(2)}, u32[]{:S(2)}) async-start(bf16[4,784,256]{2,1,0:T(8,128)(2,1)} %shard_map.114), calls=%async_computation.1 | async-start | bytes 3211264 | tf_op jit(solution)/shard_map/all_to_all | solution.py:341
  31.5 3.1 %collective-permute-start.2 = (bf16[2,128,512]{2,1,0:T(8,128)(2,1)S(1)}, bf16[2,128,512]{2,1,0:T(8,128)(2,1)S(1)}, u32[]{:S(2)}, u32[]{:S(2)}) collective-permute-start(bf16[2,128,512]{2,1,0:T(8,128)(2,1)S(1)} %copy-done.5), channel_id=1, source_target_pairs={{0,8},{4,12},{8,0},{12,4},{1,9},{5,13},{9,1},{13,5},{2,10},{6,14},... | collective-permute-start | bytes 786440 | tf_op jit(solution)/shard_map/ppermute | solution.py:325
  34.6 2.7 %collective-permute-start.1 = (bf16[2,128,512]{2,1,0:T(8,128)(2,1)S(1)}, bf16[2,128,512]{2,1,0:T(8,128)(2,1)S(1)}, u32[]{:S(2)}, u32[]{:S(2)}) collective-permute-start(bf16[2,128,512]{2,1,0:T(8,128)(2,1)S(1)} %copy-done.5), channel_id=1, source_target_pairs={{0,4},{4,8},{8,12},{12,0},{1,5},{5,9},{9,13},{13,1},{2,6},{6,10},{... | collective-permute-start | bytes 786440 | tf_op jit(solution)/shard_map/ppermute | solution.py:325
  37.2 4.4 %collective-permute-start.3 = (bf16[2,128,512]{2,1,0:T(8,128)(2,1)S(1)}, bf16[2,128,512]{2,1,0:T(8,128)(2,1)S(1)}, u32[]{:S(2)}, u32[]{:S(2)}) collective-permute-start(bf16[2,128,512]{2,1,0:T(8,128)(2,1)S(1)} %copy-done.5), channel_id=1, source_target_pairs={{0,12},{4,0},{8,4},{12,8},{1,13},{5,1},{9,5},{13,9},{2,14},{6,2},{... | collective-permute-start | bytes 786440 | tf_op jit(solution)/shard_map/ppermute | solution.py:325
  41.7 11.6 %collective-permute-done.2.refs_2_ = bf16[2,128,512]{2,1,0:T(8,128)(2,1)S(1)} collective-permute-done((bf16[2,128,512]{2,1,0:T(8,128)(2,1)S(1)}, bf16[2,128,512]{2,1,0:T(8,128)(2,1)S(1)}, u32[]{:S(2)}, u32[]{:S(2)}) %collective-permute-start.2) | collective-permute-done | bytes 262176 | tf_op jit(solution)/shard_map/ppermute | solution.py:325
  54.7 2.3 %collective-permute-done.3.refs_3_ = bf16[2,128,512]{2,1,0:T(8,128)(2,1)S(1)} collective-permute-done((bf16[2,128,512]{2,1,0:T(8,128)(2,1)S(1)}, bf16[2,128,512]{2,1,0:T(8,128)(2,1)S(1)}, u32[]{:S(2)}, u32[]{:S(2)}) %collective-permute-start.3) | collective-permute-done | bytes 262176 | tf_op jit(solution)/shard_map/ppermute | solution.py:325
  58.6 3.4 %collective-permute-start.4 = (bf16[4,384,256]{2,1,0:T(8,128)(2,1)}, bf16[4,384,256]{2,1,0:T(8,128)(2,1)S(1)}, u32[]{:S(2)}, u32[]{:S(2)}) collective-permute-start(bf16[4,384,256]{2,1,0:T(8,128)(2,1)} %slice.3), channel_id=1, source_target_pairs={{0,16},{16,0},{1,17},{17,1},{2,18},{18,2},{3,19},{19,3},{4,20},{20... | collective-permute-start | bytes 2359304 | tf_op jit(solution)/shard_map/ppermute | solution.py:337
  62.2 1.9 collective-permute-done.4.partner_ref
  66.9 5.7 %shard_map.115 = (bf16[1024,1024]{1,0:T(8,128)(2,1)S(1)}, f32[4,2,128]{2,1,0:T(2,128)S(1)}, f32[1,256]{1,0:T(1,128)S(1)}, bf16[16,1152,1024]{2,1,0:T(8,128)(2,1)}) custom-call(s32[4]{0:T(128)S(1)} %pad_add_fusion.place_ref, s32[32,4]{1,0:T(8,128)S(1)} %copy.12.list_ref, bf16[4,784,256]{2,1,0:T(8,128)(2,1)S(1)} %all-to-all-done.1.near_ref, ...), custom_call_target="tpu_custom_call" | custom-call | tf_op jit(solution)/shard_map/pallas_call | solution.py:388
  74.0 8.4 %all_to_all.51 = f32[4,2,128]{2,1,0:T(2,128)S(1)} all-to-all(f32[4,2,128]{2,1,0:T(2,128)S(1)} %get-tuple-element.35), channel_id=1, replica_groups=mesh['x'=4,'zh'=4,'c'=2,'zl'=4,'y'=4] {'zl'}, dimensions={0} | all-to-all | bytes 8192 | tf_op jit(solution)/shard_map/all_to_all | solution.py:341
  83.0 18.8 %all_to_all.52.x_ref = bf16[16,16,256]{2,1,0:T(8,128)(2,1)S(1)} all-to-all(bf16[16,16,256]{2,1,0:T(8,128)(2,1)S(1)} %get-tuple-element.38), channel_id=1, replica_groups=mesh['x'=4,'zh'=4,'c'=2,'zl'=4,'y'=4] {'zh','zl'}, dimensions={0} | all-to-all | bytes 262144 | tf_op jit(solution)/shard_map/all_to_all | solution.py:341
  102.2 19.6 %all_to_all.53.z_ref = bf16[32,16,256]{2,1,0:T(8,128)(2,1)S(1)} all-to-all(bf16[32,16,256]{2,1,0:T(8,128)(2,1)S(1)} %get-tuple-element.40), channel_id=1, replica_groups=mesh['x'=4,'zh'=4,'c'=2,'zl'=4,'y'=4] {'x','c','y'}, dimensions={0} | all-to-all | bytes 524288 | tf_op jit(solution)/shard_map/all_to_all | solution.py:341
  122.5 14.8 %all_to_all.54.x_ref = bf16[16,16,128]{2,1,0:T(8,128)(2,1)S(1)} all-to-all(bf16[16,16,128]{2,1,0:T(8,128)(2,1)S(1)} %get-tuple-element.45), channel_id=1, replica_groups=mesh['x'=4,'zh'=4,'c'=2,'zl'=4,'y'=4] {'zh','zl'}, dimensions={0} | all-to-all | bytes 131072 | tf_op jit(solution)/shard_map/all_to_all | solution.py:341
  137.5 13.1 %all_to_all.55.z_ref = bf16[32,16,128]{2,1,0:T(8,128)(2,1)S(1)} all-to-all(bf16[32,16,128]{2,1,0:T(8,128)(2,1)S(1)} %shard_map.119), channel_id=1, replica_groups=mesh['x'=4,'zh'=4,'c'=2,'zl'=4,'y'=4] {'x','c','y'}, dimensions={0} | all-to-all | bytes 262144 | tf_op jit(solution)/shard_map/all_to_all | solution.py:341
  151.8 6.8 %all_to_all.56.scaled_ref = f32[4,2,128]{2,1,0:T(2,128)S(1)} all-to-all(f32[4,2,128]{2,1,0:T(2,128)S(1)} %get-tuple-element.50), channel_id=1, replica_groups=mesh['x'=4,'zh'=4,'c'=2,'zl'=4,'y'=4] {'zl'}, dimensions={0} | all-to-all | bytes 8192 | tf_op jit(solution)/shard_map/all_to_all | solution.py:341
  158.6 3.6 %shard_map.122 = bf16[4,384,256]{2,1,0:T(8,128)(2,1)} custom-call(s32[4]{0:T(128)S(1)} %pad_add_fusion.place_ref, bf16[16,1152,1024]{2,1,0:T(8,128)(2,1)} %get-tuple-element.33.flipped_hbm, bf16[1024,1024]{1,0:T(8,128)(2,1)S(1)} %copy-done.1, f32[4,2,128]{2,1,0:T(2,128)S(1)} %all_to_all.56.scaled_ref), custom_call_target="tpu_custom_call" | custom-call | tf_op jit(solution)/shard_map/pallas_call | solution.py:448
  162.1 3.5 %all-to-all-start.9 = ((bf16[4,384,256]{2,1,0:T(8,128)(2,1)}), bf16[4,384,256]{2,1,0:T(8,128)(2,1)S(1)}, u32[]{:S(2)}, u32[]{:S(2)}) async-start(bf16[4,384,256]{2,1,0:T(8,128)(2,1)} %shard_map.122), calls=%async_computation.9 | async-start | bytes 1572864 | tf_op jit(solution)/shard_map/all_to_all | solution.py:341
  165.6 3.8 %shard_map.121 = bf16[8,384,256]{2,1,0:T(8,128)(2,1)S(1)} custom-call(s32[4]{0:T(128)S(1)} %pad_add_fusion.place_ref, bf16[16,1152,1024]{2,1,0:T(8,128)(2,1)} %get-tuple-element.33.flipped_hbm, bf16[1024,1024]{1,0:T(8,128)(2,1)S(1)} %copy-done.1, f32[4,2,128]{2,1,0:T(2,128)S(1)} %all_to_all.56.scaled_ref), custom_call_target="tpu_custom_call" | custom-call | tf_op jit(solution)/shard_map/pallas_call | solution.py:448
  170.7 5.3 %all-to-all-done.9 = bf16[4,384,256]{2,1,0:T(8,128)(2,1)S(1)} async-done(((bf16[4,384,256]{2,1,0:T(8,128)(2,1)}), bf16[4,384,256]{2,1,0:T(8,128)(2,1)S(1)}, u32[]{:S(2)}, u32[]{:S(2)}) %all-to-all-start.9) | async-done | bytes 786464 | tf_op jit(solution)/shard_map/all_to_all | solution.py:341
  176.0 6.4 %all-to-all-start.8 = ((bf16[8,384,256]{2,1,0:T(8,128)(2,1)}), bf16[8,384,256]{2,1,0:T(8,128)(2,1)S(1)}, u32[]{:S(2)}, u32[]{:S(2)}) async-start(bf16[8,384,256]{2,1,0:T(8,128)(2,1)} %copy-done.2), calls=%async_computation.8 | async-start | bytes 3145728 | tf_op jit(solution)/shard_map/all_to_all | solution.py:341
  182.5 2.8 %collective-permute-start.5 = (bf16[384,256]{1,0:T(8,128)(2,1)S(1)}, bf16[384,256]{1,0:T(8,128)(2,1)S(1)}, u32[]{:S(2)}, u32[]{:S(2)}) collective-permute-start(bf16[384,256]{1,0:T(8,128)(2,1)S(1)} %reduce_sum.32), channel_id=1, source_target_pairs={{16,32},{32,16},{48,64},{64,48},{80,96},{96,80},{112,128},{128,112... | collective-permute-start | bytes 589832 | tf_op jit(solution)/shard_map/ppermute | solution.py:333
  185.3 17.6 %all-to-all-done.8 = bf16[8,384,256]{2,1,0:T(8,128)(2,1)S(1)} async-done(((bf16[8,384,256]{2,1,0:T(8,128)(2,1)}), bf16[8,384,256]{2,1,0:T(8,128)(2,1)S(1)}, u32[]{:S(2)}, u32[]{:S(2)}) %all-to-all-start.8) | async-done | bytes 1572896 | tf_op jit(solution)/shard_map/all_to_all | solution.py:341
  (59 shorter events, 16.8 us)
Async XLA Ops:
  0.6 24.3 %collective-permute-start = (bf16[384,256]{1,0:T(8,128)(2,1)}, bf16[384,256]{1,0:T(8,128)(2,1)S(1)}, u32[]{:S(2)}, u32[]{:S(2)}) collective-permute-start(bf16[384,256]{1,0:T(8,128)(2,1)} %own_ref.1), channel_id=1, source_target_pairs={{16,32},{32,16},{48,64},{64,48},{80,96},{96,80},{112,128},{128,112... | collective-permute-start | bytes 589832 | tf_op jit(solution)/shard_map/ppermute | solution.py:333
  24.9 0.9 copy-start.12
  27.2 4.3 %copy-start.5 = (bf16[2,128,512]{2,1,0:T(8,128)(2,1)S(1)}, bf16[2,128,512]{2,1,0:T(8,128)(2,1)}, u32[]{:S(2)}) copy-start(bf16[2,128,512]{2,1,0:T(8,128)(2,1)} %refs_0_) | copy-start | bytes 786436
  27.2 34.8 %copy-start.19 = (s32[32,4]{0,1:T(4,128)S(1)}, s32[32,4]{0,1:T(4,128)}, u32[]{:S(2)}) copy-start(s32[32,4]{0,1:T(4,128)} %param.11) | copy-start | bytes 1540
  27.2 30.5 %all-to-all-start.1 = ((bf16[4,784,256]{2,1,0:T(8,128)(2,1)}), bf16[4,784,256]{2,1,0:T(8,128)(2,1)S(1)}, u32[]{:S(2)}, u32[]{:S(2)}) async-start(bf16[4,784,256]{2,1,0:T(8,128)(2,1)} %shard_map.114), calls=%async_computation.1 | async-start | bytes 3211264 | tf_op jit(solution)/shard_map/all_to_all | solution.py:341
  31.5 21.8 %collective-permute-start.2 = (bf16[2,128,512]{2,1,0:T(8,128)(2,1)S(1)}, bf16[2,128,512]{2,1,0:T(8,128)(2,1)S(1)}, u32[]{:S(2)}, u32[]{:S(2)}) collective-permute-start(bf16[2,128,512]{2,1,0:T(8,128)(2,1)S(1)} %copy-done.5), channel_id=1, source_target_pairs={{0,8},{4,12},{8,0},{12,4},{1,9},{5,13},{9,1},{13,5},{2,10},{6,14},... | collective-permute-start | bytes 786440 | tf_op jit(solution)/shard_map/ppermute | solution.py:325
  34.6 19.4 %collective-permute-start.1 = (bf16[2,128,512]{2,1,0:T(8,128)(2,1)S(1)}, bf16[2,128,512]{2,1,0:T(8,128)(2,1)S(1)}, u32[]{:S(2)}, u32[]{:S(2)}) collective-permute-start(bf16[2,128,512]{2,1,0:T(8,128)(2,1)S(1)} %copy-done.5), channel_id=1, source_target_pairs={{0,4},{4,8},{8,12},{12,0},{1,5},{5,9},{9,13},{13,1},{2,6},{6,10},{... | collective-permute-start | bytes 786440 | tf_op jit(solution)/shard_map/ppermute | solution.py:325
  37.2 19.7 %collective-permute-start.3 = (bf16[2,128,512]{2,1,0:T(8,128)(2,1)S(1)}, bf16[2,128,512]{2,1,0:T(8,128)(2,1)S(1)}, u32[]{:S(2)}, u32[]{:S(2)}) collective-permute-start(bf16[2,128,512]{2,1,0:T(8,128)(2,1)S(1)} %copy-done.5), channel_id=1, source_target_pairs={{0,12},{4,0},{8,4},{12,8},{1,13},{5,1},{9,5},{13,9},{2,14},{6,2},{... | collective-permute-start | bytes 786440 | tf_op jit(solution)/shard_map/ppermute | solution.py:325
  58.6 5.5 %collective-permute-start.4 = (bf16[4,384,256]{2,1,0:T(8,128)(2,1)}, bf16[4,384,256]{2,1,0:T(8,128)(2,1)S(1)}, u32[]{:S(2)}, u32[]{:S(2)}) collective-permute-start(bf16[4,384,256]{2,1,0:T(8,128)(2,1)} %slice.3), channel_id=1, source_target_pairs={{0,16},{16,0},{1,17},{17,1},{2,18},{18,2},{3,19},{19,3},{4,20},{20... | collective-permute-start | bytes 2359304 | tf_op jit(solution)/shard_map/ppermute | solution.py:337
  62.2 20.2 %copy-start.4 = (bf16[2,256,256]{2,1,0:T(8,128)(2,1)S(1)}, bf16[2,256,256]{2,1,0:T(8,128)(2,1)}, u32[]{:S(2)}) copy-start(bf16[2,256,256]{2,1,0:T(8,128)(2,1)} %weight_ref.3) | copy-start | bytes 786436
  62.2 59.6 %copy-start.3 = (bf16[2,256,256]{2,1,0:T(8,128)(2,1)S(1)}, bf16[2,256,256]{2,1,0:T(8,128)(2,1)}, u32[]{:S(2)}) copy-start(bf16[2,256,256]{2,1,0:T(8,128)(2,1)} %atom_weight_ref.3) | copy-start | bytes 786436
  64.1 0.9 copy-start.7
  65.0 0.9 copy-start.9
  66.0 0.9 copy-start.11
  66.9 15.5 %copy-start.14 = (f32[256]{0:T(256)S(1)}, f32[256]{0:T(256)}, u32[]{:S(2)}) copy-start(f32[256]{0:T(256)} %param.13) | copy-start | bytes 3076
  66.9 15.5 %copy-start.15 = (f32[256]{0:T(256)S(1)}, f32[256]{0:T(256)}, u32[]{:S(2)}) copy-start(f32[256]{0:T(256)} %param.15) | copy-start | bytes 3076
  66.9 15.5 %copy-start.16 = (f32[256]{0:T(256)S(1)}, f32[256]{0:T(256)}, u32[]{:S(2)}) copy-start(f32[256]{0:T(256)} %param.16) | copy-start | bytes 3076
  72.7 1.3 copy-start
  83.0 67.6 %copy-start.17 = (f32[256]{0:T(256)S(1)}, f32[256]{0:T(256)}, u32[]{:S(2)}) copy-start(f32[256]{0:T(256)} %param.19) | copy-start | bytes 3076
  121.8 36.7 %copy-start.1 = (bf16[1024,1024]{1,0:T(8,128)(2,1)S(1)}, bf16[1024,1024]{1,0:T(8,128)(2,1)}, u32[]{:S(2)}) copy-start(bf16[1024,1024]{1,0:T(8,128)(2,1)} %copy-done) | copy-start | bytes 6291460
  162.1 13.9 %all-to-all-start.9 = ((bf16[4,384,256]{2,1,0:T(8,128)(2,1)}), bf16[4,384,256]{2,1,0:T(8,128)(2,1)S(1)}, u32[]{:S(2)}, u32[]{:S(2)}) async-start(bf16[4,384,256]{2,1,0:T(8,128)(2,1)} %shard_map.122), calls=%async_computation.9 | async-start | bytes 1572864 | tf_op jit(solution)/shard_map/all_to_all | solution.py:341
  169.5 1.2 copy-start.2
  176.0 27.0 %all-to-all-start.8 = ((bf16[8,384,256]{2,1,0:T(8,128)(2,1)}), bf16[8,384,256]{2,1,0:T(8,128)(2,1)S(1)}, u32[]{:S(2)}, u32[]{:S(2)}) async-start(bf16[8,384,256]{2,1,0:T(8,128)(2,1)} %copy-done.2), calls=%async_computation.8 | async-start | bytes 3145728 | tf_op jit(solution)/shard_map/all_to_all | solution.py:341
  182.5 20.7 %collective-permute-start.5 = (bf16[384,256]{1,0:T(8,128)(2,1)S(1)}, bf16[384,256]{1,0:T(8,128)(2,1)S(1)}, u32[]{:S(2)}, u32[]{:S(2)}) collective-permute-start(bf16[384,256]{1,0:T(8,128)(2,1)S(1)} %reduce_sum.32), channel_id=1, source_target_pairs={{16,32},{32,16},{48,64},{64,48},{80,96},{96,80},{112,128},{128,112... | collective-permute-start | bytes 589832 | tf_op jit(solution)/shard_map/ppermute | solution.py:333
  (5 other events, 3.5 us)

commit v5 on v4

--- a/solution.py
+++ b/solution.py
@@ -15,7 +15,7 @@
 WINDOW = 8
 NATOM = 512
 ROWS = 16
-SPARE = 16
+SPARE = 24
 F32 = jnp.float32
 BF16 = jnp.bfloat16
 
@@ -89,25 +89,16 @@
         out_ref[k, 2 * deep :] = windows
 
 
-def psi_kernel(place_ref, list_ref, near_ref, partner_ref, *refs):
+def spread_kernel(place_ref, list_ref, *refs):
     parts = refs[:SIDE]
-    psi_ref, dens_ref, target_ref, flipped_hbm, dense_ref, flipped_ref, acc_ref, sem = refs[SIDE:]
+    kept_hbm, dense_ref, flipped_ref, sems = refs[SIDE:]
     side = len(parts)
     per, _, wide = parts[0].shape
     zl, y, group, core = (place_ref[i] for i in range(4))
     dense_ref[...] = jnp.zeros_like(dense_ref)
     flipped_ref[...] = jnp.zeros_like(flipped_ref)
-    _, deep, width = partner_ref.shape
-    owned = deep // BLK
-    lane = lax.broadcasted_iota(jnp.int32, target_ref.shape, 1)
-    device = lane // WINDOW
-    atoms = (lane % WINDOW).astype(F32)
-    for k in range(side):
-        window = near_ref[k, 2 * deep :, :BLK].astype(F32)
-        window = window[0:1] * 16.0 + window[1:2]
-        for n in range(2 * side):
-            atoms += jnp.where(device == n * side + k, window[:, n : n + 1], 0.0)
-    target_ref[...] = jnp.where(atoms >= NATOM, atoms - NATOM, atoms)
+    count, deep = dense_ref.shape
+    owned = deep // BLK // 3
     for k, part in enumerate(parts):
         origin = lax.rem(zl - k + side, side)
         for r in range(per):
@@ -123,25 +114,61 @@
                 tile = part[r, :, j * BLK : (j + 1) * BLK]
                 dense_ref[pl.ds(row, BLK), pl.ds(col, BLK)] = tile
                 flipped_ref[pl.ds(col, BLK), pl.ds(row, BLK)] = tile.T
-    copy = pltpu.make_async_copy(flipped_ref, flipped_hbm.at[0], sem)
-    copy.start()
+    copies = [
+        pltpu.make_async_copy(dense_ref, kept_hbm.at[1, :count], sems.at[1]),
+        pltpu.make_async_copy(flipped_ref, kept_hbm.at[0, :, :count], sems.at[0]),
+    ]
+    for copy in copies:
+        copy.start()
+    for copy in copies:
+        copy.wait()
+
+
+def psi_kernel(
+    kept_hbm, near_ref, partner_ref, psi_ref, dens_ref, target_ref, dense_ref, acc_ref, sems
+):
+    side, deep, width = partner_ref.shape
+    parts = 2
+    count = dense_ref.shape[0] // parts
+    loads = [
+        pltpu.make_async_copy(
+            kept_hbm.at[1, h * count : (h + 1) * count],
+            dense_ref.at[h * count : (h + 1) * count],
+            sems.at[h],
+        )
+        for h in range(parts)
+    ]
+    for load in loads:
+        load.start()
+    lane = lax.broadcasted_iota(jnp.int32, target_ref.shape, 1)
+    device = lane // WINDOW
+    atoms = (lane % WINDOW).astype(F32)
     for k in range(side):
-        chosen = jnp.concatenate(
-            [near_ref[k, :deep], partner_ref[k], near_ref[k, deep : 2 * deep]], axis=0
-        )
-        psi = jnp.dot(dense_ref[...], chosen, preferred_element_type=F32).astype(BF16)
-        psi_ref[:, k * width : (k + 1) * width] = psi
-        wide_psi = psi.astype(F32)
-        square = wide_psi * wide_psi
-        part = square[:, :BLK] + square[:, BLK:]
-        if k == 0:
-            acc_ref[...] = part
-        else:
-            acc_ref[...] += part
-    for n in range(acc_ref.shape[0] // BLK):
-        tile = acc_ref[n * BLK : (n + 1) * BLK, :].T
-        dens_ref[n // 2, n % 2 : n % 2 + 1, :] = 2.0 * jnp.sum(tile, axis=0, keepdims=True)
-    copy.wait()
+        window = near_ref[k, 2 * deep :, :BLK].astype(F32)
+        window = window[0:1] * 16.0 + window[1:2]
+        for n in range(2 * side):
+            atoms += jnp.where(device == n * side + k, window[:, n : n + 1], 0.0)
+    target_ref[...] = jnp.where(atoms >= NATOM, atoms - NATOM, atoms)
+    for h in range(parts):
+        loads[h].wait()
+        rows = slice(h * count, (h + 1) * count)
+        for k in range(side):
+            chosen = jnp.concatenate(
+                [near_ref[k, :deep], partner_ref[k], near_ref[k, deep : 2 * deep]], axis=0
+            )
+            psi = jnp.dot(dense_ref[rows, :], chosen, preferred_element_type=F32).astype(BF16)
+            psi_ref[rows, k * width : (k + 1) * width] = psi
+            wide = psi.astype(F32)
+            square = wide * wide
+            part = square[:, :BLK] + square[:, BLK:]
+            if k == 0:
+                acc_ref[...] = part
+            else:
+                acc_ref[...] += part
+        for m in range(count // BLK):
+            n = h * count // BLK + m
+            tile = acc_ref[m * BLK : (m + 1) * BLK, :].T
+            dens_ref[n // 2, n % 2 : n % 2 + 1, :] = 2.0 * jnp.sum(tile, axis=0, keepdims=True)
 
 
 def silu(x):
@@ -284,10 +311,10 @@
 
 
 def outer_kernel(
-    place_ref, flipped_hbm, psi_ref, scaled_ref, out_ref, weighted, flipped_ref, scratch, sem
+    place_ref, kept_hbm, psi_ref, scaled_ref, out_ref, weighted, flipped_ref, scratch, sem
 ):
     side, deep, width = out_ref.shape
-    copy = pltpu.make_async_copy(flipped_hbm.at[0, 2 * deep :], flipped_ref, sem)
+    copy = pltpu.make_async_copy(kept_hbm.at[0, 2 * deep :, : psi_ref.shape[0]], flipped_ref, sem)
     copy.start()
     scaled_psi(psi_ref, scaled_ref, weighted, scratch)
     copy.wait()
@@ -301,11 +328,11 @@
 
 
 def near_kernel(
-    place_ref, flipped_hbm, psi_ref, scaled_ref, out_ref, weighted, flipped_ref, scratch, sem
+    place_ref, kept_hbm, psi_ref, scaled_ref, out_ref, weighted, flipped_ref, scratch, sem
 ):
     count, deep, width = out_ref.shape
     side = count // 2
-    copy = pltpu.make_async_copy(flipped_hbm.at[0, : 2 * deep], flipped_ref, sem)
+    copy = pltpu.make_async_copy(kept_hbm.at[0, : 2 * deep, : psi_ref.shape[0]], flipped_ref, sem)
     copy.start()
     core = place_ref[3]
     scaled_psi(psi_ref, scaled_ref, weighted, scratch)
@@ -377,32 +404,40 @@
     rows = call(rows_kernel, shape((SIDE, 2 * deep + ROWS, width), BF16), 3)(
         orbitals, outer, windows
     )
-    near = exchange(rows, ("y",))
-    near, *parts = lax.optimization_barrier((near, *from_behind(basis_values, "zl")))
-    partner = swap(near[:, :deep])
-
     total_points = SIDE * points
     everywhere = pl.BlockSpec(memory_space=pltpu.VMEM)
     scalars = pl.BlockSpec(memory_space=pltpu.SMEM)
     anywhere = pl.BlockSpec(memory_space=pl.ANY)
-    psi, squares, targets, flipped = pl.pallas_call(
+    kept = pl.pallas_call(
+        spread_kernel,
+        out_shape=shape((SPARE, 3 * deep, 3 * deep), BF16),
+        in_specs=[scalars] * 2 + [everywhere] * SIDE,
+        out_specs=anywhere,
+        scratch_shapes=[
+            pltpu.VMEM((total_points, 3 * deep), BF16),
+            pltpu.VMEM((3 * deep, total_points), BF16),
+            pltpu.SemaphoreType.DMA((2,)),
+        ],
+        compiler_params=pltpu.CompilerParams(vmem_limit_bytes=VMEM),
+    )(place, block_lists, *from_behind(basis_values, "zl"))
+    near, kept = lax.optimization_barrier((exchange(rows, ("y",)), kept))
+    partner = swap(near[:, :deep])
+    psi, squares, targets = pl.pallas_call(
         psi_kernel,
         out_shape=(
             shape((total_points, SIDE * width), BF16),
             shape((SIDE, batches, batch_points), F32),
             shape((1, plane * WINDOW), F32),
-            shape((SPARE, 3 * deep, total_points), BF16),
         ),
-        in_specs=[scalars] * 2 + [everywhere] * (2 + SIDE),
-        out_specs=(everywhere, everywhere, everywhere, anywhere),
+        in_specs=[anywhere, everywhere, everywhere],
+        out_specs=(everywhere, everywhere, everywhere),
         scratch_shapes=[
             pltpu.VMEM((total_points, 3 * deep), BF16),
-            pltpu.VMEM((3 * deep, total_points), BF16),
-            pltpu.VMEM((total_points, BLK), F32),
-            pltpu.SemaphoreType.DMA,
+            pltpu.VMEM((total_points // 2, BLK), F32),
+            pltpu.SemaphoreType.DMA((2,)),
         ],
         compiler_params=pltpu.CompilerParams(vmem_limit_bytes=VMEM),
-    )(place, block_lists, near, partner, *parts)
+    )(kept, near, partner)
     squares = exchange(squares, ("zl",))
     radius = jnp.cbrt(jnp.sum(squares, axis=0))
 
@@ -457,7 +492,7 @@
                 pltpu.SemaphoreType.DMA,
             ],
             compiler_params=pltpu.CompilerParams(vmem_limit_bytes=VMEM),
-        )(place, flipped, psi, scaled)
+        )(place, kept, psi, scaled)
 
     outer = fock_terms(outer_kernel, SIDE, deep)
     near = fock_terms(near_kernel, 2 * SIDE, 2 * deep)

time: 205 us -> 203 us (level)
  local copies, waits for them, and re-layouts: 10.8 us -> 4.96 us
  Pallas kernels: 17.9 us -> 20.5 us
    unnamed x41 -> x29, local copies, waits for them, and re-layouts: 9.85 us -> 4.89 us
    pallas_call x0 -> x1, Pallas kernels: none -> 3.7 us  [local(): pl.pallas_call(spread_kernel, out_shape=shape((SPARE, 3 * deep, 3 * deep)...]
  transfers between devices with their start and end apart: 9 -> 9, of which waited for: 5 -> 5; matrix products, arithmetic and copies ran while one was open for 0% -> 0% of each run, Pallas kernels for 2% -> 4%
where the time goes in v5:
time: 203 us; the launch traced here: 202 us
  blocking collectives  93.7 us (46%)
  starting transfers between devices  40.9 us (20%)
  waiting for transfers between devices  39.9 us (20%)
  Pallas kernels  20.5 us (10%)
  local copies, waits for them, and re-layouts  4.96 us (2%)
    all_to_all x7, blocking collectives, exchange(): return lax.all_to_all(parts, axes, split_axis=0, concat_axis=0, tiled=True)  93.7 us
    all_to_all x3, waiting for transfers between devices, exchange(): return lax.all_to_all(parts, axes, split_axis=0, concat_axis=0, tiled=True)  22.9 us
    ppermute x3, waiting for transfers between devices, from_behind(): lax.ppermute(value, axis, [(i, (i + k) % SIDE) for i in range(SIDE)])  15.1 us
    all_to_all x3, starting transfers between devices, exchange(): return lax.all_to_all(parts, axes, split_axis=0, concat_axis=0, tiled=True)  14.2 us
    ppermute x2, starting transfers between devices, across(): return lax.ppermute(value, GRID, pairs)  13 us
    ppermute x3, starting transfers between devices, from_behind(): lax.ppermute(value, axis, [(i, (i + k) % SIDE) for i in range(SIDE)])  10.2 us
    pallas_call x2, Pallas kernels, fock_terms(): pl.pallas_call(kernel, out_shape=shape((devices, deep, width), BF16), in_...  7.57 us
    unnamed x29, local copies, waits for them, and re-layouts  4.89 us
  transfers between devices with their start and end apart: 9, of which 5 were waited for; matrix products, arithmetic and copies ran while one was open for 0% of the time, Pallas kernels for 4%

profile of v5, /device:TPU:1, one launch (start us, length us, event | category | flops | bytes accessed | tf_op | source)
XLA Modules:
  0.0 202.1 jit_solution(10071890999972610164)
XLA Ops:
  0.6 10.2 %collective-permute-start = (bf16[384,256]{1,0:T(8,128)(2,1)}, bf16[384,256]{1,0:T(8,128)(2,1)S(1)}, u32[]{:S(2)}, u32[]{:S(2)}) collective-permute-start(bf16[384,256]{1,0:T(8,128)(2,1)} %own_ref.1), channel_id=1, source_target_pairs={{16,32},{32,16},{48,64},{64,48},{80,96},{96,80},{112,128},{128,112... | collective-permute-start | bytes 589832 | tf_op jit(solution)/shard_map/ppermute | solution.py:360
  12.6 12.3 %all_to_all.50.windows_ref = bf16[8,16,128]{2,1,0:T(8,128)(2,1)S(1)} all-to-all(bf16[8,16,128]{2,1,0:T(8,128)(2,1)S(1)} %get-tuple-element.23), channel_id=1, replica_groups=mesh['x'=4,'zh'=4,'c'=2,'zl'=4,'y'=4] {'x','c'}, dimensions={0} | all-to-all | bytes 65536 | tf_op jit(solution)/shard_map/all_to_all | solution.py:368
  27.1 4.3 %all-to-all-start.1 = ((bf16[4,784,256]{2,1,0:T(8,128)(2,1)}), bf16[4,784,256]{2,1,0:T(8,128)(2,1)S(1)}, u32[]{:S(2)}, u32[]{:S(2)}) async-start(bf16[4,784,256]{2,1,0:T(8,128)(2,1)} %shard_map.114), calls=%async_computation.1 | async-start | bytes 3211264 | tf_op jit(solution)/shard_map/all_to_all | solution.py:368
  31.4 3.1 %collective-permute-start.2 = (bf16[2,128,512]{2,1,0:T(8,128)(2,1)S(1)}, bf16[2,128,512]{2,1,0:T(8,128)(2,1)S(1)}, u32[]{:S(2)}, u32[]{:S(2)}) collective-permute-start(bf16[2,128,512]{2,1,0:T(8,128)(2,1)S(1)} %copy-done.5), channel_id=1, source_target_pairs={{0,8},{4,12},{8,0},{12,4},{1,9},{5,13},{9,1},{13,5},{2,10},{6,14},... | collective-permute-start | bytes 786440 | tf_op jit(solution)/shard_map/ppermute | solution.py:352
  34.5 2.7 %collective-permute-start.1 = (bf16[2,128,512]{2,1,0:T(8,128)(2,1)S(1)}, bf16[2,128,512]{2,1,0:T(8,128)(2,1)S(1)}, u32[]{:S(2)}, u32[]{:S(2)}) collective-permute-start(bf16[2,128,512]{2,1,0:T(8,128)(2,1)S(1)} %copy-done.5), channel_id=1, source_target_pairs={{0,4},{4,8},{8,12},{12,0},{1,5},{5,9},{9,13},{13,1},{2,6},{6,10},{... | collective-permute-start | bytes 786440 | tf_op jit(solution)/shard_map/ppermute | solution.py:352
  37.2 4.4 %collective-permute-start.3 = (bf16[2,128,512]{2,1,0:T(8,128)(2,1)S(1)}, bf16[2,128,512]{2,1,0:T(8,128)(2,1)S(1)}, u32[]{:S(2)}, u32[]{:S(2)}) collective-permute-start(bf16[2,128,512]{2,1,0:T(8,128)(2,1)S(1)} %copy-done.5), channel_id=1, source_target_pairs={{0,12},{4,0},{8,4},{12,8},{1,13},{5,1},{9,5},{13,9},{2,14},{6,2},{... | collective-permute-start | bytes 786440 | tf_op jit(solution)/shard_map/ppermute | solution.py:352
  41.8 11.4 %collective-permute-done.2.refs_2_ = bf16[2,128,512]{2,1,0:T(8,128)(2,1)S(1)} collective-permute-done((bf16[2,128,512]{2,1,0:T(8,128)(2,1)S(1)}, bf16[2,128,512]{2,1,0:T(8,128)(2,1)S(1)}, u32[]{:S(2)}, u32[]{:S(2)}) %collective-permute-start.2) | collective-permute-done | bytes 262176 | tf_op jit(solution)/shard_map/ppermute | solution.py:352
  53.2 3.7 %collective-permute-done.3.refs_3_ = bf16[2,128,512]{2,1,0:T(8,128)(2,1)S(1)} collective-permute-done((bf16[2,128,512]{2,1,0:T(8,128)(2,1)S(1)}, bf16[2,128,512]{2,1,0:T(8,128)(2,1)S(1)}, u32[]{:S(2)}, u32[]{:S(2)}) %collective-permute-start.3) | collective-permute-done | bytes 262176 | tf_op jit(solution)/shard_map/ppermute | solution.py:352
  56.9 3.7 %shard_map.115.kept_hbm = bf16[24,1152,1152]{2,1,0:T(8,128)(2,1)} custom-call(s32[4]{0:T(128)S(1)} %pad_add_fusion.place_ref, s32[32,4]{1,0:T(8,128)S(1)} %copy.12.list_ref, bf16[2,128,512]{2,1,0:T(8,128)(2,1)S(1)} %copy-done.5, bf16[2,128,512]{2,1,0:T(8,128)(2,1)S(1)} %collective-permute-done.1.refs_1_, ...), custom_call_target="tpu_custom_call" | custom-call | tf_op jit(solution)/shard_map/pallas_call | solution.py:411
  60.8 3.5 %collective-permute-start.4 = (bf16[4,384,256]{2,1,0:T(8,128)(2,1)S(1)}, bf16[4,384,256]{2,1,0:T(8,128)(2,1)S(1)}, u32[]{:S(2)}, u32[]{:S(2)}) collective-permute-start(bf16[4,384,256]{2,1,0:T(8,128)(2,1)S(1)} %slice.3), channel_id=1, source_target_pairs={{0,16},{16,0},{1,17},{17,1},{2,18},{18,2},{3,19},{19,3},{4,20},{20... | collective-permute-start | bytes 2359304 | tf_op jit(solution)/shard_map/ppermute | solution.py:364
  66.2 4.5 %shard_map.116 = (bf16[1024,1024]{1,0:T(8,128)(2,1)S(1)}, f32[4,2,128]{2,1,0:T(2,128)S(1)}, f32[1,256]{1,0:T(1,128)S(1)}) custom-call(bf16[24,1152,1152]{2,1,0:T(8,128)(2,1)} %shard_map.115.kept_hbm, bf16[4,784,256]{2,1,0:T(8,128)(2,1)S(1)} %all-to-all-done.1.near_ref, bf16[4,384,256]{2,1,0:T(8,128)(2,1)S(1)} %collective-permute-done.4.partner_ref), custom_call_target="tpu_custom_call" | custom-call | tf_op jit(solution)/shard_map/pallas_call | solution.py:425
  72.0 7.7 %all_to_all.51 = f32[4,2,128]{2,1,0:T(2,128)S(1)} all-to-all(f32[4,2,128]{2,1,0:T(2,128)S(1)} %get-tuple-element.27), channel_id=1, replica_groups=mesh['x'=4,'zh'=4,'c'=2,'zl'=4,'y'=4] {'zl'}, dimensions={0} | all-to-all | bytes 8192 | tf_op jit(solution)/shard_map/all_to_all | solution.py:368
  80.3 19.1 %all_to_all.52.x_ref = bf16[16,16,256]{2,1,0:T(8,128)(2,1)S(1)} all-to-all(bf16[16,16,256]{2,1,0:T(8,128)(2,1)S(1)} %get-tuple-element.30), channel_id=1, replica_groups=mesh['x'=4,'zh'=4,'c'=2,'zl'=4,'y'=4] {'zh','zl'}, dimensions={0} | all-to-all | bytes 262144 | tf_op jit(solution)/shard_map/all_to_all | solution.py:368
  99.8 20.1 %all_to_all.53.z_ref = bf16[32,16,256]{2,1,0:T(8,128)(2,1)S(1)} all-to-all(bf16[32,16,256]{2,1,0:T(8,128)(2,1)S(1)} %get-tuple-element.32), channel_id=1, replica_groups=mesh['x'=4,'zh'=4,'c'=2,'zl'=4,'y'=4] {'x','c','y'}, dimensions={0} | all-to-all | bytes 524288 | tf_op jit(solution)/shard_map/all_to_all | solution.py:368
  120.5 14.8 %all_to_all.54.x_ref = bf16[16,16,128]{2,1,0:T(8,128)(2,1)S(1)} all-to-all(bf16[16,16,128]{2,1,0:T(8,128)(2,1)S(1)} %get-tuple-element.37), channel_id=1, replica_groups=mesh['x'=4,'zh'=4,'c'=2,'zl'=4,'y'=4] {'zh','zl'}, dimensions={0} | all-to-all | bytes 131072 | tf_op jit(solution)/shard_map/all_to_all | solution.py:368
  135.6 13.1 %all_to_all.55.z_ref = bf16[32,16,128]{2,1,0:T(8,128)(2,1)S(1)} all-to-all(bf16[32,16,128]{2,1,0:T(8,128)(2,1)S(1)} %shard_map.120), channel_id=1, replica_groups=mesh['x'=4,'zh'=4,'c'=2,'zl'=4,'y'=4] {'x','c','y'}, dimensions={0} | all-to-all | bytes 262144 | tf_op jit(solution)/shard_map/all_to_all | solution.py:368
  149.9 6.8 %all_to_all.56.scaled_ref = f32[4,2,128]{2,1,0:T(2,128)S(1)} all-to-all(f32[4,2,128]{2,1,0:T(2,128)S(1)} %get-tuple-element.42), channel_id=1, replica_groups=mesh['x'=4,'zh'=4,'c'=2,'zl'=4,'y'=4] {'zl'}, dimensions={0} | all-to-all | bytes 8192 | tf_op jit(solution)/shard_map/all_to_all | solution.py:368
  156.6 3.7 %shard_map.123 = bf16[4,384,256]{2,1,0:T(8,128)(2,1)} custom-call(s32[4]{0:T(128)S(1)} %pad_add_fusion.place_ref, bf16[24,1152,1152]{2,1,0:T(8,128)(2,1)} %shard_map.115.kept_hbm, bf16[1024,1024]{1,0:T(8,128)(2,1)S(1)} %copy-done.1, f32[4,2,128]{2,1,0:T(2,128)S(1)} %all_to_all.56.scaled_ref), custom_call_target="tpu_custom_call" | custom-call | tf_op jit(solution)/shard_map/pallas_call | solution.py:483
  160.3 3.5 %all-to-all-start.9 = ((bf16[4,384,256]{2,1,0:T(8,128)(2,1)}), bf16[4,384,256]{2,1,0:T(8,128)(2,1)S(1)}, u32[]{:S(2)}, u32[]{:S(2)}) async-start(bf16[4,384,256]{2,1,0:T(8,128)(2,1)} %shard_map.123), calls=%async_computation.9 | async-start | bytes 1572864 | tf_op jit(solution)/shard_map/all_to_all | solution.py:368
  163.8 3.9 %shard_map.122 = bf16[8,384,256]{2,1,0:T(8,128)(2,1)S(1)} custom-call(s32[4]{0:T(128)S(1)} %pad_add_fusion.place_ref, bf16[24,1152,1152]{2,1,0:T(8,128)(2,1)} %shard_map.115.kept_hbm, bf16[1024,1024]{1,0:T(8,128)(2,1)S(1)} %copy-done.1, f32[4,2,128]{2,1,0:T(2,128)S(1)} %all_to_all.56.scaled_ref), custom_call_target="tpu_custom_call" | custom-call | tf_op jit(solution)/shard_map/pallas_call | solution.py:483
  168.9 5.3 %all-to-all-done.9 = bf16[4,384,256]{2,1,0:T(8,128)(2,1)S(1)} async-done(((bf16[4,384,256]{2,1,0:T(8,128)(2,1)}), bf16[4,384,256]{2,1,0:T(8,128)(2,1)S(1)}, u32[]{:S(2)}, u32[]{:S(2)}) %all-to-all-start.9) | async-done | bytes 786464 | tf_op jit(solution)/shard_map/all_to_all | solution.py:368
  174.1 6.4 %all-to-all-start.8 = ((bf16[8,384,256]{2,1,0:T(8,128)(2,1)}), bf16[8,384,256]{2,1,0:T(8,128)(2,1)S(1)}, u32[]{:S(2)}, u32[]{:S(2)}) async-start(bf16[8,384,256]{2,1,0:T(8,128)(2,1)} %copy-done.2), calls=%async_computation.8 | async-start | bytes 3145728 | tf_op jit(solution)/shard_map/all_to_all | solution.py:368
  180.7 2.8 %collective-permute-start.5 = (bf16[384,256]{1,0:T(8,128)(2,1)S(1)}, bf16[384,256]{1,0:T(8,128)(2,1)S(1)}, u32[]{:S(2)}, u32[]{:S(2)}) collective-permute-start(bf16[384,256]{1,0:T(8,128)(2,1)S(1)} %reduce_sum.32), channel_id=1, source_target_pairs={{16,32},{32,16},{48,64},{64,48},{80,96},{96,80},{112,128},{128,112... | collective-permute-start | bytes 589832 | tf_op jit(solution)/shard_map/ppermute | solution.py:360
  183.5 17.6 %all-to-all-done.8 = bf16[8,384,256]{2,1,0:T(8,128)(2,1)S(1)} async-done(((bf16[8,384,256]{2,1,0:T(8,128)(2,1)}), bf16[8,384,256]{2,1,0:T(8,128)(2,1)S(1)}, u32[]{:S(2)}, u32[]{:S(2)}) %all-to-all-start.8) | async-done | bytes 1572896 | tf_op jit(solution)/shard_map/all_to_all | solution.py:368
  (48 shorter events, 12.9 us)
Async XLA Ops:
  0.6 24.3 %collective-permute-start = (bf16[384,256]{1,0:T(8,128)(2,1)}, bf16[384,256]{1,0:T(8,128)(2,1)S(1)}, u32[]{:S(2)}, u32[]{:S(2)}) collective-permute-start(bf16[384,256]{1,0:T(8,128)(2,1)} %own_ref.1), channel_id=1, source_target_pairs={{16,32},{32,16},{48,64},{64,48},{80,96},{96,80},{112,128},{128,112... | collective-permute-start | bytes 589832 | tf_op jit(solution)/shard_map/ppermute | solution.py:360
  10.8 0.7 copy-start.7
  11.5 0.7 copy-start.12
  24.9 0.9 copy-start.6
  27.1 4.3 %copy-start.5 = (bf16[2,128,512]{2,1,0:T(8,128)(2,1)S(1)}, bf16[2,128,512]{2,1,0:T(8,128)(2,1)}, u32[]{:S(2)}) copy-start(bf16[2,128,512]{2,1,0:T(8,128)(2,1)} %refs_0_.1) | copy-start | bytes 786436
  27.1 14.5 %copy-start.13 = (s32[32,4]{0,1:T(4,128)S(1)}, s32[32,4]{0,1:T(4,128)}, u32[]{:S(2)}) copy-start(s32[32,4]{0,1:T(4,128)} %param.11) | copy-start | bytes 1540
  27.1 33.5 %all-to-all-start.1 = ((bf16[4,784,256]{2,1,0:T(8,128)(2,1)}), bf16[4,784,256]{2,1,0:T(8,128)(2,1)S(1)}, u32[]{:S(2)}, u32[]{:S(2)}) async-start(bf16[4,784,256]{2,1,0:T(8,128)(2,1)} %shard_map.114), calls=%async_computation.1 | async-start | bytes 3211264 | tf_op jit(solution)/shard_map/all_to_all | solution.py:368
  31.4 21.8 %collective-permute-start.2 = (bf16[2,128,512]{2,1,0:T(8,128)(2,1)S(1)}, bf16[2,128,512]{2,1,0:T(8,128)(2,1)S(1)}, u32[]{:S(2)}, u32[]{:S(2)}) collective-permute-start(bf16[2,128,512]{2,1,0:T(8,128)(2,1)S(1)} %copy-done.5), channel_id=1, source_target_pairs={{0,8},{4,12},{8,0},{12,4},{1,9},{5,13},{9,1},{13,5},{2,10},{6,14},... | collective-permute-start | bytes 786440 | tf_op jit(solution)/shard_map/ppermute | solution.py:352
  34.5 18.7 %collective-permute-start.1 = (bf16[2,128,512]{2,1,0:T(8,128)(2,1)S(1)}, bf16[2,128,512]{2,1,0:T(8,128)(2,1)S(1)}, u32[]{:S(2)}, u32[]{:S(2)}) collective-permute-start(bf16[2,128,512]{2,1,0:T(8,128)(2,1)S(1)} %copy-done.5), channel_id=1, source_target_pairs={{0,4},{4,8},{8,12},{12,0},{1,5},{5,9},{9,13},{13,1},{2,6},{6,10},{... | collective-permute-start | bytes 786440 | tf_op jit(solution)/shard_map/ppermute | solution.py:352
  37.2 19.7 %collective-permute-start.3 = (bf16[2,128,512]{2,1,0:T(8,128)(2,1)S(1)}, bf16[2,128,512]{2,1,0:T(8,128)(2,1)S(1)}, u32[]{:S(2)}, u32[]{:S(2)}) collective-permute-start(bf16[2,128,512]{2,1,0:T(8,128)(2,1)S(1)} %copy-done.5), channel_id=1, source_target_pairs={{0,12},{4,0},{8,4},{12,8},{1,13},{5,1},{9,5},{13,9},{2,14},{6,2},{... | collective-permute-start | bytes 786440 | tf_op jit(solution)/shard_map/ppermute | solution.py:352
  60.7 19.1 %copy-start.4 = (bf16[2,256,256]{2,1,0:T(8,128)(2,1)S(1)}, bf16[2,256,256]{2,1,0:T(8,128)(2,1)}, u32[]{:S(2)}) copy-start(bf16[2,256,256]{2,1,0:T(8,128)(2,1)} %weight_ref.3) | copy-start | bytes 786436
  60.7 19.1 %copy-start.8 = (f32[256]{0:T(256)S(1)}, f32[256]{0:T(256)}, u32[]{:S(2)}) copy-start(f32[256]{0:T(256)} %param.13) | copy-start | bytes 3076
  60.7 19.1 %copy-start.9 = (f32[256]{0:T(256)S(1)}, f32[256]{0:T(256)}, u32[]{:S(2)}) copy-start(f32[256]{0:T(256)} %param.15) | copy-start | bytes 3076
  60.7 19.0 %copy-start.10 = (f32[256]{0:T(256)S(1)}, f32[256]{0:T(256)}, u32[]{:S(2)}) copy-start(f32[256]{0:T(256)} %param.16) | copy-start | bytes 3076
  60.7 59.1 %copy-start.3 = (bf16[2,256,256]{2,1,0:T(8,128)(2,1)S(1)}, bf16[2,256,256]{2,1,0:T(8,128)(2,1)}, u32[]{:S(2)}) copy-start(bf16[2,256,256]{2,1,0:T(8,128)(2,1)} %atom_weight_ref.3) | copy-start | bytes 786436
  60.8 5.4 %collective-permute-start.4 = (bf16[4,384,256]{2,1,0:T(8,128)(2,1)S(1)}, bf16[4,384,256]{2,1,0:T(8,128)(2,1)S(1)}, u32[]{:S(2)}, u32[]{:S(2)}) collective-permute-start(bf16[4,384,256]{2,1,0:T(8,128)(2,1)S(1)} %slice.3), channel_id=1, source_target_pairs={{0,16},{16,0},{1,17},{17,1},{2,18},{18,2},{3,19},{19,3},{4,20},{20... | collective-permute-start | bytes 2359304 | tf_op jit(solution)/shard_map/ppermute | solution.py:364
  70.7 1.3 copy-start
  80.3 68.3 %copy-start.11 = (f32[256]{0:T(256)S(1)}, f32[256]{0:T(256)}, u32[]{:S(2)}) copy-start(f32[256]{0:T(256)} %param.19) | copy-start | bytes 3076
  119.9 36.8 %copy-start.1 = (bf16[1024,1024]{1,0:T(8,128)(2,1)S(1)}, bf16[1024,1024]{1,0:T(8,128)(2,1)}, u32[]{:S(2)}) copy-start(bf16[1024,1024]{1,0:T(8,128)(2,1)} %copy-done) | copy-start | bytes 6291460
  160.3 13.9 %all-to-all-start.9 = ((bf16[4,384,256]{2,1,0:T(8,128)(2,1)}), bf16[4,384,256]{2,1,0:T(8,128)(2,1)S(1)}, u32[]{:S(2)}, u32[]{:S(2)}) async-start(bf16[4,384,256]{2,1,0:T(8,128)(2,1)} %shard_map.123), calls=%async_computation.9 | async-start | bytes 1572864 | tf_op jit(solution)/shard_map/all_to_all | solution.py:368
  167.7 1.2 copy-start.2
  174.1 27.0 %all-to-all-start.8 = ((bf16[8,384,256]{2,1,0:T(8,128)(2,1)}), bf16[8,384,256]{2,1,0:T(8,128)(2,1)S(1)}, u32[]{:S(2)}, u32[]{:S(2)}) async-start(bf16[8,384,256]{2,1,0:T(8,128)(2,1)} %copy-done.2), calls=%async_computation.8 | async-start | bytes 3145728 | tf_op jit(solution)/shard_map/all_to_all | solution.py:368
  180.7 20.7 %collective-permute-start.5 = (bf16[384,256]{1,0:T(8,128)(2,1)S(1)}, bf16[384,256]{1,0:T(8,128)(2,1)S(1)}, u32[]{:S(2)}, u32[]{:S(2)}) collective-permute-start(bf16[384,256]{1,0:T(8,128)(2,1)S(1)} %reduce_sum.32), channel_id=1, source_target_pairs={{16,32},{32,16},{48,64},{64,48},{80,96},{96,80},{112,128},{128,112... | collective-permute-start | bytes 589832 | tf_op jit(solution)/shard_map/ppermute | solution.py:360

commit v6 on v5

--- a/solution.py
+++ b/solution.py
@@ -314,15 +314,18 @@
     place_ref, kept_hbm, psi_ref, scaled_ref, out_ref, weighted, flipped_ref, scratch, sem
 ):
     side, deep, width = out_ref.shape
-    copy = pltpu.make_async_copy(kept_hbm.at[0, 2 * deep :, : psi_ref.shape[0]], flipped_ref, sem)
+    copy = pltpu.make_async_copy(
+        kept_hbm.at[0, 2 * deep :, : psi_ref.shape[0]], flipped_ref, sem
+    )
     copy.start()
-    scaled_psi(psi_ref, scaled_ref, weighted, scratch)
+    scale = jnp.concatenate(
+        [scaled_ref[n // 2, n % 2 : n % 2 + 1, :] for n in range(2 * side)], axis=1
+    )
     copy.wait()
+    flipped = (flipped_ref[...].astype(F32) * scale).astype(BF16)
     for k in range(side):
         terms = jnp.dot(
-            flipped_ref[...],
-            weighted[:, k * width : (k + 1) * width],
-            preferred_element_type=F32,
+            flipped, psi_ref[:, k * width : (k + 1) * width], preferred_element_type=F32
         )
         out_ref[k] = terms.astype(BF16)
 

time: 203 us -> 203 us (level)
  no operation moved by 1% of the time
where the time goes in v6:
time: 203 us; the launch traced here: 202 us
  blocking collectives  93.7 us (46%)
  starting transfers between devices  40.9 us (20%)
  waiting for transfers between devices  39.9 us (20%)
  Pallas kernels  20.4 us (10%)
  local copies, waits for them, and re-layouts  4.96 us (2%)
    all_to_all x7, blocking collectives, exchange(): return lax.all_to_all(parts, axes, split_axis=0, concat_axis=0, tiled=True)  93.7 us
    all_to_all x3, waiting for transfers between devices, exchange(): return lax.all_to_all(parts, axes, split_axis=0, concat_axis=0, tiled=True)  22.9 us
    ppermute x3, waiting for transfers between devices, from_behind(): lax.ppermute(value, axis, [(i, (i + k) % SIDE) for i in range(SIDE)])  15.1 us
    all_to_all x3, starting transfers between devices, exchange(): return lax.all_to_all(parts, axes, split_axis=0, concat_axis=0, tiled=True)  14.2 us
    ppermute x2, starting transfers between devices, across(): return lax.ppermute(value, GRID, pairs)  13 us
    ppermute x3, starting transfers between devices, from_behind(): lax.ppermute(value, axis, [(i, (i + k) % SIDE) for i in range(SIDE)])  10.2 us
    pallas_call x2, Pallas kernels, fock_terms(): pl.pallas_call(kernel, out_shape=shape((devices, deep, width), BF16), in_...  7.5 us
    unnamed x29, local copies, waits for them, and re-layouts  4.89 us
  transfers between devices with their start and end apart: 9, of which 5 were waited for; matrix products, arithmetic and copies ran while one was open for 0% of the time, Pallas kernels for 4%

profile of v6, /device:TPU:1, one launch (start us, length us, event | category | flops | bytes accessed | tf_op | source)
XLA Modules:
  0.0 202.1 jit_solution(1231715050133260952)
XLA Ops:
  0.6 10.2 %collective-permute-start = (bf16[384,256]{1,0:T(8,128)(2,1)}, bf16[384,256]{1,0:T(8,128)(2,1)S(1)}, u32[]{:S(2)}, u32[]{:S(2)}) collective-permute-start(bf16[384,256]{1,0:T(8,128)(2,1)} %own_ref.1), channel_id=1, source_target_pairs={{16,32},{32,16},{48,64},{64,48},{80,96},{96,80},{112,128},{128,112... | collective-permute-start | bytes 589832 | tf_op jit(solution)/shard_map/ppermute | solution.py:363
  12.6 12.3 %all_to_all.50.windows_ref = bf16[8,16,128]{2,1,0:T(8,128)(2,1)S(1)} all-to-all(bf16[8,16,128]{2,1,0:T(8,128)(2,1)S(1)} %get-tuple-element.23), channel_id=1, replica_groups=mesh['x'=4,'zh'=4,'c'=2,'zl'=4,'y'=4] {'x','c'}, dimensions={0} | all-to-all | bytes 65536 | tf_op jit(solution)/shard_map/all_to_all | solution.py:371
  27.1 4.3 %all-to-all-start.1 = ((bf16[4,784,256]{2,1,0:T(8,128)(2,1)}), bf16[4,784,256]{2,1,0:T(8,128)(2,1)S(1)}, u32[]{:S(2)}, u32[]{:S(2)}) async-start(bf16[4,784,256]{2,1,0:T(8,128)(2,1)} %shard_map.114), calls=%async_computation.1 | async-start | bytes 3211264 | tf_op jit(solution)/shard_map/all_to_all | solution.py:371
  31.4 3.1 %collective-permute-start.2 = (bf16[2,128,512]{2,1,0:T(8,128)(2,1)S(1)}, bf16[2,128,512]{2,1,0:T(8,128)(2,1)S(1)}, u32[]{:S(2)}, u32[]{:S(2)}) collective-permute-start(bf16[2,128,512]{2,1,0:T(8,128)(2,1)S(1)} %copy-done.5), channel_id=1, source_target_pairs={{0,8},{4,12},{8,0},{12,4},{1,9},{5,13},{9,1},{13,5},{2,10},{6,14},... | collective-permute-start | bytes 786440 | tf_op jit(solution)/shard_map/ppermute | solution.py:355
  34.5 2.7 %collective-permute-start.1 = (bf16[2,128,512]{2,1,0:T(8,128)(2,1)S(1)}, bf16[2,128,512]{2,1,0:T(8,128)(2,1)S(1)}, u32[]{:S(2)}, u32[]{:S(2)}) collective-permute-start(bf16[2,128,512]{2,1,0:T(8,128)(2,1)S(1)} %copy-done.5), channel_id=1, source_target_pairs={{0,4},{4,8},{8,12},{12,0},{1,5},{5,9},{9,13},{13,1},{2,6},{6,10},{... | collective-permute-start | bytes 786440 | tf_op jit(solution)/shard_map/ppermute | solution.py:355
  37.2 4.4 %collective-permute-start.3 = (bf16[2,128,512]{2,1,0:T(8,128)(2,1)S(1)}, bf16[2,128,512]{2,1,0:T(8,128)(2,1)S(1)}, u32[]{:S(2)}, u32[]{:S(2)}) collective-permute-start(bf16[2,128,512]{2,1,0:T(8,128)(2,1)S(1)} %copy-done.5), channel_id=1, source_target_pairs={{0,12},{4,0},{8,4},{12,8},{1,13},{5,1},{9,5},{13,9},{2,14},{6,2},{... | collective-permute-start | bytes 786440 | tf_op jit(solution)/shard_map/ppermute | solution.py:355
  41.8 11.4 %collective-permute-done.2.refs_2_ = bf16[2,128,512]{2,1,0:T(8,128)(2,1)S(1)} collective-permute-done((bf16[2,128,512]{2,1,0:T(8,128)(2,1)S(1)}, bf16[2,128,512]{2,1,0:T(8,128)(2,1)S(1)}, u32[]{:S(2)}, u32[]{:S(2)}) %collective-permute-start.2) | collective-permute-done | bytes 262176 | tf_op jit(solution)/shard_map/ppermute | solution.py:355
  53.2 3.7 %collective-permute-done.3.refs_3_ = bf16[2,128,512]{2,1,0:T(8,128)(2,1)S(1)} collective-permute-done((bf16[2,128,512]{2,1,0:T(8,128)(2,1)S(1)}, bf16[2,128,512]{2,1,0:T(8,128)(2,1)S(1)}, u32[]{:S(2)}, u32[]{:S(2)}) %collective-permute-start.3) | collective-permute-done | bytes 262176 | tf_op jit(solution)/shard_map/ppermute | solution.py:355
  56.9 3.7 %shard_map.115.kept_hbm = bf16[24,1152,1152]{2,1,0:T(8,128)(2,1)} custom-call(s32[4]{0:T(128)S(1)} %pad_add_fusion.place_ref, s32[32,4]{1,0:T(8,128)S(1)} %copy.12.list_ref, bf16[2,128,512]{2,1,0:T(8,128)(2,1)S(1)} %copy-done.5, bf16[2,128,512]{2,1,0:T(8,128)(2,1)S(1)} %collective-permute-done.1.refs_1_, ...), custom_call_target="tpu_custom_call" | custom-call | tf_op jit(solution)/shard_map/pallas_call | solution.py:414
  60.8 3.5 %collective-permute-start.4 = (bf16[4,384,256]{2,1,0:T(8,128)(2,1)S(1)}, bf16[4,384,256]{2,1,0:T(8,128)(2,1)S(1)}, u32[]{:S(2)}, u32[]{:S(2)}) collective-permute-start(bf16[4,384,256]{2,1,0:T(8,128)(2,1)S(1)} %slice.3), channel_id=1, source_target_pairs={{0,16},{16,0},{1,17},{17,1},{2,18},{18,2},{3,19},{19,3},{4,20},{20... | collective-permute-start | bytes 2359304 | tf_op jit(solution)/shard_map/ppermute | solution.py:367
  66.2 4.5 %shard_map.116 = (bf16[1024,1024]{1,0:T(8,128)(2,1)S(1)}, f32[4,2,128]{2,1,0:T(2,128)S(1)}, f32[1,256]{1,0:T(1,128)S(1)}) custom-call(bf16[24,1152,1152]{2,1,0:T(8,128)(2,1)} %shard_map.115.kept_hbm, bf16[4,784,256]{2,1,0:T(8,128)(2,1)S(1)} %all-to-all-done.1.near_ref, bf16[4,384,256]{2,1,0:T(8,128)(2,1)S(1)} %collective-permute-done.4.partner_ref), custom_call_target="tpu_custom_call" | custom-call | tf_op jit(solution)/shard_map/pallas_call | solution.py:428
  72.0 7.7 %all_to_all.51 = f32[4,2,128]{2,1,0:T(2,128)S(1)} all-to-all(f32[4,2,128]{2,1,0:T(2,128)S(1)} %get-tuple-element.27), channel_id=1, replica_groups=mesh['x'=4,'zh'=4,'c'=2,'zl'=4,'y'=4] {'zl'}, dimensions={0} | all-to-all | bytes 8192 | tf_op jit(solution)/shard_map/all_to_all | solution.py:371
  80.3 19.1 %all_to_all.52.x_ref = bf16[16,16,256]{2,1,0:T(8,128)(2,1)S(1)} all-to-all(bf16[16,16,256]{2,1,0:T(8,128)(2,1)S(1)} %get-tuple-element.30), channel_id=1, replica_groups=mesh['x'=4,'zh'=4,'c'=2,'zl'=4,'y'=4] {'zh','zl'}, dimensions={0} | all-to-all | bytes 262144 | tf_op jit(solution)/shard_map/all_to_all | solution.py:371
  99.8 20.1 %all_to_all.53.z_ref = bf16[32,16,256]{2,1,0:T(8,128)(2,1)S(1)} all-to-all(bf16[32,16,256]{2,1,0:T(8,128)(2,1)S(1)} %get-tuple-element.32), channel_id=1, replica_groups=mesh['x'=4,'zh'=4,'c'=2,'zl'=4,'y'=4] {'x','c','y'}, dimensions={0} | all-to-all | bytes 524288 | tf_op jit(solution)/shard_map/all_to_all | solution.py:371
  120.5 14.8 %all_to_all.54.x_ref = bf16[16,16,128]{2,1,0:T(8,128)(2,1)S(1)} all-to-all(bf16[16,16,128]{2,1,0:T(8,128)(2,1)S(1)} %get-tuple-element.37), channel_id=1, replica_groups=mesh['x'=4,'zh'=4,'c'=2,'zl'=4,'y'=4] {'zh','zl'}, dimensions={0} | all-to-all | bytes 131072 | tf_op jit(solution)/shard_map/all_to_all | solution.py:371
  135.6 13.1 %all_to_all.55.z_ref = bf16[32,16,128]{2,1,0:T(8,128)(2,1)S(1)} all-to-all(bf16[32,16,128]{2,1,0:T(8,128)(2,1)S(1)} %shard_map.120), channel_id=1, replica_groups=mesh['x'=4,'zh'=4,'c'=2,'zl'=4,'y'=4] {'x','c','y'}, dimensions={0} | all-to-all | bytes 262144 | tf_op jit(solution)/shard_map/all_to_all | solution.py:371
  149.9 6.8 %all_to_all.56.scaled_ref = f32[4,2,128]{2,1,0:T(2,128)S(1)} all-to-all(f32[4,2,128]{2,1,0:T(2,128)S(1)} %get-tuple-element.42), channel_id=1, replica_groups=mesh['x'=4,'zh'=4,'c'=2,'zl'=4,'y'=4] {'zl'}, dimensions={0} | all-to-all | bytes 8192 | tf_op jit(solution)/shard_map/all_to_all | solution.py:371
  156.6 3.6 %shard_map.123 = bf16[4,384,256]{2,1,0:T(8,128)(2,1)} custom-call(s32[4]{0:T(128)S(1)} %pad_add_fusion.place_ref, bf16[24,1152,1152]{2,1,0:T(8,128)(2,1)} %shard_map.115.kept_hbm, bf16[1024,1024]{1,0:T(8,128)(2,1)S(1)} %copy-done.1, f32[4,2,128]{2,1,0:T(2,128)S(1)} %all_to_all.56.scaled_ref), custom_call_target="tpu_custom_call" | custom-call | tf_op jit(solution)/shard_map/pallas_call | solution.py:486
  160.2 3.5 %all-to-all-start.9 = ((bf16[4,384,256]{2,1,0:T(8,128)(2,1)}), bf16[4,384,256]{2,1,0:T(8,128)(2,1)S(1)}, u32[]{:S(2)}, u32[]{:S(2)}) async-start(bf16[4,384,256]{2,1,0:T(8,128)(2,1)} %shard_map.123), calls=%async_computation.9 | async-start | bytes 1572864 | tf_op jit(solution)/shard_map/all_to_all | solution.py:371
  163.7 3.9 %shard_map.122 = bf16[8,384,256]{2,1,0:T(8,128)(2,1)S(1)} custom-call(s32[4]{0:T(128)S(1)} %pad_add_fusion.place_ref, bf16[24,1152,1152]{2,1,0:T(8,128)(2,1)} %shard_map.115.kept_hbm, bf16[1024,1024]{1,0:T(8,128)(2,1)S(1)} %copy-done.1, f32[4,2,128]{2,1,0:T(2,128)S(1)} %all_to_all.56.scaled_ref), custom_call_target="tpu_custom_call" | custom-call | tf_op jit(solution)/shard_map/pallas_call | solution.py:486
  168.8 5.3 %all-to-all-done.9 = bf16[4,384,256]{2,1,0:T(8,128)(2,1)S(1)} async-done(((bf16[4,384,256]{2,1,0:T(8,128)(2,1)}), bf16[4,384,256]{2,1,0:T(8,128)(2,1)S(1)}, u32[]{:S(2)}, u32[]{:S(2)}) %all-to-all-start.9) | async-done | bytes 786464 | tf_op jit(solution)/shard_map/all_to_all | solution.py:371
  174.1 6.4 %all-to-all-start.8 = ((bf16[8,384,256]{2,1,0:T(8,128)(2,1)}), bf16[8,384,256]{2,1,0:T(8,128)(2,1)S(1)}, u32[]{:S(2)}, u32[]{:S(2)}) async-start(bf16[8,384,256]{2,1,0:T(8,128)(2,1)} %copy-done.2), calls=%async_computation.8 | async-start | bytes 3145728 | tf_op jit(solution)/shard_map/all_to_all | solution.py:371
  180.6 2.8 %collective-permute-start.5 = (bf16[384,256]{1,0:T(8,128)(2,1)S(1)}, bf16[384,256]{1,0:T(8,128)(2,1)S(1)}, u32[]{:S(2)}, u32[]{:S(2)}) collective-permute-start(bf16[384,256]{1,0:T(8,128)(2,1)S(1)} %reduce_sum.32), channel_id=1, source_target_pairs={{16,32},{32,16},{48,64},{64,48},{80,96},{96,80},{112,128},{128,112... | collective-permute-start | bytes 589832 | tf_op jit(solution)/shard_map/ppermute | solution.py:363
  183.4 17.6 %all-to-all-done.8 = bf16[8,384,256]{2,1,0:T(8,128)(2,1)S(1)} async-done(((bf16[8,384,256]{2,1,0:T(8,128)(2,1)}), bf16[8,384,256]{2,1,0:T(8,128)(2,1)S(1)}, u32[]{:S(2)}, u32[]{:S(2)}) %all-to-all-start.8) | async-done | bytes 1572896 | tf_op jit(solution)/shard_map/all_to_all | solution.py:371
  (48 shorter events, 12.8 us)
Async XLA Ops:
  0.6 24.3 %collective-permute-start = (bf16[384,256]{1,0:T(8,128)(2,1)}, bf16[384,256]{1,0:T(8,128)(2,1)S(1)}, u32[]{:S(2)}, u32[]{:S(2)}) collective-permute-start(bf16[384,256]{1,0:T(8,128)(2,1)} %own_ref.1), channel_id=1, source_target_pairs={{16,32},{32,16},{48,64},{64,48},{80,96},{96,80},{112,128},{128,112... | collective-permute-start | bytes 589832 | tf_op jit(solution)/shard_map/ppermute | solution.py:363
  10.8 0.7 copy-start.7
  11.5 0.7 copy-start.12
  24.9 0.9 copy-start.6
  27.1 4.3 %copy-start.5 = (bf16[2,128,512]{2,1,0:T(8,128)(2,1)S(1)}, bf16[2,128,512]{2,1,0:T(8,128)(2,1)}, u32[]{:S(2)}) copy-start(bf16[2,128,512]{2,1,0:T(8,128)(2,1)} %refs_0_.1) | copy-start | bytes 786436
  27.1 14.5 %copy-start.13 = (s32[32,4]{0,1:T(4,128)S(1)}, s32[32,4]{0,1:T(4,128)}, u32[]{:S(2)}) copy-start(s32[32,4]{0,1:T(4,128)} %param.11) | copy-start | bytes 1540
  27.1 33.5 %all-to-all-start.1 = ((bf16[4,784,256]{2,1,0:T(8,128)(2,1)}), bf16[4,784,256]{2,1,0:T(8,128)(2,1)S(1)}, u32[]{:S(2)}, u32[]{:S(2)}) async-start(bf16[4,784,256]{2,1,0:T(8,128)(2,1)} %shard_map.114), calls=%async_computation.1 | async-start | bytes 3211264 | tf_op jit(solution)/shard_map/all_to_all | solution.py:371
  31.4 21.8 %collective-permute-start.2 = (bf16[2,128,512]{2,1,0:T(8,128)(2,1)S(1)}, bf16[2,128,512]{2,1,0:T(8,128)(2,1)S(1)}, u32[]{:S(2)}, u32[]{:S(2)}) collective-permute-start(bf16[2,128,512]{2,1,0:T(8,128)(2,1)S(1)} %copy-done.5), channel_id=1, source_target_pairs={{0,8},{4,12},{8,0},{12,4},{1,9},{5,13},{9,1},{13,5},{2,10},{6,14},... | collective-permute-start | bytes 786440 | tf_op jit(solution)/shard_map/ppermute | solution.py:355
  34.5 18.7 %collective-permute-start.1 = (bf16[2,128,512]{2,1,0:T(8,128)(2,1)S(1)}, bf16[2,128,512]{2,1,0:T(8,128)(2,1)S(1)}, u32[]{:S(2)}, u32[]{:S(2)}) collective-permute-start(bf16[2,128,512]{2,1,0:T(8,128)(2,1)S(1)} %copy-done.5), channel_id=1, source_target_pairs={{0,4},{4,8},{8,12},{12,0},{1,5},{5,9},{9,13},{13,1},{2,6},{6,10},{... | collective-permute-start | bytes 786440 | tf_op jit(solution)/shard_map/ppermute | solution.py:355
  37.2 19.7 %collective-permute-start.3 = (bf16[2,128,512]{2,1,0:T(8,128)(2,1)S(1)}, bf16[2,128,512]{2,1,0:T(8,128)(2,1)S(1)}, u32[]{:S(2)}, u32[]{:S(2)}) collective-permute-start(bf16[2,128,512]{2,1,0:T(8,128)(2,1)S(1)} %copy-done.5), channel_id=1, source_target_pairs={{0,12},{4,0},{8,4},{12,8},{1,13},{5,1},{9,5},{13,9},{2,14},{6,2},{... | collective-permute-start | bytes 786440 | tf_op jit(solution)/shard_map/ppermute | solution.py:355
  60.7 19.1 %copy-start.4 = (bf16[2,256,256]{2,1,0:T(8,128)(2,1)S(1)}, bf16[2,256,256]{2,1,0:T(8,128)(2,1)}, u32[]{:S(2)}) copy-start(bf16[2,256,256]{2,1,0:T(8,128)(2,1)} %weight_ref.3) | copy-start | bytes 786436
  60.7 19.1 %copy-start.8 = (f32[256]{0:T(256)S(1)}, f32[256]{0:T(256)}, u32[]{:S(2)}) copy-start(f32[256]{0:T(256)} %param.13) | copy-start | bytes 3076
  60.7 19.0 %copy-start.9 = (f32[256]{0:T(256)S(1)}, f32[256]{0:T(256)}, u32[]{:S(2)}) copy-start(f32[256]{0:T(256)} %param.15) | copy-start | bytes 3076
  60.7 19.0 %copy-start.10 = (f32[256]{0:T(256)S(1)}, f32[256]{0:T(256)}, u32[]{:S(2)}) copy-start(f32[256]{0:T(256)} %param.16) | copy-start | bytes 3076
  60.7 59.1 %copy-start.3 = (bf16[2,256,256]{2,1,0:T(8,128)(2,1)S(1)}, bf16[2,256,256]{2,1,0:T(8,128)(2,1)}, u32[]{:S(2)}) copy-start(bf16[2,256,256]{2,1,0:T(8,128)(2,1)} %atom_weight_ref.3) | copy-start | bytes 786436
  60.8 5.4 %collective-permute-start.4 = (bf16[4,384,256]{2,1,0:T(8,128)(2,1)S(1)}, bf16[4,384,256]{2,1,0:T(8,128)(2,1)S(1)}, u32[]{:S(2)}, u32[]{:S(2)}) collective-permute-start(bf16[4,384,256]{2,1,0:T(8,128)(2,1)S(1)} %slice.3), channel_id=1, source_target_pairs={{0,16},{16,0},{1,17},{17,1},{2,18},{18,2},{3,19},{19,3},{4,20},{20... | collective-permute-start | bytes 2359304 | tf_op jit(solution)/shard_map/ppermute | solution.py:367
  70.7 1.3 copy-start
  80.3 68.3 %copy-start.11 = (f32[256]{0:T(256)S(1)}, f32[256]{0:T(256)}, u32[]{:S(2)}) copy-start(f32[256]{0:T(256)} %param.19) | copy-start | bytes 3076
  119.9 36.7 %copy-start.1 = (bf16[1024,1024]{1,0:T(8,128)(2,1)S(1)}, bf16[1024,1024]{1,0:T(8,128)(2,1)}, u32[]{:S(2)}) copy-start(bf16[1024,1024]{1,0:T(8,128)(2,1)} %copy-done) | copy-start | bytes 6291460
  160.2 13.9 %all-to-all-start.9 = ((bf16[4,384,256]{2,1,0:T(8,128)(2,1)}), bf16[4,384,256]{2,1,0:T(8,128)(2,1)S(1)}, u32[]{:S(2)}, u32[]{:S(2)}) async-start(bf16[4,384,256]{2,1,0:T(8,128)(2,1)} %shard_map.123), calls=%async_computation.9 | async-start | bytes 1572864 | tf_op jit(solution)/shard_map/all_to_all | solution.py:371
  167.7 1.2 copy-start.2
  174.1 27.0 %all-to-all-start.8 = ((bf16[8,384,256]{2,1,0:T(8,128)(2,1)}), bf16[8,384,256]{2,1,0:T(8,128)(2,1)S(1)}, u32[]{:S(2)}, u32[]{:S(2)}) async-start(bf16[8,384,256]{2,1,0:T(8,128)(2,1)} %copy-done.2), calls=%async_computation.8 | async-start | bytes 3145728 | tf_op jit(solution)/shard_map/all_to_all | solution.py:371
  180.6 20.7 %collective-permute-start.5 = (bf16[384,256]{1,0:T(8,128)(2,1)S(1)}, bf16[384,256]{1,0:T(8,128)(2,1)S(1)}, u32[]{:S(2)}, u32[]{:S(2)}) collective-permute-start(bf16[384,256]{1,0:T(8,128)(2,1)S(1)} %reduce_sum.32), channel_id=1, source_target_pairs={{16,32},{32,16},{48,64},{64,48},{80,96},{96,80},{112,128},{128,112... | collective-permute-start | bytes 589832 | tf_op jit(solution)/shard_map/ppermute | solution.py:363

commit v7 on v6

--- a/solution.py
+++ b/solution.py
@@ -99,6 +99,7 @@
     flipped_ref[...] = jnp.zeros_like(flipped_ref)
     count, deep = dense_ref.shape
     owned = deep // BLK // 3
+    copies = []
     for k, part in enumerate(parts):
         origin = lax.rem(zl - k + side, side)
         for r in range(per):
@@ -114,12 +115,13 @@
                 tile = part[r, :, j * BLK : (j + 1) * BLK]
                 dense_ref[pl.ds(row, BLK), pl.ds(col, BLK)] = tile
                 flipped_ref[pl.ds(col, BLK), pl.ds(row, BLK)] = tile.T
-    copies = [
-        pltpu.make_async_copy(dense_ref, kept_hbm.at[1, :count], sems.at[1]),
-        pltpu.make_async_copy(flipped_ref, kept_hbm.at[0, :, :count], sems.at[0]),
-    ]
-    for copy in copies:
-        copy.start()
+        rows = pl.ds(pl.multiple_of(origin * per * BLK, per * BLK), per * BLK)
+        copies.append(
+            pltpu.make_async_copy(dense_ref.at[rows], kept_hbm.at[1, rows], sems.at[1 + k])
+        )
+        copies[k].start()
+    copies.append(pltpu.make_async_copy(flipped_ref, kept_hbm.at[0, :, :count], sems.at[0]))
+    copies[side].start()
     for copy in copies:
         copy.wait()
 
@@ -419,7 +421,7 @@
         scratch_shapes=[
             pltpu.VMEM((total_points, 3 * deep), BF16),
             pltpu.VMEM((3 * deep, total_points), BF16),
-            pltpu.SemaphoreType.DMA((2,)),
+            pltpu.SemaphoreType.DMA((SIDE + 1,)),
         ],
         compiler_params=pltpu.CompilerParams(vmem_limit_bytes=VMEM),
     )(place, block_lists, *from_behind(basis_values, "zl"))

time: 203 us -> 203 us (level)
  no operation moved by 1% of the time
where the time goes in v7:
time: 203 us; the launch traced here: 202 us
  blocking collectives  93.7 us (46%)
  starting transfers between devices  40.9 us (20%)
  waiting for transfers between devices  39.9 us (20%)
  Pallas kernels  20.4 us (10%)
  local copies, waits for them, and re-layouts  4.96 us (2%)
    all_to_all x7, blocking collectives, exchange(): return lax.all_to_all(parts, axes, split_axis=0, concat_axis=0, tiled=True)  93.7 us
    all_to_all x3, waiting for transfers between devices, exchange(): return lax.all_to_all(parts, axes, split_axis=0, concat_axis=0, tiled=True)  22.9 us
    ppermute x3, waiting for transfers between devices, from_behind(): lax.ppermute(value, axis, [(i, (i + k) % SIDE) for i in range(SIDE)])  15.1 us
    all_to_all x3, starting transfers between devices, exchange(): return lax.all_to_all(parts, axes, split_axis=0, concat_axis=0, tiled=True)  14.2 us
    ppermute x2, starting transfers between devices, across(): return lax.ppermute(value, GRID, pairs)  13 us
    ppermute x3, starting transfers between devices, from_behind(): lax.ppermute(value, axis, [(i, (i + k) % SIDE) for i in range(SIDE)])  10.2 us
    pallas_call x2, Pallas kernels, fock_terms(): pl.pallas_call(kernel, out_shape=shape((devices, deep, width), BF16), in_...  7.5 us
    unnamed x29, local copies, waits for them, and re-layouts  4.89 us
  transfers between devices with their start and end apart: 9, of which 5 were waited for; matrix products, arithmetic and copies ran while one was open for 0% of the time, Pallas kernels for 4%

profile of v7, /device:TPU:1, one launch (start us, length us, event | category | flops | bytes accessed | tf_op | source)
XLA Modules:
  0.0 202.0 jit_solution(7573810342693230889)
XLA Ops:
  0.6 10.2 %collective-permute-start = (bf16[384,256]{1,0:T(8,128)(2,1)}, bf16[384,256]{1,0:T(8,128)(2,1)S(1)}, u32[]{:S(2)}, u32[]{:S(2)}) collective-permute-start(bf16[384,256]{1,0:T(8,128)(2,1)} %own_ref.1), channel_id=1, source_target_pairs={{16,32},{32,16},{48,64},{64,48},{80,96},{96,80},{112,128},{128,112... | collective-permute-start | bytes 589832 | tf_op jit(solution)/shard_map/ppermute | solution.py:365
  12.6 12.3 %all_to_all.50.windows_ref = bf16[8,16,128]{2,1,0:T(8,128)(2,1)S(1)} all-to-all(bf16[8,16,128]{2,1,0:T(8,128)(2,1)S(1)} %get-tuple-element.23), channel_id=1, replica_groups=mesh['x'=4,'zh'=4,'c'=2,'zl'=4,'y'=4] {'x','c'}, dimensions={0} | all-to-all | bytes 65536 | tf_op jit(solution)/shard_map/all_to_all | solution.py:373
  27.1 4.3 %all-to-all-start.1 = ((bf16[4,784,256]{2,1,0:T(8,128)(2,1)}), bf16[4,784,256]{2,1,0:T(8,128)(2,1)S(1)}, u32[]{:S(2)}, u32[]{:S(2)}) async-start(bf16[4,784,256]{2,1,0:T(8,128)(2,1)} %shard_map.114), calls=%async_computation.1 | async-start | bytes 3211264 | tf_op jit(solution)/shard_map/all_to_all | solution.py:373
  31.4 3.1 %collective-permute-start.2 = (bf16[2,128,512]{2,1,0:T(8,128)(2,1)S(1)}, bf16[2,128,512]{2,1,0:T(8,128)(2,1)S(1)}, u32[]{:S(2)}, u32[]{:S(2)}) collective-permute-start(bf16[2,128,512]{2,1,0:T(8,128)(2,1)S(1)} %copy-done.5), channel_id=1, source_target_pairs={{0,8},{4,12},{8,0},{12,4},{1,9},{5,13},{9,1},{13,5},{2,10},{6,14},... | collective-permute-start | bytes 786440 | tf_op jit(solution)/shard_map/ppermute | solution.py:357
  34.5 2.7 %collective-permute-start.1 = (bf16[2,128,512]{2,1,0:T(8,128)(2,1)S(1)}, bf16[2,128,512]{2,1,0:T(8,128)(2,1)S(1)}, u32[]{:S(2)}, u32[]{:S(2)}) collective-permute-start(bf16[2,128,512]{2,1,0:T(8,128)(2,1)S(1)} %copy-done.5), channel_id=1, source_target_pairs={{0,4},{4,8},{8,12},{12,0},{1,5},{5,9},{9,13},{13,1},{2,6},{6,10},{... | collective-permute-start | bytes 786440 | tf_op jit(solution)/shard_map/ppermute | solution.py:357
  37.2 4.4 %collective-permute-start.3 = (bf16[2,128,512]{2,1,0:T(8,128)(2,1)S(1)}, bf16[2,128,512]{2,1,0:T(8,128)(2,1)S(1)}, u32[]{:S(2)}, u32[]{:S(2)}) collective-permute-start(bf16[2,128,512]{2,1,0:T(8,128)(2,1)S(1)} %copy-done.5), channel_id=1, source_target_pairs={{0,12},{4,0},{8,4},{12,8},{1,13},{5,1},{9,5},{13,9},{2,14},{6,2},{... | collective-permute-start | bytes 786440 | tf_op jit(solution)/shard_map/ppermute | solution.py:357
  41.8 11.4 %collective-permute-done.2.refs_2_ = bf16[2,128,512]{2,1,0:T(8,128)(2,1)S(1)} collective-permute-done((bf16[2,128,512]{2,1,0:T(8,128)(2,1)S(1)}, bf16[2,128,512]{2,1,0:T(8,128)(2,1)S(1)}, u32[]{:S(2)}, u32[]{:S(2)}) %collective-permute-start.2) | collective-permute-done | bytes 262176 | tf_op jit(solution)/shard_map/ppermute | solution.py:357
  53.2 3.7 %collective-permute-done.3.refs_3_ = bf16[2,128,512]{2,1,0:T(8,128)(2,1)S(1)} collective-permute-done((bf16[2,128,512]{2,1,0:T(8,128)(2,1)S(1)}, bf16[2,128,512]{2,1,0:T(8,128)(2,1)S(1)}, u32[]{:S(2)}, u32[]{:S(2)}) %collective-permute-start.3) | collective-permute-done | bytes 262176 | tf_op jit(solution)/shard_map/ppermute | solution.py:357
  56.9 3.6 %shard_map.115.kept_hbm = bf16[24,1152,1152]{2,1,0:T(8,128)(2,1)} custom-call(s32[4]{0:T(128)S(1)} %pad_add_fusion.place_ref, s32[32,4]{1,0:T(8,128)S(1)} %copy.12.list_ref, bf16[2,128,512]{2,1,0:T(8,128)(2,1)S(1)} %copy-done.5, bf16[2,128,512]{2,1,0:T(8,128)(2,1)S(1)} %collective-permute-done.1.refs_1_, ...), custom_call_target="tpu_custom_call" | custom-call | tf_op jit(solution)/shard_map/pallas_call | solution.py:416
  60.7 3.5 %collective-permute-start.4 = (bf16[4,384,256]{2,1,0:T(8,128)(2,1)S(1)}, bf16[4,384,256]{2,1,0:T(8,128)(2,1)S(1)}, u32[]{:S(2)}, u32[]{:S(2)}) collective-permute-start(bf16[4,384,256]{2,1,0:T(8,128)(2,1)S(1)} %slice.3), channel_id=1, source_target_pairs={{0,16},{16,0},{1,17},{17,1},{2,18},{18,2},{3,19},{19,3},{4,20},{20... | collective-permute-start | bytes 2359304 | tf_op jit(solution)/shard_map/ppermute | solution.py:369
  66.1 4.5 %shard_map.116 = (bf16[1024,1024]{1,0:T(8,128)(2,1)S(1)}, f32[4,2,128]{2,1,0:T(2,128)S(1)}, f32[1,256]{1,0:T(1,128)S(1)}) custom-call(bf16[24,1152,1152]{2,1,0:T(8,128)(2,1)} %shard_map.115.kept_hbm, bf16[4,784,256]{2,1,0:T(8,128)(2,1)S(1)} %all-to-all-done.1.near_ref, bf16[4,384,256]{2,1,0:T(8,128)(2,1)S(1)} %collective-permute-done.4.partner_ref), custom_call_target="tpu_custom_call" | custom-call | tf_op jit(solution)/shard_map/pallas_call | solution.py:430
  72.0 7.7 %all_to_all.51 = f32[4,2,128]{2,1,0:T(2,128)S(1)} all-to-all(f32[4,2,128]{2,1,0:T(2,128)S(1)} %get-tuple-element.27), channel_id=1, replica_groups=mesh['x'=4,'zh'=4,'c'=2,'zl'=4,'y'=4] {'zl'}, dimensions={0} | all-to-all | bytes 8192 | tf_op jit(solution)/shard_map/all_to_all | solution.py:373
  80.3 19.1 %all_to_all.52.x_ref = bf16[16,16,256]{2,1,0:T(8,128)(2,1)S(1)} all-to-all(bf16[16,16,256]{2,1,0:T(8,128)(2,1)S(1)} %get-tuple-element.30), channel_id=1, replica_groups=mesh['x'=4,'zh'=4,'c'=2,'zl'=4,'y'=4] {'zh','zl'}, dimensions={0} | all-to-all | bytes 262144 | tf_op jit(solution)/shard_map/all_to_all | solution.py:373
  99.8 20.1 %all_to_all.53.z_ref = bf16[32,16,256]{2,1,0:T(8,128)(2,1)S(1)} all-to-all(bf16[32,16,256]{2,1,0:T(8,128)(2,1)S(1)} %get-tuple-element.32), channel_id=1, replica_groups=mesh['x'=4,'zh'=4,'c'=2,'zl'=4,'y'=4] {'x','c','y'}, dimensions={0} | all-to-all | bytes 524288 | tf_op jit(solution)/shard_map/all_to_all | solution.py:373
  120.5 14.8 %all_to_all.54.x_ref = bf16[16,16,128]{2,1,0:T(8,128)(2,1)S(1)} all-to-all(bf16[16,16,128]{2,1,0:T(8,128)(2,1)S(1)} %get-tuple-element.37), channel_id=1, replica_groups=mesh['x'=4,'zh'=4,'c'=2,'zl'=4,'y'=4] {'zh','zl'}, dimensions={0} | all-to-all | bytes 131072 | tf_op jit(solution)/shard_map/all_to_all | solution.py:373
  135.5 13.1 %all_to_all.55.z_ref = bf16[32,16,128]{2,1,0:T(8,128)(2,1)S(1)} all-to-all(bf16[32,16,128]{2,1,0:T(8,128)(2,1)S(1)} %shard_map.120), channel_id=1, replica_groups=mesh['x'=4,'zh'=4,'c'=2,'zl'=4,'y'=4] {'x','c','y'}, dimensions={0} | all-to-all | bytes 262144 | tf_op jit(solution)/shard_map/all_to_all | solution.py:373
  149.8 6.8 %all_to_all.56.scaled_ref = f32[4,2,128]{2,1,0:T(2,128)S(1)} all-to-all(f32[4,2,128]{2,1,0:T(2,128)S(1)} %get-tuple-element.42), channel_id=1, replica_groups=mesh['x'=4,'zh'=4,'c'=2,'zl'=4,'y'=4] {'zl'}, dimensions={0} | all-to-all | bytes 8192 | tf_op jit(solution)/shard_map/all_to_all | solution.py:373
  156.6 3.6 %shard_map.123 = bf16[4,384,256]{2,1,0:T(8,128)(2,1)} custom-call(s32[4]{0:T(128)S(1)} %pad_add_fusion.place_ref, bf16[24,1152,1152]{2,1,0:T(8,128)(2,1)} %shard_map.115.kept_hbm, bf16[1024,1024]{1,0:T(8,128)(2,1)S(1)} %copy-done.1, f32[4,2,128]{2,1,0:T(2,128)S(1)} %all_to_all.56.scaled_ref), custom_call_target="tpu_custom_call" | custom-call | tf_op jit(solution)/shard_map/pallas_call | solution.py:488
  160.1 3.5 %all-to-all-start.9 = ((bf16[4,384,256]{2,1,0:T(8,128)(2,1)}), bf16[4,384,256]{2,1,0:T(8,128)(2,1)S(1)}, u32[]{:S(2)}, u32[]{:S(2)}) async-start(bf16[4,384,256]{2,1,0:T(8,128)(2,1)} %shard_map.123), calls=%async_computation.9 | async-start | bytes 1572864 | tf_op jit(solution)/shard_map/all_to_all | solution.py:373
  163.7 3.9 %shard_map.122 = bf16[8,384,256]{2,1,0:T(8,128)(2,1)S(1)} custom-call(s32[4]{0:T(128)S(1)} %pad_add_fusion.place_ref, bf16[24,1152,1152]{2,1,0:T(8,128)(2,1)} %shard_map.115.kept_hbm, bf16[1024,1024]{1,0:T(8,128)(2,1)S(1)} %copy-done.1, f32[4,2,128]{2,1,0:T(2,128)S(1)} %all_to_all.56.scaled_ref), custom_call_target="tpu_custom_call" | custom-call | tf_op jit(solution)/shard_map/pallas_call | solution.py:488
  168.8 5.3 %all-to-all-done.9 = bf16[4,384,256]{2,1,0:T(8,128)(2,1)S(1)} async-done(((bf16[4,384,256]{2,1,0:T(8,128)(2,1)}), bf16[4,384,256]{2,1,0:T(8,128)(2,1)S(1)}, u32[]{:S(2)}, u32[]{:S(2)}) %all-to-all-start.9) | async-done | bytes 786464 | tf_op jit(solution)/shard_map/all_to_all | solution.py:373
  174.0 6.4 %all-to-all-start.8 = ((bf16[8,384,256]{2,1,0:T(8,128)(2,1)}), bf16[8,384,256]{2,1,0:T(8,128)(2,1)S(1)}, u32[]{:S(2)}, u32[]{:S(2)}) async-start(bf16[8,384,256]{2,1,0:T(8,128)(2,1)} %copy-done.2), calls=%async_computation.8 | async-start | bytes 3145728 | tf_op jit(solution)/shard_map/all_to_all | solution.py:373
  180.5 2.8 %collective-permute-start.5 = (bf16[384,256]{1,0:T(8,128)(2,1)S(1)}, bf16[384,256]{1,0:T(8,128)(2,1)S(1)}, u32[]{:S(2)}, u32[]{:S(2)}) collective-permute-start(bf16[384,256]{1,0:T(8,128)(2,1)S(1)} %reduce_sum.32), channel_id=1, source_target_pairs={{16,32},{32,16},{48,64},{64,48},{80,96},{96,80},{112,128},{128,112... | collective-permute-start | bytes 589832 | tf_op jit(solution)/shard_map/ppermute | solution.py:365
  183.4 17.6 %all-to-all-done.8 = bf16[8,384,256]{2,1,0:T(8,128)(2,1)S(1)} async-done(((bf16[8,384,256]{2,1,0:T(8,128)(2,1)}), bf16[8,384,256]{2,1,0:T(8,128)(2,1)S(1)}, u32[]{:S(2)}, u32[]{:S(2)}) %all-to-all-start.8) | async-done | bytes 1572896 | tf_op jit(solution)/shard_map/all_to_all | solution.py:373
  (48 shorter events, 12.8 us)
Async XLA Ops:
  0.6 24.3 %collective-permute-start = (bf16[384,256]{1,0:T(8,128)(2,1)}, bf16[384,256]{1,0:T(8,128)(2,1)S(1)}, u32[]{:S(2)}, u32[]{:S(2)}) collective-permute-start(bf16[384,256]{1,0:T(8,128)(2,1)} %own_ref.1), channel_id=1, source_target_pairs={{16,32},{32,16},{48,64},{64,48},{80,96},{96,80},{112,128},{128,112... | collective-permute-start | bytes 589832 | tf_op jit(solution)/shard_map/ppermute | solution.py:365
  10.8 0.7 copy-start.7
  11.5 0.7 copy-start.12
  24.9 0.9 copy-start.6
  27.1 4.3 %copy-start.5 = (bf16[2,128,512]{2,1,0:T(8,128)(2,1)S(1)}, bf16[2,128,512]{2,1,0:T(8,128)(2,1)}, u32[]{:S(2)}) copy-start(bf16[2,128,512]{2,1,0:T(8,128)(2,1)} %refs_0_.1) | copy-start | bytes 786436
  27.1 14.5 %copy-start.13 = (s32[32,4]{0,1:T(4,128)S(1)}, s32[32,4]{0,1:T(4,128)}, u32[]{:S(2)}) copy-start(s32[32,4]{0,1:T(4,128)} %param.11) | copy-start | bytes 1540
  27.1 33.4 %all-to-all-start.1 = ((bf16[4,784,256]{2,1,0:T(8,128)(2,1)}), bf16[4,784,256]{2,1,0:T(8,128)(2,1)S(1)}, u32[]{:S(2)}, u32[]{:S(2)}) async-start(bf16[4,784,256]{2,1,0:T(8,128)(2,1)} %shard_map.114), calls=%async_computation.1 | async-start | bytes 3211264 | tf_op jit(solution)/shard_map/all_to_all | solution.py:373
  31.4 21.8 %collective-permute-start.2 = (bf16[2,128,512]{2,1,0:T(8,128)(2,1)S(1)}, bf16[2,128,512]{2,1,0:T(8,128)(2,1)S(1)}, u32[]{:S(2)}, u32[]{:S(2)}) collective-permute-start(bf16[2,128,512]{2,1,0:T(8,128)(2,1)S(1)} %copy-done.5), channel_id=1, source_target_pairs={{0,8},{4,12},{8,0},{12,4},{1,9},{5,13},{9,1},{13,5},{2,10},{6,14},... | collective-permute-start | bytes 786440 | tf_op jit(solution)/shard_map/ppermute | solution.py:357
  34.5 18.7 %collective-permute-start.1 = (bf16[2,128,512]{2,1,0:T(8,128)(2,1)S(1)}, bf16[2,128,512]{2,1,0:T(8,128)(2,1)S(1)}, u32[]{:S(2)}, u32[]{:S(2)}) collective-permute-start(bf16[2,128,512]{2,1,0:T(8,128)(2,1)S(1)} %copy-done.5), channel_id=1, source_target_pairs={{0,4},{4,8},{8,12},{12,0},{1,5},{5,9},{9,13},{13,1},{2,6},{6,10},{... | collective-permute-start | bytes 786440 | tf_op jit(solution)/shard_map/ppermute | solution.py:357
  37.2 19.7 %collective-permute-start.3 = (bf16[2,128,512]{2,1,0:T(8,128)(2,1)S(1)}, bf16[2,128,512]{2,1,0:T(8,128)(2,1)S(1)}, u32[]{:S(2)}, u32[]{:S(2)}) collective-permute-start(bf16[2,128,512]{2,1,0:T(8,128)(2,1)S(1)} %copy-done.5), channel_id=1, source_target_pairs={{0,12},{4,0},{8,4},{12,8},{1,13},{5,1},{9,5},{13,9},{2,14},{6,2},{... | collective-permute-start | bytes 786440 | tf_op jit(solution)/shard_map/ppermute | solution.py:357
  60.6 19.1 %copy-start.4 = (bf16[2,256,256]{2,1,0:T(8,128)(2,1)S(1)}, bf16[2,256,256]{2,1,0:T(8,128)(2,1)}, u32[]{:S(2)}) copy-start(bf16[2,256,256]{2,1,0:T(8,128)(2,1)} %weight_ref.3) | copy-start | bytes 786436
  60.6 19.0 %copy-start.8 = (f32[256]{0:T(256)S(1)}, f32[256]{0:T(256)}, u32[]{:S(2)}) copy-start(f32[256]{0:T(256)} %param.13) | copy-start | bytes 3076
  60.7 19.0 %copy-start.9 = (f32[256]{0:T(256)S(1)}, f32[256]{0:T(256)}, u32[]{:S(2)}) copy-start(f32[256]{0:T(256)} %param.15) | copy-start | bytes 3076
  60.7 19.0 %copy-start.10 = (f32[256]{0:T(256)S(1)}, f32[256]{0:T(256)}, u32[]{:S(2)}) copy-start(f32[256]{0:T(256)} %param.16) | copy-start | bytes 3076
  60.7 59.1 %copy-start.3 = (bf16[2,256,256]{2,1,0:T(8,128)(2,1)S(1)}, bf16[2,256,256]{2,1,0:T(8,128)(2,1)}, u32[]{:S(2)}) copy-start(bf16[2,256,256]{2,1,0:T(8,128)(2,1)} %atom_weight_ref.3) | copy-start | bytes 786436
  60.7 5.4 %collective-permute-start.4 = (bf16[4,384,256]{2,1,0:T(8,128)(2,1)S(1)}, bf16[4,384,256]{2,1,0:T(8,128)(2,1)S(1)}, u32[]{:S(2)}, u32[]{:S(2)}) collective-permute-start(bf16[4,384,256]{2,1,0:T(8,128)(2,1)S(1)} %slice.3), channel_id=1, source_target_pairs={{0,16},{16,0},{1,17},{17,1},{2,18},{18,2},{3,19},{19,3},{4,20},{20... | collective-permute-start | bytes 2359304 | tf_op jit(solution)/shard_map/ppermute | solution.py:369
  70.6 1.3 copy-start
  80.3 68.3 %copy-start.11 = (f32[256]{0:T(256)S(1)}, f32[256]{0:T(256)}, u32[]{:S(2)}) copy-start(f32[256]{0:T(256)} %param.19) | copy-start | bytes 3076
  119.8 36.7 %copy-start.1 = (bf16[1024,1024]{1,0:T(8,128)(2,1)S(1)}, bf16[1024,1024]{1,0:T(8,128)(2,1)}, u32[]{:S(2)}) copy-start(bf16[1024,1024]{1,0:T(8,128)(2,1)} %copy-done) | copy-start | bytes 6291460
  160.1 13.9 %all-to-all-start.9 = ((bf16[4,384,256]{2,1,0:T(8,128)(2,1)}), bf16[4,384,256]{2,1,0:T(8,128)(2,1)S(1)}, u32[]{:S(2)}, u32[]{:S(2)}) async-start(bf16[4,384,256]{2,1,0:T(8,128)(2,1)} %shard_map.123), calls=%async_computation.9 | async-start | bytes 1572864 | tf_op jit(solution)/shard_map/all_to_all | solution.py:373
  167.6 1.2 copy-start.2
  174.0 27.0 %all-to-all-start.8 = ((bf16[8,384,256]{2,1,0:T(8,128)(2,1)}), bf16[8,384,256]{2,1,0:T(8,128)(2,1)S(1)}, u32[]{:S(2)}, u32[]{:S(2)}) async-start(bf16[8,384,256]{2,1,0:T(8,128)(2,1)} %copy-done.2), calls=%async_computation.8 | async-start | bytes 3145728 | tf_op jit(solution)/shard_map/all_to_all | solution.py:373
  180.5 20.7 %collective-permute-start.5 = (bf16[384,256]{1,0:T(8,128)(2,1)S(1)}, bf16[384,256]{1,0:T(8,128)(2,1)S(1)}, u32[]{:S(2)}, u32[]{:S(2)}) collective-permute-start(bf16[384,256]{1,0:T(8,128)(2,1)S(1)} %reduce_sum.32), channel_id=1, source_target_pairs={{16,32},{32,16},{48,64},{64,48},{80,96},{96,80},{112,128},{128,112... | collective-permute-start | bytes 589832 | tf_op jit(solution)/shard_map/ppermute | solution.py:365
